TPU v7x, 128 devices: a whole 4x4x4 slice. The times are simulated.
128 devices in a mesh: seq: 8 (over z, x_hi), dp: 16 (over y, x_lo, core).
Axes of the slice: x: 4 (x_hi: 2, x_lo: 2; x = x_hi * 2 + x_lo), y: 4, z: 4, core: 2. Of those that a mesh axis runs over, the one named last changes fastest.
Arguments:
- query_rows: bfloat16 [16, 6144, 1536], P('dp', 'seq'), may hold values from -8 to 8
- key_rows: bfloat16 [16, 6144, 1536], P('dp', 'seq'), may hold values from -8 to 8
- value_rows: bfloat16 [16, 6144, 1536], P('dp', 'seq'), may hold values from -6 to 6
- attention_out: bfloat16 [16, 6144, 1536], P('dp', 'seq'), may hold values from -6 to 6
- output_grad: bfloat16 [16, 6144, 3072], P('dp', 'seq'), may hold values from -6 to 6
- output_weight: bfloat16 [1536, 3072], P('dp'), may hold values from -0.15625 to 0.15625
- tile_mask: int32 [16, 16, 3], P('dp', 'seq'), may hold values from 0 to 1, as said below
- live_tiles: int32 [16, 8], P('dp'), may hold values from 1 to 2, as said below
Outputs:
- query_grad: bfloat16 [16, 6144, 1536], P('dp', 'seq')
- key_grad: bfloat16 [16, 6144, 1536], P('dp', 'seq')
- value_grad: bfloat16 [16, 6144, 1536], P('dp', 'seq')
- weight_grad: float32 [1536, 3072], P('dp')
Inputs may be any that keep to these rules, and one draw needn't show every extreme that they name: `tile_mask`: 1 marks an attended neighbour; entry 1 (the tile itself) is always 1, and so is every entry that points into another slab; entries pointing outside the video are ignored. `live_tiles`: tiles of a slab at or beyond its count are padding; every sample has a slab with all 2 tiles live.
All inputs are finite; a program needn't handle non-finite values.
Results may differ from a plain program's by a relative error of at most 0.027.
Values may be sent and summed in bfloat16 or wider, within the bound.
No kernel may reach another device: no remote copies, remote signals or barrier semaphores. Data moves between devices by JAX's collectives and lax.ppermute only.
A program may use at most 320 MiB of HBM per device.

v0:
```python
import math

import jax
import jax.numpy as jnp
from jax import lax
from jax.sharding import PartitionSpec as P

HDIM = 128
TILE = 384


MASKED_SCORE = -1e30


def padded(block, sides, width):
    for axis, dim in sides:
        count = lax.axis_size(axis)
        forward = [(i, i + 1) for i in range(count - 1)]
        backward = [(target, source) for source, target in forward]
        low = lax.ppermute(
            lax.slice_in_dim(block, block.shape[dim] - width, None, axis=dim), axis, forward
        )
        high = lax.ppermute(lax.slice_in_dim(block, 0, width, axis=dim), axis, backward)
        block = jnp.concatenate([low, block, high], axis=dim)
    return block


def passed_along(block, axis, distance):
    devices = range(lax.axis_size(axis))
    route = [(i - distance, i) for i in devices if i - distance in devices]
    return lax.ppermute(block, axis, route)


def tile_backward(query_tile, back_tile, output_tile, key_block, value_block, allowed, scaling):
    scores = (
        jnp.einsum("qhd,khd->hqk", query_tile, key_block, preferred_element_type=jnp.float32)
        * scaling
    )
    scores = jnp.where(allowed[None, None, :], scores, MASKED_SCORE)
    highest = jnp.max(scores, axis=2, keepdims=True)
    weights = jnp.where(allowed[None, None, :], jnp.exp(scores - highest), 0.0)
    totals = jnp.maximum(jnp.sum(weights, axis=2, keepdims=True), 1.0)
    attention_weights = weights / totals
    weights_low = attention_weights.astype(jnp.bfloat16)
    row_dots = jnp.einsum("qhd,qhd->hq", back_tile, output_tile, preferred_element_type=jnp.float32)
    grad_weights = jnp.einsum(
        "qhd,khd->hqk", back_tile, value_block, preferred_element_type=jnp.float32
    )
    grad_scores = (attention_weights * (grad_weights - row_dots[:, :, None]) * scaling).astype(
        jnp.bfloat16
    )
    query_part = jnp.einsum(
        "hqk,khd->qhd", grad_scores, key_block, preferred_element_type=jnp.float32
    )
    key_part = jnp.einsum(
        "hqk,qhd->khd", grad_scores, query_tile, preferred_element_type=jnp.float32
    )
    value_part = jnp.einsum(
        "hqk,qhd->khd", weights_low, back_tile, preferred_element_type=jnp.float32
    )
    return (query_part, key_part, value_part)


def count_of(counts, wanted):
    matches = jnp.arange(counts.shape[0], dtype=jnp.int32) == wanted
    return jnp.sum(jnp.where(matches, counts, 0))


def body(
    query_rows,
    key_rows,
    value_rows,
    attention_out,
    output_grad,
    output_weight,
    tile_mask,
    live_tiles,
):
    tokens = query_rows.shape[1]
    features = query_rows.shape[2]
    num_heads = features // HDIM
    per_slab = tokens // TILE
    slab_index = lax.axis_index("seq")
    slab_count = lax.axis_size("seq")
    replicas = lax.axis_size("dp")
    scaling = 1.0 / math.sqrt(HDIM)
    grad_rows = output_grad[0]
    output_local = attention_out[0]
    out_back = lax.dot_general(
        grad_rows,
        lax.all_gather(output_weight, "dp", axis=0, tiled=True),
        (((1,), (1,)), ((), ())),
        preferred_element_type=jnp.float32,
    ).astype(jnp.bfloat16)
    stacked = jnp.stack([key_rows[0], value_rows[0]])
    widened = padded(stacked, (("seq", 1),), TILE)
    widened = widened.reshape(2, (per_slab + 2) * TILE, num_heads, HDIM)
    counts = live_tiles[0]
    positions = jnp.arange(per_slab + 2, dtype=jnp.int32)
    global_tile = slab_index * per_slab + positions - 1
    owner_slab = jnp.clip(global_tile // per_slab, 0, slab_count - 1)
    slab_ids = jnp.arange(slab_count, dtype=jnp.int32)
    owner_count = jnp.sum(
        jnp.where(owner_slab[:, None] == slab_ids[None, :], counts[None, :], 0), axis=1
    )
    key_live = (
        (global_tile >= 0)
        & (global_tile < slab_count * per_slab)
        & (global_tile % per_slab < owner_count)
    )
    own_count = count_of(counts, slab_index)
    query_tiles = query_rows[0].reshape(per_slab, TILE, num_heads, HDIM)
    back_tiles = out_back.reshape(per_slab, TILE, num_heads, HDIM)
    output_tiles = output_local.reshape(per_slab, TILE, num_heads, HDIM)
    key_sums = jnp.zeros(((per_slab + 2) * TILE, num_heads, HDIM), jnp.float32)
    value_sums = jnp.zeros(((per_slab + 2) * TILE, num_heads, HDIM), jnp.float32)
    query_parts = []
    for tile_index in range(per_slab):
        key_block = widened[0, tile_index * TILE : (tile_index + 3) * TILE]
        value_block = widened[1, tile_index * TILE : (tile_index + 3) * TILE]
        query_live = tile_index < own_count
        allowed_tiles = (
            (tile_mask[0, tile_index] == 1) & key_live[tile_index : tile_index + 3] & query_live
        )
        allowed = jnp.repeat(allowed_tiles, TILE)
        operands = (
            query_tiles[tile_index],
            back_tiles[tile_index],
            output_tiles[tile_index],
            key_block,
            value_block,
            allowed,
        )
        results = tile_backward(
            operands[0], operands[1], operands[2], operands[3], operands[4], operands[5], scaling
        )
        query_parts.append(results[0].astype(jnp.bfloat16))
        key_sums = key_sums.at[tile_index * TILE : (tile_index + 3) * TILE].add(results[1])
        value_sums = value_sums.at[tile_index * TILE : (tile_index + 3) * TILE].add(results[2])
    lower_send = jnp.stack([key_sums[:TILE], value_sums[:TILE]]).astype(jnp.bfloat16)
    upper_send = jnp.stack([key_sums[-TILE:], value_sums[-TILE:]]).astype(jnp.bfloat16)
    from_above = passed_along(lower_send, "seq", -1)
    from_below = passed_along(upper_send, "seq", 1)
    inner_grad = jnp.stack([key_sums[TILE:-TILE], value_sums[TILE:-TILE]])
    inner_grad = inner_grad.at[:, :TILE].add(from_below.astype(jnp.float32))
    inner_grad = inner_grad.at[:, -TILE:].add(from_above.astype(jnp.float32))
    key_grad = inner_grad[0].reshape(tokens, features).astype(jnp.bfloat16)[None]
    value_grad = inner_grad[1].reshape(tokens, features).astype(jnp.bfloat16)[None]
    query_grad = jnp.concatenate(query_parts, 0).reshape(tokens, features)[None]
    normaliser = 1.0 / math.sqrt(replicas * slab_count * tokens)
    own_block = lax.psum_scatter(
        lax.dot_general(
            output_local, grad_rows, (((0,), (0,)), ((), ())), preferred_element_type=jnp.float32
        ).astype(jnp.bfloat16),
        "dp",
        scatter_dimension=0,
        tiled=True,
    )
    summed = lax.psum(own_block, "seq").astype(jnp.float32)
    weight_grad = summed * normaliser
    return (query_grad, key_grad, value_grad, weight_grad)


def solution(mesh):
    in_specs = (
        P("dp", "seq", None),
        P("dp", "seq", None),
        P("dp", "seq", None),
        P("dp", "seq", None),
        P("dp", "seq", None),
        P("dp", None),
        P("dp", "seq", None),
        P("dp", None),
    )
    out_specs = (P("dp", "seq", None), P("dp", "seq", None), P("dp", "seq", None), P("dp", None))
    return jax.shard_map(body, mesh=mesh, in_specs=in_specs, out_specs=out_specs, check_vma=False)
```

profile of v0, /device:TPU:0, one launch (start us, length us, event | category | flops | bytes accessed | tf_op | source)
XLA Modules:
  0.0 523.7 jit_solution(9345003646802769815)
XLA Ops:
  7.9 2.8 copy.60
  10.8 4.3 copy.61
  15.1 4.0 fusion.33
  19.1 1.4 collective-permute-start.1
  20.5 7.4 %collective-permute-start = (bf16[2,384,1536]{1,2,0:T(8,128)(2,1)}, bf16[2,384,1536]{1,2,0:T(8,128)(2,1)}, u32[]{:S(2)}, u32[]{:S(2)}) collective-permute-start(bf16[2,384,1536]{1,2,0:T(8,128)(2,1)} %get-tuple-element.90), channel_id=1, source_target_pairs={{0,16},{16,32},{32,48},{48,64},{64,80},{80,96},{96,112},{1,17},{17... | collective-permute-start | bytes 7077896 | tf_op jit(solution)/shard_map/ppermute | solution.py:20
  28.0 9.9 %convolution_convert_fusion = bf16[1536,3072]{1,0:T(8,128)(2,1)} fusion(bf16[1,768,3072]{2,1,0:T(8,128)(2,1)S(1)} %copy-done.9, bf16[1,768,1536]{2,1,0:T(8,128)(2,1)S(1)} %copy-done.4), kind=kOutput, calls=%fused_computation.18 | convolution fusion | flops 7252475904 | bytes 16515072 | tf_op jit(solution)/shard_map/dot_general | solution.py:152
  38.0 2.8 fusion.77
  40.8 1.4 copy.128
  44.5 3.2 fusion.76
  47.7 1.7 copy.126
  49.4 2.4 copy.124
  51.9 2.4 copy.122
  54.3 65.8 %collective-permute-done.1 = bf16[2,384,1536]{1,2,0:T(8,128)(2,1)} collective-permute-done((bf16[2,384,1536]{1,2,0:T(8,128)(2,1)}, bf16[2,384,1536]{1,2,0:T(8,128)(2,1)}, u32[]{:S(2)}, u32[]{:S(2)}) %collective-permute-start.1) | collective-permute-done | bytes 2359328 | tf_op jit(solution)/shard_map/ppermute | solution.py:23
  120.1 8.1 %pad_maximum_fusion.1 = bf16[2,1536,1536]{1,2,0:T(8,128)(2,1)} fusion(bf16[2,384,1536]{1,2,0:T(8,128)(2,1)} %collective-permute-done.1, bf16[1,768,1536]{1,2,0:T(8,128)(2,1)} %copy.61, bf16[1,768,1536]{1,2,0:T(8,128)(2,1)S(1)} %copy.60, bf16[2,384,1536]{1,2,0:T(8,128)(2,1)} %collective-permute-done), kind=kLoop, calls=%fused_computation.26 | loop fusion | flops 37748736 | bytes 18874368 | tf_op jit(solution)/shard_map/concatenate | solution.py:24
  128.2 15.8 %fusion.9 = (f32[12,384]{1,0:T(8,128)S(1)}, f32[12,384,1152]{1,2,0:T(8,128)}) fusion(pred[1152]{0:T(1024)(128)(4,1)S(1)} %broadcast_in_dim.81, bf16[384,12,128]{0,2,1:T(8,128)(2,1)S(1)} %bitcast.166, bf16[2,1536,12,128]{1,3,2,0:T(8,128)(2,1)} %bitcast.155), kind=kOutput, calls=%fused_computation.17 | convolution fusion | flops 1385497728 | bytes 25974784 | tf_op jit(solution)/shard_map/sub | solution.py:41
  144.5 15.9 %fusion.7 = (f32[12,384]{1,0:T(8,128)S(1)}, f32[12,384,1152]{1,2,0:T(8,128)}) fusion(pred[1152]{0:T(1024)(128)(4,1)S(1)} %broadcast_in_dim.75, bf16[384,12,128]{0,2,1:T(8,128)(2,1)S(1)} %bitcast.169, bf16[2,1536,12,128]{1,3,2,0:T(8,128)(2,1)} %bitcast.156), kind=kOutput, calls=%fused_computation.15 | convolution fusion | flops 1385497728 | bytes 25974784 | tf_op jit(solution)/shard_map/sub | solution.py:41
  161.1 11.6 %fusion.28 = bf16[768,1536]{1,0:T(8,128)(2,1)S(1)} fusion(bf16[1536,3072]{1,0:T(8,128)(2,1)} %all-gather.2.cloned.1.call-done, bf16[1,768,3072]{2,1,0:T(8,128)(2,1)} %param.24), kind=kOutput, calls=%fused_computation.49 | convolution fusion | flops 7248936960 | bytes 16515072 | tf_op jit(solution)/shard_map/dot_general | solution.py:89
  172.7 1.6 fusion.78
  174.2 2.4 copy.75
  176.6 2.4 copy.65
  179.0 2.2 fusion.35
  181.2 2.6 fusion.36
  183.8 14.7 %fusion.16 = f32[1152,12,128]{0,2,1:T(8,128)} fusion(bf16[384,12,128]{0,2,1:T(8,128)(2,1)} %bitcast.178, f32[12,384]{1,0:T(8,128)} %broadcast_maximum_fusion.1, pred[1152]{0:T(1024)(128)(4,1)S(1)} %broadcast_in_dim.75, bf16[384,12,128]{0,2,1:T(8,128)(2,1)S(1)} %bitcast.170, bf16[2,1536,12,128]{1,3,2,0:T(8,128)(2,1)} %bitcast.157), kind=kOutput, calls=%fused_computation.31 | convolution fusion | flops 2749765120 | bytes 13004800 | tf_op jit(solution)/shard_map/hqk,qhd->khd/dot_general | solution.py:58
  198.5 15.1 %fusion.15 = f32[1152,12,128]{0,2,1:T(8,128)} fusion(f32[1152,12,128]{0,2,1:T(8,128)} %fusion.16, bf16[384,12,128]{0,2,1:T(8,128)(2,1)S(1)} %bitcast.175, f32[12,384]{1,0:T(8,128)} %broadcast_maximum_fusion, pred[1152]{0:T(1024)(128)(4,1)S(1)} %broadcast_in_dim.81, bf16[384,12,128]{0,2,1:T(8,128)(2,1)S(1)} %bitcast.167, bf16[2,1536,12,128]{1,3,2,0:T(8,128)(2,1)} %bitcast.158), kind=kOutput, calls=%fused_computation.30 | convolution fusion | flops 2751534592 | bytes 20082688 | tf_op jit(solution)/shard_map/hqk,qhd->khd/dot_general | solution.py:58
  213.7 17.1 %multiply_convert_fusion.1 = bf16[12,384,1152]{1,2,0:T(8,128)(2,1)} fusion(bf16[384,12,128]{0,2,1:T(8,128)(2,1)} %bitcast.179, f32[12,384]{1,0:T(8,128)} %fusion.36, bf16[2,1536,12,128]{1,3,2,0:T(8,128)(2,1)} %bitcast.159, f32[12,384]{1,0:T(8,128)} %broadcast_maximum_fusion.1, f32[12,384,1152]{1,2,0:T(8,128)} %get-tuple-element.103, ...), kind=kOutput, calls=%fused_computation.11 | convolution fusion | flops 1390804992 | bytes 36619392 | tf_op jit(solution)/shard_map/qhd,khd->hqk/dot_general | solution.py:46
  230.8 10.5 %convolution_bitcast_fusion = f32[1152,12,128]{0,2,1:T(8,128)} fusion(bf16[12,384,1152]{1,2,0:T(8,128)(2,1)} %multiply_convert_fusion.1, bf16[384,12,128]{0,2,1:T(8,128)(2,1)S(1)} %bitcast.171), kind=kOutput, calls=%fused_computation.32 | convolution fusion | flops 1358954496 | bytes 18874368 | tf_op jit(solution)/shard_map/hqk,qhd->khd/dot_general | solution.py:55
  241.3 17.0 %multiply_convert_fusion = bf16[12,384,1152]{1,2,0:T(8,128)(2,1)} fusion(bf16[384,12,128]{0,2,1:T(8,128)(2,1)S(1)} %bitcast.176, f32[12,384]{1,0:T(8,128)S(1)} %copy-done.6, bf16[2,1536,12,128]{1,3,2,0:T(8,128)(2,1)} %bitcast.160, f32[12,384]{1,0:T(8,128)S(1)} %copy-done.7, f32[12,384,1152]{1,2,0:T(8,128)} %get-tuple-element.101, ...), kind=kOutput, calls=%fused_computation.8 | convolution fusion | flops 1390804992 | bytes 36607104 | tf_op jit(solution)/shard_map/qhd,khd->hqk/dot_general | solution.py:46
  258.3 11.8 %fusion.14 = f32[1152,12,128]{0,2,1:T(8,128)} fusion(f32[1152,12,128]{0,2,1:T(8,128)} %convolution_bitcast_fusion, bf16[12,384,1152]{1,2,0:T(8,128)(2,1)} %multiply_convert_fusion, bf16[384,12,128]{0,2,1:T(8,128)(2,1)S(1)} %bitcast.168), kind=kOutput, calls=%fused_computation.29 | convolution fusion | flops 1360723968 | bytes 25952256 | tf_op jit(solution)/shard_map/hqk,qhd->khd/dot_general | solution.py:55
  270.1 2.7 fusion.41
  272.8 1.7 pad_maximum_fusion.4
  274.5 97.2 %collective-permute-start.2 = (bf16[2,384,12,128]{1,3,2,0:T(8,128)(2,1)}, bf16[2,384,12,128]{1,3,2,0:T(8,128)(2,1)}, u32[]{:S(2)}, u32[]{:S(2)}) collective-permute-start(bf16[2,384,12,128]{1,3,2,0:T(8,128)(2,1)} %pad_maximum_fusion.4), channel_id=1, source_target_pairs={{0,16},{16,32},{32,48},{48,64},{64,80},{80,96},{96,112},{1,17},{17... | collective-permute-start | bytes 7077896 | tf_op jit(solution)/shard_map/ppermute | solution.py:31
  371.7 2.7 fusion.43
  374.4 1.7 pad_maximum_fusion.5
  376.1 1.7 collective-permute-start.3
  377.8 4.8 fusion.40
  382.7 5.3 %fusion.39 = bf16[384,12,128]{0,2,1:T(8,128)(2,1)} fusion(bf16[12,384,1152]{1,2,0:T(8,128)(2,1)S(1)} %bitcast.154, bf16[2,1536,12,128]{1,3,2,0:T(8,128)(2,1)} %bitcast.162), kind=kOutput, calls=%fused_computation.68 | convolution fusion | flops 1359544320 | bytes 15335424 | tf_op jit(solution)/shard_map/hqk,khd->qhd/dot_general | solution.py:52
  388.1 8.5 %slice_bitcast_fusion = (f32[1,768,12,128]{1,3,2,0:T(8,128)}, f32[1,768,12,128]{1,3,2,0:T(8,128)}) fusion(f32[1152,12,128]{0,2,1:T(8,128)} %fusion.15, f32[1152,12,128]{0,2,1:T(8,128)} %fusion.14), kind=kLoop, calls=%fused_computation.38 | loop fusion | bytes 18874368 | tf_op jit(solution)/shard_map/stack | solution.py:144
  396.8 2.4 copy.86
  399.3 8.3 %pad_maximum_fusion = f32[2,768,12,128]{1,3,2,0:T(8,128)} fusion(f32[1,768,12,128]{1,3,2,0:T(8,128)} %get-tuple-element.104, f32[1,768,12,128]{1,3,2,0:T(8,128)} %get-tuple-element.105), kind=kLoop, calls=%fused_computation.20 | loop fusion | flops 2359296 | bytes 18874368 | tf_op jit(solution)/shard_map/stack | solution.py:144
  407.6 73.7 %all-reduce.4.cloned.1.call-done = bf16[96,3072]{1,0:T(8,128)(2,1)} async-done(((bf16[96,3072]{1,0:T(8,128)(2,1)}), bf16[96,3072]{1,0:T(8,128)(2,1)}) %all-reduce.4.cloned.1.call-update) | async-done | bytes 589840 | tf_op jit(solution)/shard_map/psum | solution.py:159
  481.3 2.2 convert_multiply_fusion.2
  483.5 6.1 %fusion.23 = f32[2,768,12,128]{1,3,2,0:T(8,128)} fusion(f32[2,768,12,128]{1,3,2,0:T(8,128)} %pad_maximum_fusion, f32[1,768,12,128]{1,3,2,0:T(8,128)} %get-tuple-element.105, f32[1,768,12,128]{1,3,2,0:T(8,128)} %get-tuple-element.104, bf16[2,384,12,128]{1,3,2,0:T(8,128)(2,1)} %collective-permute-done.2), kind=kLoop, calls=%fused_computation.35 | loop fusion | flops 3538944 | bytes 16515072 | tf_op jit(solution)/shard_map/scatter-add | solution.py:145
  489.6 8.6 %collective-permute-done.3 = bf16[2,384,12,128]{1,3,2,0:T(8,128)(2,1)} collective-permute-done((bf16[2,384,12,128]{1,3,2,0:T(8,128)(2,1)}, bf16[2,384,12,128]{1,3,2,0:T(8,128)(2,1)}, u32[]{:S(2)}, u32[]{:S(2)}) %collective-permute-start.3) | collective-permute-done | bytes 2359328 | tf_op jit(solution)/shard_map/ppermute | solution.py:31
  498.2 6.1 %fusion.24 = f32[2,768,12,128]{1,3,2,0:T(8,128)} fusion(f32[2,768,12,128]{1,3,2,0:T(8,128)} %fusion.23, bf16[2,384,12,128]{1,3,2,0:T(8,128)(2,1)} %collective-permute-done.3), kind=kLoop, calls=%fused_computation.37 | loop fusion | flops 2359296 | bytes 11796480 | tf_op jit(solution)/shard_map/scatter-add | solution.py:146
  504.3 4.3 convert.28
  508.6 1.7 fusion.75
  510.3 4.3 copy.87
  514.6 2.4 copy.88
  (51 shorter events, 3.5 us)
Async XLA Ops:
  7.2 153.9 %all-gather.2.cloned.1.call-start = ((), (), s32[]{:S(2)}) async-start(), calls=%async_computation.1 | async-start | bytes 10027008 | tf_op jit(solution)/shard_map/all_gather | solution.py:91
  7.9 380.1 %reduce-scatter.2.cloned.1.call-start = ((), (), s32[]{:S(2)}) async-start(), calls=%async_computation.2 | async-start | bytes 10027008 | tf_op jit(solution)/shard_map/reduce_scatter | solution.py:151
  15.1 12.9 %copy-start.4 = (bf16[1,768,1536]{2,1,0:T(8,128)(2,1)S(1)}, bf16[1,768,1536]{2,1,0:T(8,128)(2,1)}, u32[]{:S(2)}) copy-start(bf16[1,768,1536]{2,1,0:T(8,128)(2,1)} %param.23) | copy-start | bytes 7077892
  15.1 12.9 %copy-start.9 = (bf16[1,768,3072]{2,1,0:T(8,128)(2,1)S(1)}, bf16[1,768,3072]{2,1,0:T(8,128)(2,1)}, u32[]{:S(2)}) copy-start(bf16[1,768,3072]{2,1,0:T(8,128)(2,1)} %param.24) | copy-start | bytes 14155780
  19.1 100.9 %collective-permute-start.1 = (bf16[2,384,1536]{1,2,0:T(8,128)(2,1)}, bf16[2,384,1536]{1,2,0:T(8,128)(2,1)}, u32[]{:S(2)}, u32[]{:S(2)}) collective-permute-start(bf16[2,384,1536]{1,2,0:T(8,128)(2,1)} %get-tuple-element.91), channel_id=1, source_target_pairs={{16,0},{32,16},{48,32},{64,48},{80,64},{96,80},{112,96},{17,1},{33... | collective-permute-start | bytes 7077896 | tf_op jit(solution)/shard_map/ppermute | solution.py:23
  20.5 99.5 %collective-permute-start = (bf16[2,384,1536]{1,2,0:T(8,128)(2,1)}, bf16[2,384,1536]{1,2,0:T(8,128)(2,1)}, u32[]{:S(2)}, u32[]{:S(2)}) collective-permute-start(bf16[2,384,1536]{1,2,0:T(8,128)(2,1)} %get-tuple-element.90), channel_id=1, source_target_pairs={{0,16},{16,32},{32,48},{48,64},{64,80},{80,96},{96,112},{1,17},{17... | collective-permute-start | bytes 7077896 | tf_op jit(solution)/shard_map/ppermute | solution.py:20
  37.9 4.3 copy-start.10
  37.9 6.4 %copy-start.8 = (s32[1,2,3]{2,1,0:T(2,128)S(1)}, s32[1,2,3]{2,1,0:T(2,128)}, u32[]{:S(2)}) copy-start(s32[1,2,3]{2,1,0:T(2,128)} %param.26) | copy-start | bytes 76
  37.9 443.4 %all-reduce.4.cloned.1.call-start = ((), (), s32[]{:S(2)}) async-start(), calls=%async_computation.3 | async-start | bytes 1179648 | tf_op jit(solution)/shard_map/psum | solution.py:159
  128.2 16.4 %copy-start.1 = (bf16[1,384,1536]{1,2,0:T(8,128)(2,1)S(1)}, bf16[1,384,1536]{1,2,0:T(8,128)(2,1)}, u32[]{:S(2)}) copy-start(bf16[1,384,1536]{1,2,0:T(8,128)(2,1)} %copy.122) | copy-start | bytes 3538948
  172.7 6.3 %copy-start.2 = (bf16[1,384,1536]{1,2,0:T(8,128)(2,1)S(1)}, bf16[1,384,1536]{1,2,0:T(8,128)(2,1)}, u32[]{:S(2)}) copy-start(bf16[1,384,1536]{1,2,0:T(8,128)(2,1)} %copy.128) | copy-start | bytes 3538948
  183.8 14.7 %copy-start.3 = (bf16[384,1536]{0,1:T(8,128)(2,1)S(1)}, bf16[384,1536]{0,1:T(8,128)(2,1)}, u32[]{:S(2)}) copy-start(bf16[384,1536]{0,1:T(8,128)(2,1)} %copy.75) | copy-start | bytes 3538948
  230.8 10.5 %copy-start.6 = (f32[12,384]{1,0:T(8,128)S(1)}, f32[12,384]{1,0:T(8,128)}, u32[]{:S(2)}) copy-start(f32[12,384]{1,0:T(8,128)} %fusion.35) | copy-start | bytes 55300
  230.8 10.5 %copy-start.7 = (f32[12,384]{1,0:T(8,128)S(1)}, f32[12,384]{1,0:T(8,128)}, u32[]{:S(2)}) copy-start(f32[12,384]{1,0:T(8,128)} %broadcast_maximum_fusion) | copy-start | bytes 55300
  272.8 105.0 %copy-start = (bf16[12,384,1152]{1,2,0:T(8,128)(2,1)S(1)}, bf16[12,384,1152]{1,2,0:T(8,128)(2,1)}, u32[]{:S(2)}) copy-start(bf16[12,384,1152]{1,2,0:T(8,128)(2,1)} %multiply_convert_fusion) | copy-start | bytes 31850500
  274.5 209.0 %collective-permute-start.2 = (bf16[2,384,12,128]{1,3,2,0:T(8,128)(2,1)}, bf16[2,384,12,128]{1,3,2,0:T(8,128)(2,1)}, u32[]{:S(2)}, u32[]{:S(2)}) collective-permute-start(bf16[2,384,12,128]{1,3,2,0:T(8,128)(2,1)} %pad_maximum_fusion.4), channel_id=1, source_target_pairs={{0,16},{16,32},{32,48},{48,64},{64,80},{80,96},{96,112},{1,17},{17... | collective-permute-start | bytes 7077896 | tf_op jit(solution)/shard_map/ppermute | solution.py:31
  374.4 8.2 %slice-start = ((s8[10616832]{0:T(1024)(128)(4,1)}), s8[4194304]{0:T(1024)(128)(4,1)S(1)}, s32[]{:S(2)}) async-start(s8[10616832]{0:T(1024)(128)(4,1)} %bitcast.153), calls=%async_computation.4 | async-start | bytes 8388608
  376.1 6.6 %slice-start.1 = ((s8[10616832]{0:T(1024)(128)(4,1)}), s8[4194304]{0:T(1024)(128)(4,1)S(1)}, s32[]{:S(2)}) async-start(s8[10616832]{0:T(1024)(128)(4,1)} %bitcast.153), calls=%async_computation.5 | async-start | bytes 8388608
  376.1 6.6 %slice-start.2 = ((s8[10616832]{0:T(1024)(128)(4,1)}), s8[2228224]{0:T(1024)(128)(4,1)S(1)}, s32[]{:S(2)}) async-start(s8[10616832]{0:T(1024)(128)(4,1)} %bitcast.153), calls=%async_computation.6 | async-start | bytes 4456448
  376.1 122.1 %collective-permute-start.3 = (bf16[2,384,12,128]{1,3,2,0:T(8,128)(2,1)}, bf16[2,384,12,128]{1,3,2,0:T(8,128)(2,1)}, u32[]{:S(2)}, u32[]{:S(2)}) collective-permute-start(bf16[2,384,12,128]{1,3,2,0:T(8,128)(2,1)} %pad_maximum_fusion.5), channel_id=1, source_target_pairs={{16,0},{32,16},{48,32},{64,48},{80,64},{96,80},{112,96},{17,1},{33... | collective-permute-start | bytes 7077896 | tf_op jit(solution)/shard_map/ppermute | solution.py:31
  388.0 8.5 %copy-start.5 = (bf16[384,12,128]{0,2,1:T(8,128)(2,1)S(1)}, bf16[384,12,128]{0,2,1:T(8,128)(2,1)}, u32[]{:S(2)}) copy-start(bf16[384,12,128]{0,2,1:T(8,128)(2,1)} %fusion.39) | copy-start | bytes 3538948
Sparse Core Ops, SparseCore 0:
  9.7 98.1 all-gather.1
  110.3 112.2 reduce-scatter.1
  388.2 93.1 all-reduce.3
where the time goes:
time: 532 us; the launch traced here: 524 us
  matrix products  150 us (28%)
  waiting for transfers between devices  149 us (28%)
  starting transfers between devices  108 us (20%)
  local copies, waits for them, and re-layouts  52.4 us (10%)
  other arithmetic  49.7 us (9%)
  between operations  15.4 us (3%)
    ppermute x2, starting transfers between devices, passed_along(): return lax.ppermute(block, axis, route)  98.9 us
    psum x1, waiting for transfers between devices, body(): summed = lax.psum(own_block, 'seq').astype(jnp.float32)  73.7 us
    ppermute x1, waiting for transfers between devices, padded(): lax.ppermute(lax.slice_in_dim(block, 0, width, axis=dim), axis, backward)  65.8 us
    dot_general x2, matrix products, tile_backward(): jnp.einsum('qhd,khd->hqk', back_tile, value_block, preferred_element_type...  34.1 us
    sub x2, matrix products, tile_backward(): weights = jnp.where(allowed[None, None, :], jnp.exp(scores - highest), 0.0)  31.7 us
    dot_general x2, matrix products, tile_backward(): jnp.einsum('hqk,qhd->khd', weights_low, back_tile, preferred_element_type...  29.9 us
    unnamed x37, local copies, waits for them, and re-layouts  24.2 us
    dot_general x2, matrix products, tile_backward(): jnp.einsum('hqk,qhd->khd', grad_scores, query_tile, preferred_element_typ...  22.3 us
  transfers between devices with their start and end apart: 7, of which 3 were waited for; matrix products, arithmetic and copies ran while one was open for 44% of the time, Pallas kernels for 0%

commit v1 on v0

v1 whole, which is shorter than its diff:
```python
import functools
import math

import jax
import jax.numpy as jnp
from jax import lax
from jax.experimental import pallas as pl
from jax.experimental.pallas import tpu as pltpu
from jax.sharding import PartitionSpec as P

HDIM = 128
TILE = 384
SLAB = 768
FEAT = 1536
WIDTH = 3072
GROUP = 3
BLOCK = GROUP * HDIM
QUARTER = WIDTH // 4
ROWS = 96
AXES = ("seq", "dp")
SCALE = 1.0 / math.sqrt(HDIM)
SCALE2 = SCALE / math.log(2.0)
NEVER = 1e30
LIMIT = 48 * 1024 * 1024
F32 = jnp.float32
BF16 = jnp.bfloat16


def place(z, y, x, core):
    return ((z % 4) * 2 + (x % 4) // 2) * 16 + (y % 4) * 4 + (x % 2) * 2 + core


def route(target):
    pairs = []
    for z in range(4):
        for y in range(4):
            for x in range(4):
                for core in range(2):
                    to = target(z, y, x, core)
                    if to is not None:
                        pairs.append((place(z, y, x, core), place(*to)))
    return pairs


def slab_step(step):
    def target(z, y, x, core):
        slab = z * 2 + x // 2 + step
        if slab < 0 or slab > 7:
            return None
        return (slab // 2, y, (slab % 2) * 2 + x % 2, core)

    return route(target)


UP = slab_step(1)
DOWN = slab_step(-1)
SWAP_LOW = route(lambda z, y, x, core: (z, y, x ^ 1, core))
SWAP_HIGH = route(lambda z, y, x, core: (z, y, x ^ 2, core))
SWAP_CORE = route(lambda z, y, x, core: (z, y, x, 1 - core))


def from_first(step):
    return route(
        lambda z, y, x, core: (z, y - step, x, core) if core == 0 else (z - step, y, x, core)
    )


def from_second(step):
    return route(
        lambda z, y, x, core: (z - step, y, x, core) if core == 0 else (z, y - step, x, core)
    )


def send(block, pairs):
    return lax.ppermute(block, AXES, pairs)


def dot(a, b, dims):
    return lax.dot_general(a, b, (dims, ((), ())), preferred_element_type=F32)


NT = ((1,), (1,))
NN = ((1,), (0,))
TN = ((0,), (0,))


def params(**kwargs):
    return pltpu.CompilerParams(vmem_limit_bytes=LIMIT, **kwargs)


def cost(flops, moved, exps=0):
    return pl.CostEstimate(flops=int(flops), bytes_accessed=int(moved), transcendentals=int(exps))


def head_of(dy, j, where):
    return lax.rem(where[0] + dy, 4) * GROUP + j


def own_stats_kernel(where, q, k, bias, out):
    queries = q[...]
    first = dot(k[:TILE], queries, NT) * SCALE2 + bias[0:1]
    second = dot(k[TILE:], queries, NT) * SCALE2 + bias[1:2]
    highest = jnp.maximum(
        jnp.max(first, axis=0, keepdims=True), jnp.max(second, axis=0, keepdims=True)
    )
    total = jnp.sum(jnp.exp2(first - highest), axis=0, keepdims=True) + jnp.sum(
        jnp.exp2(second - highest), axis=0, keepdims=True
    )
    out[0] = highest + jnp.log2(total)


def own_stats(where, q, k, bias):
    return pl.pallas_call(
        own_stats_kernel,
        grid_spec=pltpu.PrefetchScalarGridSpec(
            num_scalar_prefetch=1,
            grid=(4, GROUP),
            in_specs=[
                pl.BlockSpec((SLAB, HDIM), lambda d, j, w: (0, head_of(d, j, w))),
                pl.BlockSpec((SLAB, HDIM), lambda d, j, w: (0, head_of(d, j, w))),
                pl.BlockSpec((2, SLAB), lambda d, j, w: (0, 0)),
            ],
            out_specs=pl.BlockSpec((1, 1, SLAB), lambda d, j, w: (d * GROUP + j, 0, 0)),
        ),
        out_shape=jax.ShapeDtypeStruct((12, 1, SLAB), F32),
        compiler_params=params(),
        cost_estimate=cost(2 * SLAB * SLAB * FEAT, 5e6, 12 * SLAB * SLAB),
        name="own_stats",
    )(where, q, k, bias)


def far_stats_kernel(where, qb, qa, k, out_b, out_a):
    for queries, keys, out in ((qb, k[:TILE], out_b), (qa, k[TILE:], out_a)):
        scores = dot(keys, queries[...], NT) * SCALE2
        highest = jnp.max(scores, axis=0, keepdims=True)
        total = jnp.sum(jnp.exp2(scores - highest), axis=0, keepdims=True)
        out[0] = highest + jnp.log2(total)


def far_stats(where, qb, qa, k):
    half = pl.BlockSpec((TILE, HDIM), lambda d, j, w: (0, head_of(d, j, w)))
    row = pl.BlockSpec((1, 1, TILE), lambda d, j, w: (d * GROUP + j, 0, 0))
    return pl.pallas_call(
        far_stats_kernel,
        grid_spec=pltpu.PrefetchScalarGridSpec(
            num_scalar_prefetch=1,
            grid=(4, GROUP),
            in_specs=[
                half,
                half,
                pl.BlockSpec((SLAB, HDIM), lambda d, j, w: (0, head_of(d, j, w))),
            ],
            out_specs=[row, row],
        ),
        out_shape=[jax.ShapeDtypeStruct((12, 1, TILE), F32)] * 2,
        compiler_params=params(),
        cost_estimate=cost(SLAB * SLAB * FEAT, 5e6, 6 * SLAB * SLAB),
        name="far_stats",
    )(where, qb, qa, k)


def back_kernel(where, g, mine, other, o, up, down, dots, total, weight):
    dz = pl.program_id(1)

    @pl.when(where[2] == 0)
    def _():
        for low in range(2):
            weight[pl.ds(low * 192, ROWS)] = mine[0, 0, low]
            weight[pl.ds(low * 192 + ROWS, ROWS)] = other[0, 0, low]

    @pl.when(where[2] == 1)
    def _():
        for low in range(2):
            weight[pl.ds(low * 192, ROWS)] = other[0, 0, low]
            weight[pl.ds(low * 192 + ROWS, ROWS)] = mine[0, 0, low]

    product = dot(g[...], weight[...], NT)

    @pl.when(dz == 0)
    def _():
        total[...] = product

    @pl.when(dz > 0)
    def _():
        total[...] += product

    @pl.when(dz == 3)
    def _():
        ones = jnp.ones((8, HDIM), BF16)
        for j in range(GROUP):
            columns = slice(j * HDIM, (j + 1) * HDIM)
            back = total[:, columns].astype(BF16)
            down[0, :, columns] = back[:TILE]
            up[0, :, columns] = back[TILE:]
            products = back.astype(F32) * o[:, columns].astype(F32)
            coarse = products.astype(BF16)
            fine = (products - coarse.astype(F32)).astype(BF16)
            dots[0, j] = (dot(ones, coarse, NT) + dot(ones, fine, NT))[0:1]


def back(where, g, mine, other, o, dy0, count):
    def straight(d, e, w):
        return jnp.where(w[2] == 0, e, dy0 + d), jnp.where(w[2] == 0, dy0 + d, e)

    def crossed(d, e, w):
        return jnp.where(w[2] == 0, dy0 + d, e), jnp.where(w[2] == 0, e, dy0 + d)

    piece = (1, 1, 2, ROWS, QUARTER)
    half = pl.BlockSpec((1, TILE, BLOCK), lambda d, e, w: (d, 0, 0))
    return pl.pallas_call(
        back_kernel,
        grid_spec=pltpu.PrefetchScalarGridSpec(
            num_scalar_prefetch=1,
            grid=(count, 4),
            in_specs=[
                pl.BlockSpec((SLAB, QUARTER), lambda d, e, w: (0, lax.rem(w[1] + e, 4))),
                pl.BlockSpec(piece, lambda d, e, w: straight(d, e, w) + (0, 0, 0)),
                pl.BlockSpec(piece, lambda d, e, w: crossed(d, e, w) + (0, 0, 0)),
                pl.BlockSpec((SLAB, BLOCK), lambda d, e, w: (0, lax.rem(w[0] + dy0 + d, 4))),
            ],
            out_specs=[
                half,
                half,
                pl.BlockSpec((1, GROUP, 1, SLAB), lambda d, e, w: (d, 0, 0, 0)),
            ],
            scratch_shapes=[pltpu.VMEM((SLAB, BLOCK), F32), pltpu.VMEM((BLOCK, QUARTER), BF16)],
        ),
        out_shape=[
            jax.ShapeDtypeStruct((count, TILE, BLOCK), BF16),
            jax.ShapeDtypeStruct((count, TILE, BLOCK), BF16),
            jax.ShapeDtypeStruct((count, GROUP, 1, SLAB), F32),
        ],
        compiler_params=params(),
        cost_estimate=cost(count * 2 * SLAB * BLOCK * WIDTH, count * 9e6),
        name="out_back",
    )(where, g, mine, other, o)


def own_kernel(where, q, k, v, up, down, rows, dots, dq, dk, dv):
    queries = q[...]
    backs = jnp.concatenate([down[0], up[0]], axis=0)
    row_dots = dots[0, 0]
    query_total = None
    for tile in range(2):
        part = slice(tile * TILE, (tile + 1) * TILE)
        keys = k[part]
        weights = jnp.exp2(dot(keys, queries, NT) * SCALE2 - rows[0, tile : tile + 1])
        grads = (weights * (dot(v[part], backs, NT) - row_dots)).astype(BF16)
        dv[0, part] = dot(weights.astype(BF16), backs, NN)
        dk[0, part] = dot(grads, queries, NN) * SCALE
        share = dot(grads, keys, TN)
        query_total = share if query_total is None else query_total + share
    dq[0] = query_total * SCALE


def own_grads(where, q, k, v, up, down, rows, dots, dy0, count):
    full = pl.BlockSpec((SLAB, HDIM), lambda d, j, w: (0, head_of(dy0 + d, j, w)))
    half = pl.BlockSpec((1, TILE, HDIM), lambda d, j, w: (d, 0, j))
    result = pl.BlockSpec((1, SLAB, HDIM), lambda d, j, w: (d, 0, j))
    return pl.pallas_call(
        own_kernel,
        grid_spec=pltpu.PrefetchScalarGridSpec(
            num_scalar_prefetch=1,
            grid=(count, GROUP),
            in_specs=[
                full,
                full,
                full,
                half,
                half,
                pl.BlockSpec((1, 2, SLAB), lambda d, j, w: ((dy0 + d) * GROUP + j, 0, 0)),
                pl.BlockSpec((1, 1, 1, SLAB), lambda d, j, w: (d, j, 0, 0)),
            ],
            out_specs=[result] * 3,
        ),
        out_shape=[jax.ShapeDtypeStruct((count, SLAB, BLOCK), F32)] * 3,
        compiler_params=params(),
        cost_estimate=cost(
            count * GROUP * 10 * SLAB * SLAB * HDIM, count * 7e6, count * GROUP * SLAB * SLAB
        ),
        name="own_grads",
    )(where, q, k, v, up, down, rows, dots)


def far_kernel(
    where, qb, qa, backb, backa, rowb, rowa, k, v, dk_own, dv_own, *rest
):
    dqb, dqa, dk, dv = rest[-4:]
    sides = ((qb, backb, rowb, dqb), (qa, backa, rowa, dqa))
    for tile, (q, b, row, dq) in enumerate(sides):
        part = slice(tile * TILE, (tile + 1) * TILE)
        keys = k[part]
        queries = q[...]
        backs = b[0]
        weights = jnp.exp2(dot(keys, queries, NT) * SCALE2 - row[0, 0:1])
        grads = (weights * (dot(v[part], backs, NT) - row[0, 1:2])).astype(BF16)
        dq[0] = (dot(grads, keys, TN) * SCALE).astype(BF16)
        dk[part] = (dk_own[0, part] + dot(grads, queries, NN) * SCALE).astype(BF16)
        dv[part] = (dv_own[0, part] + dot(weights.astype(BF16), backs, NN)).astype(BF16)


def far_grads(where, qb, qa, backb, backa, rowb, rowa, k, v, dk_own, dv_own, held, dy0, count):
    full = pl.BlockSpec((SLAB, HDIM), lambda d, j, w: (0, head_of(dy0 + d, j, w)))
    edge = pl.BlockSpec((TILE, HDIM), lambda d, j, w: (0, head_of(dy0 + d, j, w)))
    half = pl.BlockSpec((1, TILE, HDIM), lambda d, j, w: (d, 0, j))
    own = pl.BlockSpec((1, SLAB, HDIM), lambda d, j, w: (d, 0, j))
    row = pl.BlockSpec((1, 2, TILE), lambda d, j, w: ((dy0 + d) * GROUP + j, 0, 0))
    aliases = {11: 2, 12: 3} if held else {}
    return pl.pallas_call(
        far_kernel,
        grid_spec=pltpu.PrefetchScalarGridSpec(
            num_scalar_prefetch=1,
            grid=(count, GROUP),
            in_specs=[edge, edge, half, half, row, row, full, full, own, own]
            + [pl.BlockSpec(memory_space=pl.ANY)] * len(held),
            out_specs=[half, half, full, full],
        ),
        out_shape=[jax.ShapeDtypeStruct((count, TILE, BLOCK), BF16)] * 2
        + [jax.ShapeDtypeStruct((SLAB, FEAT), BF16)] * 2,
        input_output_aliases=aliases,
        compiler_params=params(),
        cost_estimate=cost(
            count * GROUP * 5 * SLAB * SLAB * HDIM, count * 6e6, count * GROUP * SLAB * TILE
        ),
        name="far_grads",
    )(where, qb, qa, backb, backa, rowb, rowa, k, v, dk_own, dv_own, *held)


def join_kernel(where, own, low, high, *rest):
    out = rest[-1]
    out[:TILE] = (own[0, :TILE] + low[0].astype(F32)).astype(BF16)
    out[TILE:] = (own[0, TILE:] + high[0].astype(F32)).astype(BF16)


def join(where, own, low, high, held, dy0, count):
    half = pl.BlockSpec((1, TILE, BLOCK), lambda d, w: (d, 0, 0))
    return pl.pallas_call(
        join_kernel,
        grid_spec=pltpu.PrefetchScalarGridSpec(
            num_scalar_prefetch=1,
            grid=(count,),
            in_specs=[pl.BlockSpec((1, SLAB, BLOCK), lambda d, w: (d, 0, 0)), half, half]
            + [pl.BlockSpec(memory_space=pl.ANY)] * len(held),
            out_specs=pl.BlockSpec((SLAB, BLOCK), lambda d, w: (0, lax.rem(w[0] + dy0 + d, 4))),
        ),
        out_shape=jax.ShapeDtypeStruct((SLAB, FEAT), BF16),
        input_output_aliases={4: 0} if held else {},
        compiler_params=params(),
        cost_estimate=cost(count * SLAB * BLOCK, count * 3e6),
        name="join_query_grad",
    )(where, own, low, high, *held)


def weight_term_kernel(o, g, out):
    product = dot(o[...], g[...], TN).astype(BF16)
    for low in range(2):
        for core in range(2):
            start = (low * 2 + core) * ROWS
            out[0, core, 0, low] = product[start : start + ROWS]


def weight_term(o, g):
    return pl.pallas_call(
        weight_term_kernel,
        grid=(4, 4),
        in_specs=[
            pl.BlockSpec((SLAB, BLOCK), lambda y, z: (0, y)),
            pl.BlockSpec((SLAB, QUARTER), lambda y, z: (0, z)),
        ],
        out_specs=pl.BlockSpec((1, 2, 1, 2, ROWS, QUARTER), lambda y, z: (y, 0, z, 0, 0, 0)),
        out_shape=jax.ShapeDtypeStruct((4, 2, 4, 2, ROWS, QUARTER), BF16),
        compiler_params=params(),
        cost_estimate=cost(2 * SLAB * FEAT * WIDTH, 3.5e7),
        name="weight_term",
    )(o, g)


def gather_weight(weight, z, low):
    quarter = lax.dynamic_slice(weight, (0, z * QUARTER), (ROWS, QUARTER))
    partner = send(quarter, SWAP_LOW)
    pair = jnp.where(
        low == 0, jnp.stack([quarter, partner]), jnp.stack([partner, quarter])
    )
    line = jnp.stack([pair] + [send(pair, from_first(step)) for step in (1, 2, 3)])
    plane = jnp.stack([line] + [send(line, from_second(step)) for step in (1, 2, 3)])
    return plane, send(plane, SWAP_CORE)


def weight_gradient(term, z, low, normaliser):
    groups = [
        [place(z, y, x, core) for y in range(4) for core in range(2) for z in range(4)]
        for x in range(4)
    ]
    part = lax.psum_scatter(
        term.reshape(32 * 2 * ROWS, QUARTER),
        AXES,
        scatter_dimension=0,
        axis_index_groups=groups,
        tiled=True,
    ).reshape(2, ROWS, QUARTER)
    kept = jnp.where(low == 0, part[0], part[1]).astype(F32)
    given = jnp.where(low == 0, part[1], part[0])
    both = (kept + send(given, SWAP_LOW).astype(F32)).astype(BF16)
    whole = both.astype(F32) + send(both, SWAP_HIGH).astype(F32)
    lines = [
        [place(z, y, x, core) for z in range(4)]
        for y in range(4)
        for x in range(4)
        for core in range(2)
    ]
    return lax.all_gather(
        whole * normaliser, AXES, axis=1, axis_index_groups=lines, tiled=True
    )


RUNS = ((0, 2), (2, 2))


def body(
    query_rows,
    key_rows,
    value_rows,
    attention_out,
    output_grad,
    output_weight,
    tile_mask,
    live_tiles,
):
    q, k, v, o, g = (
        a[0] for a in (query_rows, key_rows, value_rows, attention_out, output_grad)
    )
    slab = lax.axis_index("seq")
    row = lax.axis_index("dp")
    z = slab // 2
    y = row // 4
    low = (row // 2) % 2
    core = row % 2
    where = jnp.stack([y, z, core]).astype(jnp.int32)

    q_below = send(q[TILE:], UP)
    q_above = send(q[:TILE], DOWN)
    mine, other = gather_weight(output_weight, z, low)

    counts = live_tiles[0]
    slabs = jnp.arange(8, dtype=jnp.int32)

    def live(which, tile):
        return jnp.any((slabs == which) & (counts > tile))

    lives = [live(slab - 1, 1), live(slab, 0), live(slab, 1), live(slab + 1, 0)]
    marks = tile_mask[0] == 1
    allowed = [
        [marks[a, b] & lives[a + 1] & lives[a + b] for b in range(3)] for a in range(2)
    ]

    def by_query(first, second):
        return jnp.concatenate(
            [jnp.broadcast_to(first, (1, TILE)), jnp.broadcast_to(second, (1, TILE))], axis=1
        )

    own_allowed = [by_query(allowed[0][1], allowed[1][0]), by_query(allowed[0][2], allowed[1][1])]
    far_allowed = by_query(allowed[0][0], allowed[1][2])
    bias = jnp.where(jnp.concatenate(own_allowed, axis=0), 0.0, -NEVER).astype(F32)

    own_row = own_stats(where, q, k, bias)
    stat_b, stat_a = far_stats(where, q_below, q_above, k)
    far_row = jnp.concatenate([send(stat_a, UP), send(stat_b, DOWN)], axis=2)
    far_row = jnp.where(far_allowed[None], far_row, -NEVER)
    top = jnp.maximum(own_row, far_row)
    row_total = top + jnp.log2(jnp.exp2(own_row - top) + jnp.exp2(far_row - top))
    own_rows = jnp.concatenate(
        [jnp.where(a[None], row_total, NEVER) for a in own_allowed], axis=1
    )
    far_rows = jnp.where(far_allowed[None], row_total, NEVER)

    backs = [back(where, g, mine, other, o, *run) for run in RUNS]
    dots = jnp.concatenate([b[2] for b in backs], axis=0).reshape(12, 1, SLAB)
    message = jnp.concatenate([far_rows, dots], axis=1)
    row_b = send(message[:, :, TILE:], UP)
    row_a = send(message[:, :, :TILE], DOWN)
    row_b = jnp.where(slab == 0, NEVER, row_b)
    row_a = jnp.where(slab == 7, NEVER, row_a)

    back_b = [send(b[0], UP) for b in backs]
    back_a = [send(b[1], DOWN) for b in backs]

    term = weight_term(o, g)
    weight_grad = weight_gradient(term, z, low, 1.0 / math.sqrt(16 * 6144))

    held = ()
    joined = ()
    finished = []
    for index, (dy0, count) in enumerate(RUNS):
        up, down, own_dots = backs[index]
        dq, dk, dv = own_grads(where, q, k, v, up, down, own_rows, own_dots, dy0, count)
        dqb, dqa, *held = far_grads(
            where,
            q_below,
            q_above,
            back_b[index],
            back_a[index],
            row_b,
            row_a,
            k,
            v,
            dk,
            dv,
            tuple(held),
            dy0,
            count,
        )
        finished.append((dq, send(dqa, UP), send(dqb, DOWN), dy0, count))
    for dq, from_below, from_above, dy0, count in finished:
        joined = (join(where, dq, from_below, from_above, joined, dy0, count),)
    return joined[0][None], held[0][None], held[1][None], weight_grad


def solution(mesh):
    in_specs = (
        P("dp", "seq", None),
        P("dp", "seq", None),
        P("dp", "seq", None),
        P("dp", "seq", None),
        P("dp", "seq", None),
        P("dp", None),
        P("dp", "seq", None),
        P("dp", None),
    )
    out_specs = (P("dp", "seq", None), P("dp", "seq", None), P("dp", "seq", None), P("dp", None))
    return jax.shard_map(body, mesh=mesh, in_specs=in_specs, out_specs=out_specs, check_vma=False)
```

time: 532 us -> 369 us (0.69)
  matrix products: 150 us -> 0 us
  Pallas kernels: 0 us -> 119 us
  waiting for transfers between devices: 149 us -> 93.5 us
  other arithmetic: 49.7 us -> 12.1 us
  local copies, waits for them, and re-layouts: 52.4 us -> 20.5 us
  starting transfers between devices: 108 us -> 95.5 us
  between operations: 15.4 us -> 25.4 us
    pallas_call x0 -> x11, Pallas kernels: none -> 119 us  [the longest x2 27.1 us: own_grads(): pl.pallas_call(own_kernel, grid_spec=pltpu.PrefetchScalarGridSpec(num_sca...]
    dot_general x10 -> x0, matrix products: 118 us -> none  [the longest x2 34.1 us: tile_backward(): jnp.einsum('qhd,khd->hqk', back_tile, value_block, preferred_element_type...]
    psum x1 -> x0, waiting for transfers between devices: 73.7 us -> none  [body(): summed = lax.psum(own_block, 'seq').astype(jnp.float32)]
    sub x2 -> x0, matrix products: 31.7 us -> none  [tile_backward(): weights = jnp.where(allowed[None, None, :], jnp.exp(scores - highest), 0.0)]
    ppermute x4 -> x24, waiting for transfers between devices: 74.4 us -> 93.4 us  [send(): return lax.ppermute(block, AXES, pairs)]
    another operation x5 -> x3, other arithmetic: 20 us -> 3.18 us  [the longest x2 3.1 us: gather_weight(): jnp.stack([line] + [send(line, from_second(step)) for step in (1, 2, 3)])]
    another operation x3 -> x2, local copies, waits for them, and re-layouts: 14 us -> 0.03 us  [gather_weight(): jnp.stack([quarter, partner])]
    ppermute x4 -> x24, starting transfers between devices: 108 us -> 95.4 us  [send(): return lax.ppermute(block, AXES, pairs)]
  transfers between devices with their start and end apart: 7 -> 26, of which waited for: 3 -> 11; matrix products, arithmetic and copies ran while one was open for 44% -> 4% of each run, Pallas kernels for 0% -> 27%
where the time goes in v1:
time: 369 us; the launch traced here: 366 us
  Pallas kernels  119 us (32%)
  starting transfers between devices  95.5 us (26%)
  waiting for transfers between devices  93.5 us (25%)
  between operations  25.4 us (7%)
  local copies, waits for them, and re-layouts  20.5 us (6%)
  other arithmetic  12.1 us (3%)
    ppermute x24, starting transfers between devices, send(): return lax.ppermute(block, AXES, pairs)  95.4 us
    ppermute x24, waiting for transfers between devices, send(): return lax.ppermute(block, AXES, pairs)  93.4 us
    pallas_call x2, Pallas kernels, own_grads(): pl.pallas_call(own_kernel, grid_spec=pltpu.PrefetchScalarGridSpec(num_sca...  27.1 us
    pallas_call x2, Pallas kernels, back(): pl.pallas_call(back_kernel, grid_spec=pltpu.PrefetchScalarGridSpec(num_sc...  25.1 us
    pallas_call x2, Pallas kernels, far_grads(): pl.pallas_call(far_kernel, grid_spec=pltpu.PrefetchScalarGridSpec(num_sca...  22 us
    pallas_call x1, Pallas kernels, weight_term(): pl.pallas_call(weight_term_kernel, grid=(4, 4), in_specs=[pl.BlockSpec((S...  19.3 us
    unnamed x57, local copies, waits for them, and re-layouts  18.1 us
    pallas_call x1, Pallas kernels, own_stats(): pl.pallas_call(own_stats_kernel, grid_spec=pltpu.PrefetchScalarGridSpec(n...  11.6 us
  transfers between devices with their start and end apart: 26, of which 11 were waited for; matrix products, arithmetic and copies ran while one was open for 4% of the time, Pallas kernels for 27%

profile of v1, /device:TPU:0, one launch (start us, length us, event | category | flops | bytes accessed | tf_op | source)
XLA Modules:
  0.0 365.9 jit_solution(11226881296699353818)
XLA Ops:
  7.2 1.7 copy-done.2
  8.9 19.3 %weight_term.1 = bf16[4,2,4,2,96,768]{5,4,3,2,1,0:T(8,128)(2,1)} custom-call(bf16[768,1536]{1,0:T(8,128)(2,1)S(1)} %bitcast.53, bf16[768,3072]{1,0:T(8,128)(2,1)} %bitcast.65), custom_call_target="tpu_custom_call" | custom-call | flops 7247757312 | bytes 35000000 | tf_op jit(solution)/shard_map/weight_term/pallas_call | solution.py:363
  28.4 1.7 collective-permute-start
  30.1 3.8 %collective-permute-done = bf16[96,768]{1,0:T(8,128)(2,1)S(1)} collective-permute-done((bf16[96,768]{1,0:T(8,128)(2,1)S(1)}, bf16[96,768]{1,0:T(8,128)(2,1)S(1)}, u32[]{:S(2)}, u32[]{:S(2)}) %collective-permute-start) | collective-permute-done | bytes 147488 | tf_op jit(solution)/shard_map/ppermute | solution.py:75
  33.9 1.9 collective-permute-start.3
  35.8 2.9 collective-permute-start.2
  38.7 1.3 collective-permute-start.1
  40.1 1.8 collective-permute-done.3
  42.0 4.6 %collective-permute-done.2 = bf16[2,96,768]{2,1,0:T(8,128)(2,1)S(1)} collective-permute-done((bf16[2,96,768]{2,1,0:T(8,128)(2,1)S(1)}, bf16[2,96,768]{2,1,0:T(8,128)(2,1)S(1)}, u32[]{:S(2)}, u32[]{:S(2)}) %collective-permute-start.2) | collective-permute-done | bytes 294944 | tf_op jit(solution)/shard_map/ppermute | solution.py:75
  46.8 4.0 %collective-permute-start.5 = (bf16[4,2,96,768]{3,2,1,0:T(8,128)(2,1)S(1)}, bf16[4,2,96,768]{3,2,1,0:T(8,128)(2,1)S(1)}, u32[]{:S(2)}, u32[]{:S(2)}) collective-permute-start(bf16[4,2,96,768]{3,2,1,0:T(8,128)(2,1)S(1)} %get-tuple-element.57), channel_id=1, source_target_pairs={{0,64},{1,9},{2,66},{3,11},{16,80},{17,25},{18,82},{19,27},{4,68},... | collective-permute-start | bytes 3538952 | tf_op jit(solution)/shard_map/ppermute | solution.py:75
  51.4 1.3 collective-permute-start.6
  52.8 12.3 %collective-permute-done.5 = bf16[4,2,96,768]{3,2,1,0:T(8,128)(2,1)S(1)} collective-permute-done((bf16[4,2,96,768]{3,2,1,0:T(8,128)(2,1)S(1)}, bf16[4,2,96,768]{3,2,1,0:T(8,128)(2,1)S(1)}, u32[]{:S(2)}, u32[]{:S(2)}) %collective-permute-start.5) | collective-permute-done | bytes 1179680 | tf_op jit(solution)/shard_map/ppermute | solution.py:75
  65.0 13.6 %collective-permute-done.4 = bf16[4,2,96,768]{3,2,1,0:T(8,128)(2,1)S(1)} collective-permute-done((bf16[4,2,96,768]{3,2,1,0:T(8,128)(2,1)S(1)}, bf16[4,2,96,768]{3,2,1,0:T(8,128)(2,1)S(1)}, u32[]{:S(2)}, u32[]{:S(2)}) %collective-permute-start.4) | collective-permute-done | bytes 1179680 | tf_op jit(solution)/shard_map/ppermute | solution.py:75
  78.6 2.9 pad_maximum_fusion.mine
  81.6 1.6 slice_bitcast_fusion
  83.1 1.4 collective-permute-start.9
  84.5 7.1 %collective-permute-start.8 = (bf16[384,1536]{1,0:T(8,128)(2,1)}, bf16[384,1536]{1,0:T(8,128)(2,1)}, u32[]{:S(2)}, u32[]{:S(2)}) collective-permute-start(bf16[384,1536]{1,0:T(8,128)(2,1)} %get-tuple-element.55), channel_id=1, source_target_pairs={{0,16},{1,17},{2,18},{3,19},{16,32},{17,33},{18,34},{19,35},{4,20}... | collective-permute-start | bytes 3538952 | tf_op jit(solution)/shard_map/ppermute | solution.py:75
  100.9 14.7 %collective-permute-done.9.qa = bf16[384,1536]{1,0:T(8,128)(2,1)S(1)} collective-permute-done((bf16[384,1536]{1,0:T(8,128)(2,1)}, bf16[384,1536]{1,0:T(8,128)(2,1)S(1)}, u32[]{:S(2)}, u32[]{:S(2)}) %collective-permute-start.9) | collective-permute-done | bytes 1179680 | tf_op jit(solution)/shard_map/ppermute | solution.py:75
  116.4 10.5 %far_stats.1 = (f32[12,1,384]{2,1,0:T(1,128)}, f32[12,1,384]{2,1,0:T(1,128)}) custom-call(s32[3]{0:T(128)S(1)} %pad_add_fusion.where, bf16[384,1536]{1,0:T(8,128)(2,1)} %collective-permute-done.8.qb, bf16[384,1536]{1,0:T(8,128)(2,1)S(1)} %collective-permute-done.9.qa, bf16[768,1536]{1,0:T(8,128)(2,1)S(1)} %bitcast.60), custom_call_target="tpu_custom_call" | custom-call | flops 905969664 | bytes 5000000 | tf_op jit(solution)/shard_map/far_stats/pallas_call | solution.py:143
  126.8 26.4 %collective-permute-start.10 = (f32[12,1,384]{2,1,0:T(1,128)}, f32[12,1,384]{2,1,0:T(1,128)}, u32[]{:S(2)}, u32[]{:S(2)}) collective-permute-start(f32[12,1,384]{2,1,0:T(1,128)} %get-tuple-element.28), channel_id=1, source_target_pairs={{0,16},{1,17},{2,18},{3,19},{16,32},{17,33},{18,34},{19,35},{4,20}... | collective-permute-start | bytes 55304 | tf_op jit(solution)/shard_map/ppermute | solution.py:75
  153.2 1.3 collective-permute-start.11
  154.5 11.6 %own_stats.1 = f32[12,1,768]{2,1,0:T(1,128)S(1)} custom-call(s32[3]{0:T(128)S(1)} %pad_add_fusion.where, bf16[768,1536]{1,0:T(8,128)(2,1)S(1)} %bitcast.64, bf16[768,1536]{1,0:T(8,128)(2,1)S(1)} %bitcast.61, f32[2,768]{1,0:T(2,128)S(1)} %add_select_fusion.bias), custom_call_target="tpu_custom_call" | custom-call | flops 1811939328 | bytes 5000000 | tf_op jit(solution)/shard_map/own_stats/pallas_call | solution.py:113
  170.5 1.6 broadcast_select_fusion.2
  172.8 12.1 %out_back.3 = (bf16[2,384,384]{2,1,0:T(8,128)(2,1)S(1)}, bf16[2,384,384]{2,1,0:T(8,128)(2,1)S(1)}, f32[2,3,1,768]{3,2,1,0:T(1,128)S(1)}) custom-call(s32[3]{0:T(128)S(1)} %pad_add_fusion.where, bf16[768,3072]{1,0:T(8,128)(2,1)} %bitcast.66, bf16[4,4,2,96,768]{4,3,2,1,0:T(8,128)(2,1)} %pad_maximum_fusion.mine, ...), custom_call_target="tpu_custom_call" | custom-call | flops 3623878656 | bytes 18000000 | tf_op jit(solution)/shard_map/out_back/pallas_call | solution.py:210
  187.2 13.0 %out_back.2 = (bf16[2,384,384]{2,1,0:T(8,128)(2,1)S(1)}, bf16[2,384,384]{2,1,0:T(8,128)(2,1)}, f32[2,3,1,768]{3,2,1,0:T(1,128)S(1)}) custom-call(s32[3]{0:T(128)S(1)} %pad_add_fusion.where, bf16[768,3072]{1,0:T(8,128)(2,1)} %bitcast.67, bf16[4,4,2,96,768]{4,3,2,1,0:T(8,128)(2,1)} %pad_maximum_fusion.mine, ...), custom_call_target="tpu_custom_call" | custom-call | flops 3623878656 | bytes 18000000 | tf_op jit(solution)/shard_map/out_back/pallas_call | solution.py:210
  202.6 1.3 collective-permute-start.22
  204.7 1.4 pad_maximum_fusion.3
  207.4 9.0 %collective-permute-start.16 = (bf16[2,384,384]{2,1,0:T(8,128)(2,1)}, bf16[2,384,384]{2,1,0:T(8,128)(2,1)}, u32[]{:S(2)}, u32[]{:S(2)}) collective-permute-start(bf16[2,384,384]{2,1,0:T(8,128)(2,1)} %copy-done.21), channel_id=1, source_target_pairs={{0,16},{1,17},{2,18},{3,19},{16,32},{17,33},{18,34},{19,35},{4,20}... | collective-permute-start | bytes 1769480 | tf_op jit(solution)/shard_map/ppermute | solution.py:75
  217.7 7.0 %collective-permute-start.12 = (bf16[2,384,384]{2,1,0:T(8,128)(2,1)}, bf16[2,384,384]{2,1,0:T(8,128)(2,1)}, u32[]{:S(2)}, u32[]{:S(2)}) collective-permute-start(bf16[2,384,384]{2,1,0:T(8,128)(2,1)} %copy-done.17), channel_id=1, source_target_pairs={{0,16},{1,17},{2,18},{3,19},{16,32},{17,33},{18,34},{19,35},{4,20}... | collective-permute-start | bytes 1769480 | tf_op jit(solution)/shard_map/ppermute | solution.py:75
  225.8 3.8 %collective-permute-start.23 = (bf16[96,768]{1,0:T(8,128)(2,1)S(1)}, bf16[96,768]{1,0:T(8,128)(2,1)S(1)}, u32[]{:S(2)}, u32[]{:S(2)}) collective-permute-start(bf16[96,768]{1,0:T(8,128)(2,1)S(1)} %add_convert_fusion), channel_id=1, source_target_pairs={{0,16},{1,17},{2,18},{3,19},{16,0},{17,1},{18,2},{19,3},{4,20},{5,... | collective-permute-start | bytes 442376 | tf_op jit(solution)/shard_map/ppermute | solution.py:75
  233.3 13.6 %own_grads.3 = (f32[2,768,384]{2,1,0:T(8,128)S(1)}, f32[2,768,384]{2,1,0:T(8,128)S(1)}, f32[2,768,384]{2,1,0:T(8,128)}) custom-call(s32[3]{0:T(128)S(1)} %pad_add_fusion.where, bf16[768,1536]{1,0:T(8,128)(2,1)} %bitcast.62, bf16[768,1536]{1,0:T(8,128)(2,1)} %bitcast.56, bf16[768,1536]{1,0:T(8,128)(2,1)} %bitcast.68, bf16[2,384,384]{2,1,0:T(8,128)(2,1)S(1)} %copy-done.22, ...), custom_call_target="tpu_custom_call" | custom-call | flops 4529848320 | bytes 14000000 | tf_op jit(solution)/shard_map/own_grads/pallas_call | solution.py:260
  246.9 1.4 copy-done.9
  248.3 12.1 %collective-permute-done.23 = bf16[96,768]{1,0:T(8,128)(2,1)S(1)} collective-permute-done((bf16[96,768]{1,0:T(8,128)(2,1)S(1)}, bf16[96,768]{1,0:T(8,128)(2,1)S(1)}, u32[]{:S(2)}, u32[]{:S(2)}) %collective-permute-start.23) | collective-permute-done | bytes 147488 | tf_op jit(solution)/shard_map/ppermute | solution.py:75
  260.5 1.3 collective-permute-start.13
  265.2 13.6 %own_grads.2 = (f32[2,768,384]{2,1,0:T(8,128)S(1)}, f32[2,768,384]{2,1,0:T(8,128)S(1)}, f32[2,768,384]{2,1,0:T(8,128)}) custom-call(s32[3]{0:T(128)S(1)} %pad_add_fusion.where, bf16[768,1536]{1,0:T(8,128)(2,1)} %bitcast.63, bf16[768,1536]{1,0:T(8,128)(2,1)} %bitcast.57, bf16[768,1536]{1,0:T(8,128)(2,1)} %bitcast.69, bf16[2,384,384]{2,1,0:T(8,128)(2,1)S(1)} %copy-done.18, ...), custom_call_target="tpu_custom_call" | custom-call | flops 4529848320 | bytes 14000000 | tf_op jit(solution)/shard_map/own_grads/pallas_call | solution.py:260
  278.7 1.4 copy-done.6
  280.1 6.0 %collective-permute-start.14 = (f32[12,2,384]{2,1,0:T(2,128)S(1)}, f32[12,2,384]{2,1,0:T(2,128)S(1)}, u32[]{:S(2)}, u32[]{:S(2)}) collective-permute-start(f32[12,2,384]{2,1,0:T(2,128)S(1)} %copy-done.23), channel_id=1, source_target_pairs={{0,16},{1,17},{2,18},{3,19},{16,32},{17,33},{18,34},{19,35},{4,20}... | collective-permute-start | bytes 110600 | tf_op jit(solution)/shard_map/ppermute | solution.py:75
  287.9 11.0 %far_grads.2 = (bf16[2,384,384]{2,1,0:T(8,128)(2,1)S(1)}, bf16[2,384,384]{2,1,0:T(8,128)(2,1)S(1)}, bf16[768,1536]{1,0:T(8,128)(2,1)}, bf16[768,1536]{1,0:T(8,128)(2,1)}) custom-call(s32[3]{0:T(128)S(1)} %pad_add_fusion.where, bf16[384,1536]{1,0:T(8,128)(2,1)} %collective-permute-done.8.qb, bf16[384,1536]{1,0:T(8,128)(2,1)S(1)} %collective-permute-done.9.qa, ...), custom_call_target="tpu_custom_call" | custom-call | flops 2264924160 | bytes 12000000 | tf_op jit(solution)/shard_map/far_grads/pallas_call | solution.py:309
  298.9 5.8 %collective-permute-start.20 = (bf16[2,384,384]{2,1,0:T(8,128)(2,1)S(1)}, bf16[2,384,384]{2,1,0:T(8,128)(2,1)S(1)}, u32[]{:S(2)}, u32[]{:S(2)}) collective-permute-start(bf16[2,384,384]{2,1,0:T(8,128)(2,1)S(1)} %get-tuple-element.44), channel_id=1, source_target_pairs={{0,16},{1,17},{2,18},{3,19},{16,32},{17,33},{18,34},{19,35},{4,20}... | collective-permute-start | bytes 1769480 | tf_op jit(solution)/shard_map/ppermute | solution.py:75
  304.7 1.3 collective-permute-start.21
  306.0 11.0 %far_grads.3 = (bf16[2,384,384]{2,1,0:T(8,128)(2,1)S(1)}, bf16[2,384,384]{2,1,0:T(8,128)(2,1)S(1)}, bf16[768,1536]{1,0:T(8,128)(2,1)}, bf16[768,1536]{1,0:T(8,128)(2,1)}) custom-call(s32[3]{0:T(128)S(1)} %pad_add_fusion.where, bf16[384,1536]{1,0:T(8,128)(2,1)} %collective-permute-done.8.qb, ...), custom_call_target="tpu_custom_call", output_to_operand_aliasing={{2}: (11, {}), {3}: (12, {})} | custom-call | flops 2264924160 | bytes 12000000 | tf_op jit(solution)/shard_map/far_grads/pallas_call | solution.py:309
  317.0 6.1 %collective-permute-start.18 = (bf16[2,384,384]{2,1,0:T(8,128)(2,1)S(1)}, bf16[2,384,384]{2,1,0:T(8,128)(2,1)S(1)}, u32[]{:S(2)}, u32[]{:S(2)}) collective-permute-start(bf16[2,384,384]{2,1,0:T(8,128)(2,1)S(1)} %get-tuple-element.41), channel_id=1, source_target_pairs={{0,16},{1,17},{2,18},{3,19},{16,32},{17,33},{18,34},{19,35},{4,20}... | collective-permute-start | bytes 1769480 | tf_op jit(solution)/shard_map/ppermute | solution.py:75
  323.1 1.3 collective-permute-start.19
  324.4 9.9 %collective-permute-done.21.high = bf16[2,384,384]{2,1,0:T(8,128)(2,1)S(1)} collective-permute-done((bf16[2,384,384]{2,1,0:T(8,128)(2,1)S(1)}, bf16[2,384,384]{2,1,0:T(8,128)(2,1)S(1)}, u32[]{:S(2)}, u32[]{:S(2)}) %collective-permute-start.21) | collective-permute-done | bytes 589856 | tf_op jit(solution)/shard_map/ppermute | solution.py:75
  334.2 1.7 join_query_grad.2.rest_0_
  336.0 19.0 %collective-permute-done.19.high = bf16[2,384,384]{2,1,0:T(8,128)(2,1)S(1)} collective-permute-done((bf16[2,384,384]{2,1,0:T(8,128)(2,1)S(1)}, bf16[2,384,384]{2,1,0:T(8,128)(2,1)S(1)}, u32[]{:S(2)}, u32[]{:S(2)}) %collective-permute-start.19) | collective-permute-done | bytes 589856 | tf_op jit(solution)/shard_map/ppermute | solution.py:75
  355.0 1.7 join_query_grad.3
  356.7 2.4 copy.19
  (105 shorter events, 23.2 us)
Async XLA Ops:
  7.2 21.2 %copy-start = (bf16[96,3072]{1,0:T(8,128)(2,1)S(1)}, bf16[96,3072]{1,0:T(8,128)(2,1)}, u32[]{:S(2)}) copy-start(bf16[96,3072]{1,0:T(8,128)(2,1)} %param.13) | copy-start | bytes 1769476
  7.2 194.4 %reduce-scatter.2.cloned.1.call-start = ((), (), s32[]{:S(2)}) async-start(), calls=%async_computation.1 | async-start | bytes 9732096 | tf_op jit(solution)/shard_map/reduce_scatter | solution.py:394
  7.2 1.7 copy-start.2
  28.3 328.4 %all-gather.2.cloned.1.call-start = ((), (), s32[]{:S(2)}) async-start(), calls=%async_computation.2 | async-start | bytes 1474560 | tf_op jit(solution)/shard_map/all_gather | solution.py:411
  28.4 5.5 %collective-permute-start = (bf16[96,768]{1,0:T(8,128)(2,1)S(1)}, bf16[96,768]{1,0:T(8,128)(2,1)S(1)}, u32[]{:S(2)}, u32[]{:S(2)}) collective-permute-start(bf16[96,768]{1,0:T(8,128)(2,1)S(1)} %constant_dynamic-slice_fusion), channel_id=1, source_target_pairs={{0,2},{1,3},{2,0},{3,1},{16,18},{17,19},{18,16},{19,17},{4,6},{5,7... | collective-permute-start | bytes 442376 | tf_op jit(solution)/shard_map/ppermute | solution.py:75
  33.9 8.0 %collective-permute-start.3 = (bf16[2,96,768]{2,1,0:T(8,128)(2,1)S(1)}, bf16[2,96,768]{2,1,0:T(8,128)(2,1)S(1)}, u32[]{:S(2)}, u32[]{:S(2)}) collective-permute-start(bf16[2,96,768]{2,1,0:T(8,128)(2,1)S(1)} %maximum_select_fusion.1), channel_id=1, source_target_pairs={{0,4},{1,33},{2,6},{3,35},{16,20},{17,49},{18,22},{19,51},{4,8},{5... | collective-permute-start | bytes 884744 | tf_op jit(solution)/shard_map/ppermute | solution.py:75
  35.8 10.8 %collective-permute-start.2 = (bf16[2,96,768]{2,1,0:T(8,128)(2,1)S(1)}, bf16[2,96,768]{2,1,0:T(8,128)(2,1)S(1)}, u32[]{:S(2)}, u32[]{:S(2)}) collective-permute-start(bf16[2,96,768]{2,1,0:T(8,128)(2,1)S(1)} %maximum_select_fusion.1), channel_id=1, source_target_pairs={{0,8},{1,65},{2,10},{3,67},{16,24},{17,81},{18,26},{19,83},{4,12},... | collective-permute-start | bytes 884744 | tf_op jit(solution)/shard_map/ppermute | solution.py:75
  38.7 7.9 %collective-permute-start.1 = (bf16[2,96,768]{2,1,0:T(8,128)(2,1)S(1)}, bf16[2,96,768]{2,1,0:T(8,128)(2,1)S(1)}, u32[]{:S(2)}, u32[]{:S(2)}) collective-permute-start(bf16[2,96,768]{2,1,0:T(8,128)(2,1)S(1)} %maximum_select_fusion.1), channel_id=1, source_target_pairs={{0,12},{1,97},{2,14},{3,99},{16,28},{17,113},{18,30},{19,115},{4,0... | collective-permute-start | bytes 884744 | tf_op jit(solution)/shard_map/ppermute | solution.py:75
  46.8 18.2 %collective-permute-start.5 = (bf16[4,2,96,768]{3,2,1,0:T(8,128)(2,1)S(1)}, bf16[4,2,96,768]{3,2,1,0:T(8,128)(2,1)S(1)}, u32[]{:S(2)}, u32[]{:S(2)}) collective-permute-start(bf16[4,2,96,768]{3,2,1,0:T(8,128)(2,1)S(1)} %get-tuple-element.57), channel_id=1, source_target_pairs={{0,64},{1,9},{2,66},{3,11},{16,80},{17,25},{18,82},{19,27},{4,68},... | collective-permute-start | bytes 3538952 | tf_op jit(solution)/shard_map/ppermute | solution.py:75
  50.7 27.9 %collective-permute-start.4 = (bf16[4,2,96,768]{3,2,1,0:T(8,128)(2,1)S(1)}, bf16[4,2,96,768]{3,2,1,0:T(8,128)(2,1)S(1)}, u32[]{:S(2)}, u32[]{:S(2)}) collective-permute-start(bf16[4,2,96,768]{3,2,1,0:T(8,128)(2,1)S(1)} %get-tuple-element.57), channel_id=1, source_target_pairs={{0,96},{1,13},{2,98},{3,15},{16,112},{17,29},{18,114},{19,31},{4,1... | collective-permute-start | bytes 3538952 | tf_op jit(solution)/shard_map/ppermute | solution.py:75
  51.4 27.2 %collective-permute-start.6 = (bf16[4,2,96,768]{3,2,1,0:T(8,128)(2,1)S(1)}, bf16[4,2,96,768]{3,2,1,0:T(8,128)(2,1)S(1)}, u32[]{:S(2)}, u32[]{:S(2)}) collective-permute-start(bf16[4,2,96,768]{3,2,1,0:T(8,128)(2,1)S(1)} %get-tuple-element.57), channel_id=1, source_target_pairs={{0,32},{1,5},{2,34},{3,7},{16,48},{17,21},{18,50},{19,23},{4,36},{... | collective-permute-start | bytes 3538952 | tf_op jit(solution)/shard_map/ppermute | solution.py:75
  78.6 2.9 copy-start.7
  81.5 10.1 %copy-start.26 = (s32[1,8]{1,0:T(1,128)S(1)}, s32[1,8]{1,0:T(1,128)}, u32[]{:S(2)}) copy-start(s32[1,8]{1,0:T(1,128)} %param.15) | copy-start | bytes 100
  81.5 10.8 %copy-start.27 = (s32[1,2,3]{2,1,0:T(2,128)S(1)}, s32[1,2,3]{2,1,0:T(2,128)}, u32[]{:S(2)}) copy-start(s32[1,2,3]{2,1,0:T(2,128)} %param.14) | copy-start | bytes 76
  81.5 34.8 %copy-start.4 = (bf16[1,768,1536]{2,1,0:T(8,128)(2,1)S(1)}, bf16[1,768,1536]{2,1,0:T(8,128)(2,1)}, u32[]{:S(2)}) copy-start(bf16[1,768,1536]{2,1,0:T(8,128)(2,1)} %param.9) | copy-start | bytes 7077892
  81.5 91.3 %collective-permute-start.7 = (bf16[4,4,2,96,768]{4,3,2,1,0:T(8,128)(2,1)}, bf16[4,4,2,96,768]{4,3,2,1,0:T(8,128)(2,1)}, u32[]{:S(2)}, u32[]{:S(2)}) collective-permute-start(bf16[4,4,2,96,768]{4,3,2,1,0:T(8,128)(2,1)} %pad_maximum_fusion.mine), channel_id=1, source_target_pairs={{0,1},{1,0},{2,3},{3,2},{16,17},{17,16},{18,19},{19,18},{4,5},{5,4... | collective-permute-start | bytes 14155784 | tf_op jit(solution)/shard_map/ppermute | solution.py:75
  83.1 32.5 %collective-permute-start.9 = (bf16[384,1536]{1,0:T(8,128)(2,1)}, bf16[384,1536]{1,0:T(8,128)(2,1)S(1)}, u32[]{:S(2)}, u32[]{:S(2)}) collective-permute-start(bf16[384,1536]{1,0:T(8,128)(2,1)} %get-tuple-element.54), channel_id=1, source_target_pairs={{16,0},{17,1},{18,2},{19,3},{20,4},{21,5},{22,6},{23,7},{24,8},{25... | collective-permute-start | bytes 3538952 | tf_op jit(solution)/shard_map/ppermute | solution.py:75
  84.5 31.8 %collective-permute-start.8 = (bf16[384,1536]{1,0:T(8,128)(2,1)}, bf16[384,1536]{1,0:T(8,128)(2,1)}, u32[]{:S(2)}, u32[]{:S(2)}) collective-permute-start(bf16[384,1536]{1,0:T(8,128)(2,1)} %get-tuple-element.55), channel_id=1, source_target_pairs={{0,16},{1,17},{2,18},{3,19},{16,32},{17,33},{18,34},{19,35},{4,20}... | collective-permute-start | bytes 3538952 | tf_op jit(solution)/shard_map/ppermute | solution.py:75
  116.4 38.1 %copy-start.5 = (bf16[1,768,1536]{2,1,0:T(8,128)(2,1)S(1)}, bf16[1,768,1536]{2,1,0:T(8,128)(2,1)}, u32[]{:S(2)}) copy-start(bf16[1,768,1536]{2,1,0:T(8,128)(2,1)} %param.9) | copy-start | bytes 7077892
  116.4 38.1 %copy-start.8 = (bf16[1,768,1536]{2,1,0:T(8,128)(2,1)S(1)}, bf16[1,768,1536]{2,1,0:T(8,128)(2,1)}, u32[]{:S(2)}) copy-start(bf16[1,768,1536]{2,1,0:T(8,128)(2,1)} %param.8) | copy-start | bytes 7077892
  126.8 43.6 %collective-permute-start.10 = (f32[12,1,384]{2,1,0:T(1,128)}, f32[12,1,384]{2,1,0:T(1,128)}, u32[]{:S(2)}, u32[]{:S(2)}) collective-permute-start(f32[12,1,384]{2,1,0:T(1,128)} %get-tuple-element.28), channel_id=1, source_target_pairs={{0,16},{1,17},{2,18},{3,19},{16,32},{17,33},{18,34},{19,35},{4,20}... | collective-permute-start | bytes 55304 | tf_op jit(solution)/shard_map/ppermute | solution.py:75
  153.2 17.3 %collective-permute-start.11 = (f32[12,1,384]{2,1,0:T(1,128)}, f32[12,1,384]{2,1,0:T(1,128)}, u32[]{:S(2)}, u32[]{:S(2)}) collective-permute-start(f32[12,1,384]{2,1,0:T(1,128)} %get-tuple-element.29), channel_id=1, source_target_pairs={{16,0},{17,1},{18,2},{19,3},{20,4},{21,5},{22,6},{23,7},{24,8},{25... | collective-permute-start | bytes 55304 | tf_op jit(solution)/shard_map/ppermute | solution.py:75
  154.5 17.5 %copy-start.25 = (pred[768]{0:T(1024)(128)(4,1)S(1)}, pred[768]{0:T(1024)(128)(4,1)}, u32[]{:S(2)}) copy-start(pred[768]{0:T(1024)(128)(4,1)} %copy-done.24) | copy-start | bytes 2308
  154.5 18.3 %copy-start.3 = (bf16[1,768,1536]{2,1,0:T(8,128)(2,1)S(1)}, bf16[1,768,1536]{2,1,0:T(8,128)(2,1)}, u32[]{:S(2)}) copy-start(bf16[1,768,1536]{2,1,0:T(8,128)(2,1)} %param.11) | copy-start | bytes 7077892
  185.6 0.8 copy-start.19
  186.4 0.8 copy-start.21
  200.8 0.9 copy-start.17
  202.6 22.1 %collective-permute-start.22 = (bf16[96,768]{1,0:T(8,128)(2,1)S(1)}, bf16[96,768]{1,0:T(8,128)(2,1)S(1)}, u32[]{:S(2)}, u32[]{:S(2)}) collective-permute-start(bf16[96,768]{1,0:T(8,128)(2,1)S(1)} %broadcast_select_fusion), channel_id=1, source_target_pairs={{0,2},{1,3},{2,0},{3,1},{16,18},{17,19},{18,16},{19,17},{4,6},{5,7... | collective-permute-start | bytes 442376 | tf_op jit(solution)/shard_map/ppermute | solution.py:75
  206.2 74.0 %collective-permute-start.15 = (f32[12,2,384]{2,1,0:T(2,128)}, f32[12,2,384]{2,1,0:T(2,128)}, u32[]{:S(2)}, u32[]{:S(2)}) collective-permute-start(f32[12,2,384]{2,1,0:T(2,128)} %get-tuple-element.58), channel_id=1, source_target_pairs={{16,0},{17,1},{18,2},{19,3},{20,4},{21,5},{22,6},{23,7},{24,8},{25... | collective-permute-start | bytes 110600 | tf_op jit(solution)/shard_map/ppermute | solution.py:75
  207.4 80.4 %collective-permute-start.16 = (bf16[2,384,384]{2,1,0:T(8,128)(2,1)}, bf16[2,384,384]{2,1,0:T(8,128)(2,1)}, u32[]{:S(2)}, u32[]{:S(2)}) collective-permute-start(bf16[2,384,384]{2,1,0:T(8,128)(2,1)} %copy-done.21), channel_id=1, source_target_pairs={{0,16},{1,17},{2,18},{3,19},{16,32},{17,33},{18,34},{19,35},{4,20}... | collective-permute-start | bytes 1769480 | tf_op jit(solution)/shard_map/ppermute | solution.py:75
  216.4 71.4 %collective-permute-start.17 = (bf16[2,384,384]{2,1,0:T(8,128)(2,1)}, bf16[2,384,384]{2,1,0:T(8,128)(2,1)}, u32[]{:S(2)}, u32[]{:S(2)}) collective-permute-start(bf16[2,384,384]{2,1,0:T(8,128)(2,1)} %copy-done.19), channel_id=1, source_target_pairs={{16,0},{17,1},{18,2},{19,3},{20,4},{21,5},{22,6},{23,7},{24,8},{25... | collective-permute-start | bytes 1769480 | tf_op jit(solution)/shard_map/ppermute | solution.py:75
  217.7 88.2 %collective-permute-start.12 = (bf16[2,384,384]{2,1,0:T(8,128)(2,1)}, bf16[2,384,384]{2,1,0:T(8,128)(2,1)}, u32[]{:S(2)}, u32[]{:S(2)}) collective-permute-start(bf16[2,384,384]{2,1,0:T(8,128)(2,1)} %copy-done.17), channel_id=1, source_target_pairs={{0,16},{1,17},{2,18},{3,19},{16,32},{17,33},{18,34},{19,35},{4,20}... | collective-permute-start | bytes 1769480 | tf_op jit(solution)/shard_map/ppermute | solution.py:75
  225.8 34.7 %collective-permute-start.23 = (bf16[96,768]{1,0:T(8,128)(2,1)S(1)}, bf16[96,768]{1,0:T(8,128)(2,1)S(1)}, u32[]{:S(2)}, u32[]{:S(2)}) collective-permute-start(bf16[96,768]{1,0:T(8,128)(2,1)S(1)} %add_convert_fusion), channel_id=1, source_target_pairs={{0,16},{1,17},{2,18},{3,19},{16,0},{17,1},{18,2},{19,3},{4,20},{5,... | collective-permute-start | bytes 442376 | tf_op jit(solution)/shard_map/ppermute | solution.py:75
  229.6 0.9 copy-start.10
  231.2 1.1 copy-start.20
  232.3 1.1 copy-start.22
  246.9 1.4 copy-start.9
  260.5 45.5 %collective-permute-start.13 = (bf16[2,384,384]{2,1,0:T(8,128)(2,1)}, bf16[2,384,384]{2,1,0:T(8,128)(2,1)}, u32[]{:S(2)}, u32[]{:S(2)}) collective-permute-start(bf16[2,384,384]{2,1,0:T(8,128)(2,1)} %get-tuple-element.27.down), channel_id=1, source_target_pairs={{16,0},{17,1},{18,2},{19,3},{20,4},{21,5},{22,6},{23,7},{24,8},{25... | collective-permute-start | bytes 1769480 | tf_op jit(solution)/shard_map/ppermute | solution.py:75
  262.5 0.9 copy-start.11
  264.1 1.1 copy-start.18
  265.2 15.0 %copy-start.23 = (f32[12,2,384]{2,1,0:T(2,128)S(1)}, f32[12,2,384]{2,1,0:T(2,128)}, u32[]{:S(2)}) copy-start(f32[12,2,384]{2,1,0:T(2,128)} %get-tuple-element.59) | copy-start | bytes 110596
  278.7 1.4 copy-start.6
  280.1 7.7 %collective-permute-start.14 = (f32[12,2,384]{2,1,0:T(2,128)S(1)}, f32[12,2,384]{2,1,0:T(2,128)S(1)}, u32[]{:S(2)}, u32[]{:S(2)}) collective-permute-start(f32[12,2,384]{2,1,0:T(2,128)S(1)} %copy-done.23), channel_id=1, source_target_pairs={{0,16},{1,17},{2,18},{3,19},{16,32},{17,33},{18,34},{19,35},{4,20}... | collective-permute-start | bytes 110600 | tf_op jit(solution)/shard_map/ppermute | solution.py:75
  298.9 25.5 %collective-permute-start.20 = (bf16[2,384,384]{2,1,0:T(8,128)(2,1)S(1)}, bf16[2,384,384]{2,1,0:T(8,128)(2,1)S(1)}, u32[]{:S(2)}, u32[]{:S(2)}) collective-permute-start(bf16[2,384,384]{2,1,0:T(8,128)(2,1)S(1)} %get-tuple-element.44), channel_id=1, source_target_pairs={{0,16},{1,17},{2,18},{3,19},{16,32},{17,33},{18,34},{19,35},{4,20}... | collective-permute-start | bytes 1769480 | tf_op jit(solution)/shard_map/ppermute | solution.py:75
  304.7 29.6 %collective-permute-start.21 = (bf16[2,384,384]{2,1,0:T(8,128)(2,1)S(1)}, bf16[2,384,384]{2,1,0:T(8,128)(2,1)S(1)}, u32[]{:S(2)}, u32[]{:S(2)}) collective-permute-start(bf16[2,384,384]{2,1,0:T(8,128)(2,1)S(1)} %get-tuple-element.45), channel_id=1, source_target_pairs={{16,0},{17,1},{18,2},{19,3},{20,4},{21,5},{22,6},{23,7},{24,8},{25... | collective-permute-start | bytes 1769480 | tf_op jit(solution)/shard_map/ppermute | solution.py:75
  317.0 19.0 %collective-permute-start.18 = (bf16[2,384,384]{2,1,0:T(8,128)(2,1)S(1)}, bf16[2,384,384]{2,1,0:T(8,128)(2,1)S(1)}, u32[]{:S(2)}, u32[]{:S(2)}) collective-permute-start(bf16[2,384,384]{2,1,0:T(8,128)(2,1)S(1)} %get-tuple-element.41), channel_id=1, source_target_pairs={{0,16},{1,17},{2,18},{3,19},{16,32},{17,33},{18,34},{19,35},{4,20}... | collective-permute-start | bytes 1769480 | tf_op jit(solution)/shard_map/ppermute | solution.py:75
  323.1 31.9 %collective-permute-start.19 = (bf16[2,384,384]{2,1,0:T(8,128)(2,1)S(1)}, bf16[2,384,384]{2,1,0:T(8,128)(2,1)S(1)}, u32[]{:S(2)}, u32[]{:S(2)}) collective-permute-start(bf16[2,384,384]{2,1,0:T(8,128)(2,1)S(1)} %get-tuple-element.42), channel_id=1, source_target_pairs={{16,0},{17,1},{18,2},{19,3},{20,4},{21,5},{22,6},{23,7},{24,8},{25... | collective-permute-start | bytes 1769480 | tf_op jit(solution)/shard_map/ppermute | solution.py:75
  355.0 4.1 %copy-start.1 = (bf16[96,3072]{1,0:T(8,128)(2,1)S(1)}, bf16[96,3072]{1,0:T(8,128)(2,1)}, u32[]{:S(2)}) copy-start(bf16[96,3072]{1,0:T(8,128)(2,1)} %param.13) | copy-start | bytes 1769476
  (6 other events, 3.8 us)
Sparse Core Ops, SparseCore 0:
  28.4 123.3 reduce-scatter.1
  262.6 26.7 all-gather.1

commit v2 on v1

v2 whole, which is shorter than its diff:
```python
import functools
import math

import jax
import jax.numpy as jnp
from jax import lax
from jax.experimental import pallas as pl
from jax.experimental.pallas import tpu as pltpu
from jax.sharding import PartitionSpec as P

HDIM = 128
TILE = 384
SLAB = 768
FEAT = 1536
WIDTH = 3072
GROUP = 3
BLOCK = GROUP * HDIM
QUARTER = WIDTH // 4
ROWS = 96
AXES = ("seq", "dp")
SCALE = 1.0 / math.sqrt(HDIM)
SCALE2 = SCALE / math.log(2.0)
NEVER = 1e30
EXTRA = 16
LIMIT = 48 * 1024 * 1024
F32 = jnp.float32
BF16 = jnp.bfloat16


def place(z, y, x, core):
    return ((z % 4) * 2 + (x % 4) // 2) * 16 + (y % 4) * 4 + (x % 2) * 2 + core


def route(target):
    pairs = []
    for z in range(4):
        for y in range(4):
            for x in range(4):
                for core in range(2):
                    to = target(z, y, x, core)
                    if to is not None:
                        pairs.append((place(z, y, x, core), place(*to)))
    return pairs


def slab_step(step):
    def target(z, y, x, core):
        slab = z * 2 + x // 2 + step
        if slab < 0 or slab > 7:
            return None
        return (slab // 2, y, (slab % 2) * 2 + x % 2, core)

    return route(target)


UP = slab_step(1)
DOWN = slab_step(-1)
CORES = [frozenset(place(z, y, x, core) for z in range(4) for y in range(4) for x in range(4)) for core in range(2)]
ROUTE_A = [p for p in UP if p[0] in CORES[0]] + [p for p in DOWN if p[0] in CORES[1]]
ROUTE_B = [p for p in DOWN if p[0] in CORES[0]] + [p for p in UP if p[0] in CORES[1]]
SWAP_LOW = route(lambda z, y, x, core: (z, y, x ^ 1, core))
SWAP_HIGH = route(lambda z, y, x, core: (z, y, x ^ 2, core))
SWAP_CORE = route(lambda z, y, x, core: (z, y, x, 1 - core))


def from_along_z(step):
    return route(lambda z, y, x, core: (z - step, y, x, core))


def swap_first(bit):
    return route(
        lambda z, y, x, core: (z, y ^ bit, x, core) if core == 0 else (z ^ bit, y, x, core)
    )


def swap_second(bit):
    return route(
        lambda z, y, x, core: (z ^ bit, y, x, core) if core == 0 else (z, y ^ bit, x, core)
    )


def from_first(step):
    return route(
        lambda z, y, x, core: (z, y - step, x, core) if core == 0 else (z - step, y, x, core)
    )


def from_second(step):
    return route(
        lambda z, y, x, core: (z - step, y, x, core) if core == 0 else (z, y - step, x, core)
    )


def send(block, pairs):
    return lax.ppermute(block, AXES, pairs)


def dot(a, b, dims):
    return lax.dot_general(a, b, (dims, ((), ())), preferred_element_type=F32)


NT = ((1,), (1,))
NN = ((1,), (0,))
TN = ((0,), (0,))


def params(**kwargs):
    return pltpu.CompilerParams(vmem_limit_bytes=LIMIT, **kwargs)


HIDES = pl.CostEstimate(flops=100_000_000_000, bytes_accessed=1_000_000, transcendentals=0)
STEP = pl.CostEstimate(flops=100_000_000, bytes_accessed=100_000, transcendentals=0)


def columns(j):
    return slice(j * HDIM, (j + 1) * HDIM)


def first_tile(where):
    return pl.multiple_of((1 - where[2]) * TILE, TILE)


def second_tile(where):
    return pl.multiple_of(where[2] * TILE, TILE)


def own_stats_kernel(where, q, k, bias, out):
    for j in range(GROUP):
        keys = k[:, columns(j)]
        queries = jnp.concatenate(
            [q[pl.ds(start(where), TILE), columns(j)] for start in (first_tile, second_tile)], axis=0
        )
        first = dot(keys[:TILE], queries, NT) * SCALE2 + bias[0:1]
        second = dot(keys[TILE:], queries, NT) * SCALE2 + bias[1:2]
        highest = jnp.maximum(
            jnp.max(first, axis=0, keepdims=True), jnp.max(second, axis=0, keepdims=True)
        )
        total = jnp.sum(jnp.exp2(first - highest), axis=0, keepdims=True) + jnp.sum(
            jnp.exp2(second - highest), axis=0, keepdims=True
        )
        out[j] = highest + jnp.log2(total)


def own_stats(where, q, k, bias):
    wide = pl.BlockSpec((SLAB, BLOCK), lambda d, w: (0, lax.rem(w[0] + d, 4)))
    return pl.pallas_call(
        own_stats_kernel,
        grid_spec=pltpu.PrefetchScalarGridSpec(
            num_scalar_prefetch=1,
            grid=(4,),
            in_specs=[wide, wide, pl.BlockSpec((2, SLAB), lambda d, w: (0, 0))],
            out_specs=pl.BlockSpec((GROUP, 1, SLAB), lambda d, w: (d, 0, 0)),
        ),
        out_shape=jax.ShapeDtypeStruct((12, 1, SLAB), F32),
        compiler_params=params(),
        cost_estimate=STEP,
        name="own_stats",
    )(where, q, k, bias)


def far_stats_kernel(where, q, k, out):
    for j in range(GROUP):
        scores = dot(k[:, columns(j)], q[0, :, columns(j)], NT) * SCALE2
        highest = jnp.max(scores, axis=0, keepdims=True)
        total = jnp.sum(jnp.exp2(scores - highest), axis=0, keepdims=True)
        out[j] = highest + jnp.log2(total)


def key_tile(side, w):
    return w[2] if side == 0 else 1 - w[2]


def far_stats(where, side, q, k):
    return pl.pallas_call(
        far_stats_kernel,
        grid_spec=pltpu.PrefetchScalarGridSpec(
            num_scalar_prefetch=1,
            grid=(4,),
            in_specs=[
                pl.BlockSpec((1, TILE, BLOCK), lambda d, w: (d, 0, 0)),
                pl.BlockSpec((TILE, BLOCK), lambda d, w: (key_tile(side, w), lax.rem(w[0] + d, 4))),
            ],
            out_specs=pl.BlockSpec((GROUP, 1, TILE), lambda d, w: (d, 0, 0)),
        ),
        out_shape=jax.ShapeDtypeStruct((12, 1, TILE), F32),
        compiler_params=params(),
        cost_estimate=STEP,
        name="far_stats",
    )(where, q, k)


def back_kernel(where, g, mine_z, mine_y, other_z, other_y, o, back, dots, weight):
    for core in range(2):

        @pl.when(where[2] == core)
        def _():
            for dz in range(4):
                block = pl.ds(pl.multiple_of(lax.rem(where[1] + dz, 4) * QUARTER, QUARTER), QUARTER)
                for low in range(2):
                    for holder in range(2):
                        if core == holder:
                            piece = mine_z[dz, 0, low] if core == 0 else mine_y[0, dz, low]
                        else:
                            piece = other_y[0, dz, low] if core == 0 else other_z[dz, 0, low]
                        weight[pl.ds((low * 2 + holder) * ROWS, ROWS), block] = piece

    result = dot(g[...], weight[...], NT).astype(BF16)
    back[0, :TILE] = result
    back[0, TILE:] = jnp.zeros((EXTRA, BLOCK), BF16)
    products = result.astype(F32) * o[...].astype(F32)
    coarse = products.astype(BF16)
    fine = (products - coarse.astype(F32)).astype(BF16)
    ones = jnp.ones((8, HDIM), BF16)
    for j in range(GROUP):
        summed = dot(ones, coarse[:, columns(j)], NT) + dot(ones, fine[:, columns(j)], NT)
        dots[j] = summed[0:1]


def back(where, side, g, mine, other, o):
    def tile(w):
        return 1 - w[2] if side == 0 else w[2]

    along_z = pl.BlockSpec((4, 1, 2, ROWS, QUARTER), lambda d, w: (0, d, 0, 0, 0))
    along_y = pl.BlockSpec((1, 4, 2, ROWS, QUARTER), lambda d, w: (d, 0, 0, 0, 0))
    return pl.pallas_call(
        back_kernel,
        grid_spec=pltpu.PrefetchScalarGridSpec(
            num_scalar_prefetch=1,
            grid=(4,),
            in_specs=[
                pl.BlockSpec((TILE, WIDTH), lambda d, w: (tile(w), 0)),
                along_z,
                along_y,
                along_z,
                along_y,
                pl.BlockSpec((TILE, BLOCK), lambda d, w: (tile(w), lax.rem(w[0] + d, 4))),
            ],
            out_specs=[
                pl.BlockSpec((1, TILE + EXTRA, BLOCK), lambda d, w: (d, 0, 0)),
                pl.BlockSpec((GROUP, 1, TILE), lambda d, w: (d, 0, 0)),
            ],
            scratch_shapes=[pltpu.VMEM((BLOCK, WIDTH), BF16)],
        ),
        out_shape=[
            jax.ShapeDtypeStruct((4, TILE + EXTRA, BLOCK), BF16),
            jax.ShapeDtypeStruct((12, 1, TILE), F32),
        ],
        compiler_params=params(),
        cost_estimate=HIDES,
        name="out_back",
    )(where, g, mine, mine, other, other, o)


def pieces(value, count):
    parts = []
    for _ in range(count):
        part = lax.reduce_precision(value, exponent_bits=8, mantissa_bits=7)
        parts.append(part.astype(BF16))
        value = value - part
    return parts


def with_statistics(block, row, dots):
    parts = jnp.concatenate(pieces(row, 3) + pieces(dots, 2), axis=1)
    parts = parts.reshape(4, GROUP * 5, TILE)
    return lax.dynamic_update_slice(block, parts, (0, TILE, 0))


def own_kernel(where, q, k, v, back_a, back_b, rows, dots_a, dots_b, dk_a, dv_a, dk_b, dv_b, *rest):
    dq, dk, dv = rest[-3:]
    for j in range(GROUP):
        head = columns(j)
        queries = jnp.concatenate(
            [q[pl.ds(start(where), TILE), head] for start in (first_tile, second_tile)], axis=0
        )
        backs = jnp.concatenate([back_a[0, :TILE, head], back_b[0, :TILE, head]], axis=0)
        dots = jnp.concatenate([dots_a[j], dots_b[j]], axis=1)
        query_total = None
        sides = ((second_tile, dk_a, dv_a), (first_tile, dk_b, dv_b))
        for side, (start, dk_far, dv_far) in enumerate(sides):
            part = pl.ds(start(where), TILE)
            keys = k[part, head]
            weights = jnp.exp2(dot(keys, queries, NT) * SCALE2 - rows[j, side : side + 1])
            grads = (weights * (dot(v[part, head], backs, NT) - dots)).astype(BF16)
            dv[part, head] = (dv_far[0, :, head] + dot(weights.astype(BF16), backs, NN)).astype(BF16)
            dk[part, head] = ((dk_far[0, :, head] + dot(grads, queries, NN)) * SCALE).astype(BF16)
            share = dot(grads, keys, TN)
            query_total = share if query_total is None else query_total + share
        dq[0, :, head] = query_total * SCALE


def own_grads(where, q, k, v, back_a, back_b, rows, dots_a, dots_b, far_shares, held, dy0, count):
    full = pl.BlockSpec((SLAB, BLOCK), lambda d, w: (0, lax.rem(w[0] + dy0 + d, 4)))
    sent = pl.BlockSpec((1, TILE + EXTRA, BLOCK), lambda d, w: (dy0 + d, 0, 0))
    half = pl.BlockSpec((1, TILE, BLOCK), lambda d, w: (dy0 + d, 0, 0))
    row = pl.BlockSpec((GROUP, 1, TILE), lambda d, w: (dy0 + d, 0, 0))
    return pl.pallas_call(
        own_kernel,
        grid_spec=pltpu.PrefetchScalarGridSpec(
            num_scalar_prefetch=1,
            grid=(count,),
            in_specs=[
                full,
                full,
                full,
                sent,
                sent,
                pl.BlockSpec((GROUP, 2, SLAB), lambda d, w: (dy0 + d, 0, 0)),
                row,
                row,
            ]
            + [half] * 4
            + [pl.BlockSpec(memory_space=pl.ANY)] * len(held),
            out_specs=[pl.BlockSpec((1, SLAB, BLOCK), lambda d, w: (d, 0, 0)), full, full],
        ),
        out_shape=[jax.ShapeDtypeStruct((count, SLAB, BLOCK), F32)]
        + [jax.ShapeDtypeStruct((SLAB, FEAT), BF16)] * 2,
        input_output_aliases={13: 1, 14: 2} if held else {},
        compiler_params=params(),
        cost_estimate=STEP,
        name="own_grads",
    )(where, q, k, v, back_a, back_b, rows, dots_a, dots_b, *far_shares, *held)


def far_kernel(side, where, q, b, k, v, dq, dk, dv):
    exists = where[3 + side] == 1
    for j in range(GROUP):
        head = columns(j)
        keys = k[:, head]
        queries = q[0, :, head]
        backs = b[0, :TILE, head]
        rows = b[0, TILE:].astype(F32)
        row = sum(rows[j * 5 + i : j * 5 + i + 1] for i in range(3))
        row = jnp.where(exists, row, NEVER)
        dots = rows[j * 5 + 3 : j * 5 + 4] + rows[j * 5 + 4 : j * 5 + 5]
        weights = jnp.exp2(dot(keys, queries, NT) * SCALE2 - row)
        grads = (weights * (dot(v[:, head], backs, NT) - dots)).astype(BF16)
        dq[0, :, head] = (dot(grads, keys, TN) * SCALE).astype(BF16)
        dk[0, :, head] = dot(grads, queries, NN)
        dv[0, :, head] = dot(weights.astype(BF16), backs, NN)


def far_grads(where, side, q, b, k, v):
    edge = pl.BlockSpec((TILE, BLOCK), lambda d, w: (key_tile(side, w), lax.rem(w[0] + d, 4)))
    half = pl.BlockSpec((1, TILE, BLOCK), lambda d, w: (d, 0, 0))
    return pl.pallas_call(
        functools.partial(far_kernel, side),
        grid_spec=pltpu.PrefetchScalarGridSpec(
            num_scalar_prefetch=1,
            grid=(4,),
            in_specs=[
                half,
                pl.BlockSpec((1, TILE + EXTRA, BLOCK), lambda d, w: (d, 0, 0)),
                edge,
                edge,
            ],
            out_specs=[half, half, half],
        ),
        out_shape=[jax.ShapeDtypeStruct((4, TILE, BLOCK), t) for t in (BF16, F32, F32)],
        compiler_params=params(),
        cost_estimate=HIDES,
        name="far_grads",
    )(where, q, b, k, v)


def join_kernel(where, own, first, second, *rest):
    out = rest[-1]
    for side, (start, far) in enumerate(((first_tile, first), (second_tile, second))):
        part = slice(side * TILE, (side + 1) * TILE)
        out[pl.ds(start(where), TILE)] = (own[0, part] + far[0].astype(F32)).astype(BF16)


def join(where, own, first, second, held, dy0, count):
    half = pl.BlockSpec((1, TILE, BLOCK), lambda d, w: (dy0 + d, 0, 0))
    return pl.pallas_call(
        join_kernel,
        grid_spec=pltpu.PrefetchScalarGridSpec(
            num_scalar_prefetch=1,
            grid=(count,),
            in_specs=[pl.BlockSpec((1, SLAB, BLOCK), lambda d, w: (d, 0, 0)), half, half]
            + [pl.BlockSpec(memory_space=pl.ANY)] * len(held),
            out_specs=pl.BlockSpec((SLAB, BLOCK), lambda d, w: (0, lax.rem(w[0] + dy0 + d, 4))),
        ),
        out_shape=jax.ShapeDtypeStruct((SLAB, FEAT), BF16),
        input_output_aliases={4: 0} if held else {},
        compiler_params=params(),
        cost_estimate=STEP,
        name="join_query_grad",
    )(where, own, first, second, *held)


def weight_term_kernel(where, o, g, mine, other):
    product = dot(o[...].T, g[...], NN).astype(BF16)
    y = pl.program_id(0)
    for core in range(2):

        @pl.when(where[2] == core)
        def _():
            for out, holder in ((mine, core), (other, 1 - core)):
                for low in range(2):
                    start = (low * 2 + holder) * ROWS
                    for z in range(4):
                        piece = product[start : start + ROWS, z * QUARTER : (z + 1) * QUARTER]
                        if holder == 0:
                            out[y, z, low] = piece
                        else:
                            out[z, y, low] = piece


def weight_term(where, o, g):
    shape = (4, 4, 2, ROWS, QUARTER)
    whole = pl.BlockSpec(shape, lambda y, w: (0, 0, 0, 0, 0))
    return pl.pallas_call(
        weight_term_kernel,
        grid_spec=pltpu.PrefetchScalarGridSpec(
            num_scalar_prefetch=1,
            grid=(4,),
            in_specs=[
                pl.BlockSpec((SLAB, BLOCK), lambda y, w: (0, y)),
                pl.BlockSpec((SLAB, WIDTH), lambda y, w: (0, 0)),
            ],
            out_specs=[whole, whole],
        ),
        out_shape=[jax.ShapeDtypeStruct(shape, BF16)] * 2,
        compiler_params=params(),
        cost_estimate=HIDES,
        name="weight_term",
    )(where, o, g)


def after(value, *earlier):
    return lax.optimization_barrier((value, *earlier))[0]


def pick(flag, when_zero, when_one):
    return jnp.where(flag == 0, when_zero, when_one)


def split(value, index, axis):
    kept = lax.dynamic_index_in_dim(value, index, axis, keepdims=False)
    given = lax.dynamic_index_in_dim(value, 1 - index, axis, keepdims=False)
    return kept, given


def added(*values):
    return sum(v.astype(F32) for v in values).astype(BF16)


RUNS = ((0, 2), (2, 2))


def body(
    query_rows,
    key_rows,
    value_rows,
    attention_out,
    output_grad,
    output_weight,
    tile_mask,
    live_tiles,
):
    q, k, v, o, g = (
        a[0] for a in (query_rows, key_rows, value_rows, attention_out, output_grad)
    )
    slab = lax.axis_index("seq")
    row = lax.axis_index("dp")
    z = slab // 2
    y = row // 4
    low = (row // 2) % 2
    core = row % 2
    first_slab, last_slab = slab == 0, slab == 7
    lacks_a, lacks_b = pick(core, first_slab, last_slab), pick(core, last_slab, first_slab)
    where = jnp.stack([y, z, core, 1 - lacks_a, 1 - lacks_b]).astype(jnp.int32)

    def query_piece(second, dy0, count):
        start = core * TILE if second else (1 - core) * TILE
        return jnp.stack(
            [
                lax.dynamic_slice(q, (start, ((y + dy0 + d) % 4) * BLOCK), (TILE, BLOCK))
                for d in range(count)
            ]
        )

    quarter = lax.dynamic_slice(output_weight, (0, z * QUARTER), (ROWS, QUARTER))
    partner = send(quarter, SWAP_LOW)
    q = after(q, partner)
    qa = [send(query_piece(False, 0, 2), ROUTE_A)]
    pair = jnp.stack([pick(low, quarter, partner), pick(low, partner, quarter)])
    line = jnp.stack([pair] + [send(pair, from_first(step)) for step in (1, 2, 3)])
    line = after(line, qa[0])
    qa.append(send(query_piece(False, 2, 2), ROUTE_A))
    qb = send(query_piece(True, 0, 4), ROUTE_B)
    plane = jnp.stack([line] + [send(line, from_second(step)) for step in (1, 2, 3)])

    counts = live_tiles[0]
    slabs = jnp.arange(8, dtype=jnp.int32)

    def live(which, tile):
        return jnp.any((slabs == which) & (counts > tile))

    lives = [live(slab - 1, 1), live(slab, 0), live(slab, 1), live(slab + 1, 0)]
    marks = tile_mask[0] == 1
    allowed = [
        [marks[a, b] & lives[a + 1] & lives[a + b] for b in range(3)] for a in range(2)
    ]

    def by_query(lower, upper):
        first, second = pick(core, upper, lower), pick(core, lower, upper)
        return jnp.concatenate(
            [jnp.broadcast_to(first, (1, TILE)), jnp.broadcast_to(second, (1, TILE))], axis=1
        )

    own_allowed = [by_query(allowed[0][1], allowed[1][0]), by_query(allowed[0][2], allowed[1][1])]
    far_allowed = by_query(allowed[0][0], allowed[1][2])
    bias = jnp.where(jnp.concatenate(own_allowed, axis=0), 0.0, -NEVER).astype(F32)

    term_mine, term_other = weight_term(where, after(o, line), g)
    own_row = own_stats(where, after(q, term_mine), k, bias)
    plane = after(plane, qa[1], qb, own_row)
    other = send(plane, SWAP_CORE)
    term_far = send(after(term_other, plane), SWAP_CORE)

    qa = jnp.concatenate(qa, axis=0)
    stat_a = far_stats(where, 0, after(qa, plane), k)
    stat_b = far_stats(where, 1, after(qb, stat_a), k)
    far_row = jnp.concatenate([send(stat_a, ROUTE_B), send(stat_b, ROUTE_A)], axis=2)

    first, second = pick(core, y, z), pick(core, z, y)
    term_far = after(term_far, stat_b)
    rows_shape = (2, ROWS, QUARTER)
    kept, given = split(term_mine.reshape(2, 2, 4, *rows_shape), first % 2, 1)
    kept_far, given_far = split(term_far.reshape(2, 2, 4, *rows_shape), first % 2, 1)
    halves = added(given, given_far)
    g = after(g, halves)
    halves = send(halves, swap_first(1))

    back_a, dots_a = back(where, 0, g, plane, other, o)
    far_row = after(far_row, dots_a)
    far_row = jnp.where(far_allowed[None], far_row, -NEVER)
    top = jnp.maximum(own_row, far_row)
    row_total = top + jnp.log2(jnp.exp2(own_row - top) + jnp.exp2(far_row - top))
    own_rows = jnp.concatenate(
        [
            jnp.where(pick(core, *order)[None], row_total, NEVER)
            for order in (own_allowed, own_allowed[::-1])
        ],
        axis=1,
    )
    far_rows = jnp.where(far_allowed[None], row_total, NEVER)
    back_a = with_statistics(back_a, far_rows[:, :, :TILE], dots_a)
    far_a = send(back_a, ROUTE_A)
    back_b, dots_b = back(where, 1, after(g, back_a), plane, other, o)
    back_b = with_statistics(back_b, far_rows[:, :, TILE:], dots_b)
    far_b = send(back_b, ROUTE_B)

    kept, given = split(added(kept, kept_far, after(halves, back_b)), first // 2, 0)
    qa = after(qa, given)
    halves = send(given, swap_first(2))

    dqa, *share_a = far_grads(where, 0, qa, far_a, k, v)
    returned_a = send(dqa, ROUTE_B)
    kept = added(kept, after(halves, dqa))
    qb = after(qb, kept)

    def block_ahead(step):
        return lax.dynamic_index_in_dim(kept, (second + step) % 4, 0, keepdims=False)

    blocks = [send(block_ahead(step), from_second(4 - step)) for step in (1, 2, 3)]
    dqb, *share_b = far_grads(where, 1, qb, far_b, k, v)
    returned_b = send(dqb, ROUTE_A)

    kept = added(block_ahead(0), *after(tuple(blocks), dqb))
    kept, given = split(kept, low, 0)
    q = after(q, kept)
    beside = send(given, SWAP_LOW)
    returned_a = after(returned_a, kept)
    q = after(q, returned_a)
    arguments = (back_a, back_b, own_rows, dots_a, dots_b, share_a + share_b)
    dq0, *held = own_grads(where, q, k, v, *arguments, (), 0, 2)
    dq1, *held = own_grads(where, after(q, dq0), k, v, *arguments, held, 2, 2)
    both = added(kept, after(beside, dq1))
    both, returned_b = lax.optimization_barrier((both, returned_b))
    both_far = send(both, SWAP_HIGH)
    joined = join(where, dq0, returned_a, returned_b, (), 0, 2)
    whole = (both.astype(F32) + both_far.astype(F32)) * (1.0 / math.sqrt(16 * 6144))

    quarters = jnp.stack([whole] + [send(whole, from_along_z(step)) for step in (1, 2, 3)])
    quarters = jnp.concatenate([quarters, quarters])
    quarters = lax.dynamic_slice_in_dim(quarters, (4 - z) % 4, 4, 0)
    weight_grad = jnp.concatenate([quarters[i] for i in range(4)], axis=1)

    joined = join(where, dq1, returned_a, returned_b, (joined,), 2, 2)
    return joined[None], held[0][None], held[1][None], weight_grad


def solution(mesh):
    in_specs = (
        P("dp", "seq", None),
        P("dp", "seq", None),
        P("dp", "seq", None),
        P("dp", "seq", None),
        P("dp", "seq", None),
        P("dp", None),
        P("dp", "seq", None),
        P("dp", None),
    )
    out_specs = (P("dp", "seq", None), P("dp", "seq", None), P("dp", "seq", None), P("dp", None))
    return jax.shard_map(body, mesh=mesh, in_specs=in_specs, out_specs=out_specs, check_vma=False)
```

time: 369 us -> 295 us (0.80)
  starting transfers between devices: 95.5 us -> 62.3 us
  waiting for transfers between devices: 93.5 us -> 72.3 us
  between operations: 25.4 us -> 12.9 us
  Pallas kernels: 119 us -> 107 us
  other arithmetic: 12.1 us -> 22.8 us
  local copies, waits for them, and re-layouts: 20.5 us -> 15.7 us
    ppermute x24 -> x28, starting transfers between devices: 95.4 us -> 62.3 us  [send(): return lax.ppermute(block, AXES, pairs)]
    ppermute x24 -> x28, waiting for transfers between devices: 93.4 us -> 72.3 us  [send(): return lax.ppermute(block, AXES, pairs)]
    convert_element_type x1 -> x7, other arithmetic: 1.04 us -> 10.7 us  [the longest x5 10.5 us: added(): return sum((v.astype(F32) for v in values)).astype(BF16)]
    unnamed x57 -> x54, local copies, waits for them, and re-layouts: 18.1 us -> 10.9 us
    pallas_call x3, Pallas kernels: 41.3 us -> 35.5 us  [the longest x2 19.3 us: far_grads(): pl.pallas_call(functools.partial(far_kernel, side), grid_spec=pltpu.Prefe...]
    pallas_call x1 -> x2, Pallas kernels: 10.5 us -> 6.45 us  [far_stats(): pl.pallas_call(far_stats_kernel, grid_spec=pltpu.PrefetchScalarGridSpec(n...]
  transfers between devices with their start and end apart: 26 -> 28, of which waited for: 11 -> 11; matrix products, arithmetic and copies ran while one was open for 4% -> 8% of each run, Pallas kernels for 27% -> 37%
where the time goes in v2:
time: 295 us; the launch traced here: 293 us
  Pallas kernels  107 us (36%)
  waiting for transfers between devices  72.3 us (25%)
  starting transfers between devices  62.3 us (21%)
  other arithmetic  22.8 us (8%)
  local copies, waits for them, and re-layouts  15.7 us (5%)
  between operations  12.9 us (4%)
    ppermute x28, waiting for transfers between devices, send(): return lax.ppermute(block, AXES, pairs)  72.3 us
    ppermute x28, starting transfers between devices, send(): return lax.ppermute(block, AXES, pairs)  62.3 us
    pallas_call x2, Pallas kernels, own_grads(): pl.pallas_call(own_kernel, grid_spec=pltpu.PrefetchScalarGridSpec(num_sca...  26.7 us
    pallas_call x2, Pallas kernels, back(): pl.pallas_call(back_kernel, grid_spec=pltpu.PrefetchScalarGridSpec(num_sc...  23.8 us
    pallas_call x2, Pallas kernels, far_grads(): pl.pallas_call(functools.partial(far_kernel, side), grid_spec=pltpu.Prefe...  19.3 us
    pallas_call x1, Pallas kernels, weight_term(): pl.pallas_call(weight_term_kernel, grid_spec=pltpu.PrefetchScalarGridSpec...  16.2 us
    unnamed x54, local copies, waits for them, and re-layouts  10.9 us
    convert_element_type x5, other arithmetic, added(): return sum((v.astype(F32) for v in values)).astype(BF16)  10.5 us
  transfers between devices with their start and end apart: 28, of which 11 were waited for; matrix products, arithmetic and copies ran while one was open for 8% of the time, Pallas kernels for 37%

profile of v2, /device:TPU:0, one launch (start us, length us, event | category | flops | bytes accessed | tf_op | source)
XLA Modules:
  0.0 293.2 jit_solution(12107928331375427722)
XLA Ops:
  1.6 1.7 collective-permute-start
  4.5 1.4 fusion.18
  14.3 1.9 dynamic-slice_bitcast_fusion.11
  17.1 5.5 %collective-permute-start.4 = (bf16[2,384,384]{2,1,0:T(8,128)(2,1)}, bf16[2,384,384]{2,1,0:T(8,128)(2,1)}, u32[]{:S(2)}, u32[]{:S(2)}) collective-permute-start(bf16[2,384,384]{2,1,0:T(8,128)(2,1)} %pad_maximum_fusion.4), channel_id=1, source_target_pairs={{0,16},{2,18},{16,32},{18,34},{4,20},{6,22},{20,36},{22,38},{8,24}... | collective-permute-start | bytes 1769480 | tf_op jit(solution)/shard_map/ppermute | solution.py:95
  24.3 3.0 %collective-permute-start.1 = (bf16[2,96,768]{2,1,0:T(8,128)(2,1)}, bf16[2,96,768]{2,1,0:T(8,128)(2,1)}, u32[]{:S(2)}, u32[]{:S(2)}) collective-permute-start(bf16[2,96,768]{2,1,0:T(8,128)(2,1)} %get-tuple-element.116), channel_id=1, source_target_pairs={{0,12},{1,97},{2,14},{3,99},{16,28},{17,113},{18,30},{19,115},{4,0... | collective-permute-start | bytes 884744 | tf_op jit(solution)/shard_map/ppermute | solution.py:95
  29.2 1.4 collective-permute-start.9
  30.7 4.3 %collective-permute-done.1 = bf16[2,96,768]{2,1,0:T(8,128)(2,1)} collective-permute-done((bf16[2,96,768]{2,1,0:T(8,128)(2,1)}, bf16[2,96,768]{2,1,0:T(8,128)(2,1)}, u32[]{:S(2)}, u32[]{:S(2)}) %collective-permute-start.1) | collective-permute-done | bytes 294944 | tf_op jit(solution)/shard_map/ppermute | solution.py:95
  35.0 3.3 %collective-permute-start.8 = (bf16[2,384,384]{2,1,0:T(8,128)(2,1)S(1)}, bf16[2,384,384]{2,1,0:T(8,128)(2,1)S(1)}, u32[]{:S(2)}, u32[]{:S(2)}) collective-permute-start(bf16[2,384,384]{2,1,0:T(8,128)(2,1)S(1)} %pad_maximum_fusion.5), channel_id=1, source_target_pairs={{0,16},{2,18},{16,32},{18,34},{4,20},{6,22},{20,36},{22,38},{8,24}... | collective-permute-start | bytes 1769480 | tf_op jit(solution)/shard_map/ppermute | solution.py:95
  40.3 3.3 %collective-permute-start.5 = (bf16[4,2,96,768]{3,2,1,0:T(8,128)(2,1)S(1)}, bf16[4,2,96,768]{3,2,1,0:T(8,128)(2,1)S(1)}, u32[]{:S(2)}, u32[]{:S(2)}) collective-permute-start(bf16[4,2,96,768]{3,2,1,0:T(8,128)(2,1)S(1)} %pad_maximum_fusion.1), channel_id=1, source_target_pairs={{0,96},{1,13},{2,98},{3,15},{16,112},{17,29},{18,114},{19,31},{4,1... | collective-permute-start | bytes 3538952 | tf_op jit(solution)/shard_map/ppermute | solution.py:95
  44.8 16.2 %weight_term.1 = (bf16[4,4,2,96,768]{4,3,2,1,0:T(8,128)(2,1)}, bf16[4,4,2,96,768]{4,3,2,1,0:T(8,128)(2,1)}) custom-call(s32[5]{0:T(128)S(1)} %stack.108.where, bf16[768,1536]{1,0:T(8,128)(2,1)S(1)} %bitcast.125, bf16[768,3072]{1,0:T(8,128)(2,1)} %bitcast.141), custom_call_target="tpu_custom_call" | custom-call | flops 99999997952 | bytes 1000000 | tf_op jit(solution)/shard_map/weight_term/pallas_call | solution.py:413
  61.0 9.3 %own_stats.1 = f32[12,1,768]{2,1,0:T(1,128)S(1)} custom-call(s32[5]{0:T(128)S(1)} %stack.108.where, bf16[768,1536]{1,0:T(8,128)(2,1)S(1)} %bitcast.124, bf16[768,1536]{1,0:T(8,128)(2,1)S(1)} %bitcast.118, f32[2,768]{1,0:T(2,128)S(1)} %add_select_fusion.bias), custom_call_target="tpu_custom_call" | custom-call | flops 100000000 | bytes 100000 | tf_op jit(solution)/shard_map/own_stats/pallas_call | solution.py:146
  70.4 13.0 %collective-permute-done.7 = bf16[4,2,96,768]{3,2,1,0:T(8,128)(2,1)S(1)} collective-permute-done((bf16[4,2,96,768]{3,2,1,0:T(8,128)(2,1)S(1)}, bf16[4,2,96,768]{3,2,1,0:T(8,128)(2,1)S(1)}, u32[]{:S(2)}, u32[]{:S(2)}) %collective-permute-start.7) | collective-permute-done | bytes 1179680 | tf_op jit(solution)/shard_map/ppermute | solution.py:95
  83.4 2.5 pad_maximum_fusion.mine_z.mine_y
  87.7 3.2 %far_stats.2 = f32[12,1,384]{2,1,0:T(1,128)S(1)} custom-call(s32[5]{0:T(128)S(1)} %stack.108.where, bf16[4,384,384]{2,1,0:T(8,128)(2,1)S(1)} %constant_dynamic-update-slice_fusion.q, bf16[768,1536]{1,0:T(8,128)(2,1)S(1)} %bitcast.119), custom_call_target="tpu_custom_call" | custom-call | flops 100000000 | bytes 100000 | tf_op jit(solution)/shard_map/far_stats/pallas_call | solution.py:174
  91.0 3.2 %far_stats.3 = f32[12,1,384]{2,1,0:T(1,128)S(1)} custom-call(s32[5]{0:T(128)S(1)} %stack.108.where, bf16[4,384,384]{2,1,0:T(8,128)(2,1)S(1)} %collective-permute-done.9.q, bf16[768,1536]{1,0:T(8,128)(2,1)S(1)} %bitcast.120), custom_call_target="tpu_custom_call" | custom-call | flops 100000000 | bytes 100000 | tf_op jit(solution)/shard_map/far_stats/pallas_call | solution.py:174
  100.7 12.1 %collective-permute-done.13 = f32[12,1,384]{2,1,0:T(1,128)S(1)} collective-permute-done((f32[12,1,384]{2,1,0:T(1,128)S(1)}, f32[12,1,384]{2,1,0:T(1,128)S(1)}, u32[]{:S(2)}, u32[]{:S(2)}) %collective-permute-start.13) | collective-permute-done | bytes 18464 | tf_op jit(solution)/shard_map/ppermute | solution.py:95
  112.8 4.6 %fusion.1 = bf16[2,4,2,96,768]{4,3,2,1,0:T(8,128)(2,1)} fusion(bf16[2,2,4,2,96,768]{5,4,3,2,1,0:T(8,128)(2,1)} %bitcast.35, s32[]{:T(128)S(6)} %select_n.247, bf16[2,2,4,2,96,768]{5,4,3,2,1,0:T(8,128)(2,1)} %bitcast.134), kind=kLoop, calls=%fused_computation.4 | loop fusion | flops 4718592 | bytes 7077892 | tf_op jit(solution)/shard_map/convert_element_type | solution.py:446
  117.5 1.8 collective-permute-start.11
  119.3 11.9 %out_back.2 = (bf16[4,400,384]{2,1,0:T(8,128)(2,1)S(1)}, f32[12,1,384]{2,1,0:T(1,128)S(1)}) custom-call(s32[5]{0:T(128)S(1)} %stack.108.where, bf16[768,3072]{1,0:T(8,128)(2,1)} %bitcast.142, bf16[4,4,2,96,768]{4,3,2,1,0:T(8,128)(2,1)} %pad_maximum_fusion.mine_z.mine_y, bf16[4,4,2,96,768]{4,3,2,1,0:T(8,128)(2,1)} %pad_maximum_fusion.mine_z.mine_y, ...), custom_call_target="tpu_custom_call" | custom-call | flops 99999997952 | bytes 1000000 | tf_op jit(solution)/shard_map/out_back/pallas_call | solution.py:225
  133.3 7.4 %collective-permute-start.16 = (bf16[4,400,384]{2,1,0:T(8,128)(2,1)S(1)}, bf16[4,400,384]{2,1,0:T(8,128)(2,1)}, u32[]{:S(2)}, u32[]{:S(2)}) collective-permute-start(bf16[4,400,384]{2,1,0:T(8,128)(2,1)S(1)} %dynamic_update_slice.6.back_a), channel_id=1, source_target_pairs={{0,16},{2,18},{16,32},{18,34},{4,20},{6,22},{20,36},{22,38},{8,24}... | collective-permute-start | bytes 3686408 | tf_op jit(solution)/shard_map/ppermute | solution.py:95
  140.7 1.7 copy-done.18
  142.3 11.9 %out_back.3 = (bf16[4,400,384]{2,1,0:T(8,128)(2,1)S(1)}, f32[12,1,384]{2,1,0:T(1,128)S(1)}) custom-call(s32[5]{0:T(128)S(1)} %stack.108.where, bf16[768,3072]{1,0:T(8,128)(2,1)} %bitcast.143, bf16[4,4,2,96,768]{4,3,2,1,0:T(8,128)(2,1)} %pad_maximum_fusion.mine_z.mine_y, bf16[4,4,2,96,768]{4,3,2,1,0:T(8,128)(2,1)} %pad_maximum_fusion.mine_z.mine_y, ...), custom_call_target="tpu_custom_call" | custom-call | flops 99999997952 | bytes 1000000 | tf_op jit(solution)/shard_map/out_back/pallas_call | solution.py:225
  156.6 4.2 %fusion = bf16[2,4,2,96,768]{4,3,2,1,0:T(8,128)(2,1)S(1)} fusion(bf16[2,4,2,96,768]{4,3,2,1,0:T(8,128)(2,1)} %collective-permute-done.11, bf16[2,2,4,2,96,768]{5,4,3,2,1,0:T(8,128)(2,1)} %bitcast.35, s32[]{:T(128)S(6)} %select_n.236, bf16[2,2,4,2,96,768]{5,4,3,2,1,0:T(8,128)(2,1)} %bitcast.135), kind=kLoop, calls=%fused_computation.2 | loop fusion | flops 7077888 | bytes 9437188 | tf_op jit(solution)/shard_map/convert_element_type | solution.py:446
  161.0 2.1 collective-permute-start.15
  163.0 9.7 %far_grads.2 = (bf16[4,384,384]{2,1,0:T(8,128)(2,1)}, f32[4,384,384]{2,1,0:T(8,128)S(1)}, f32[4,384,384]{2,1,0:T(8,128)}) custom-call(s32[5]{0:T(128)S(1)} %stack.108.where, bf16[4,384,384]{2,1,0:T(8,128)(2,1)S(1)} %copy-done.5, bf16[4,400,384]{2,1,0:T(8,128)(2,1)} %collective-permute-done.16.b, bf16[768,1536]{1,0:T(8,128)(2,1)} %bitcast.114, ...), custom_call_target="tpu_custom_call" | custom-call | flops 99999997952 | bytes 1000000 | tf_op jit(solution)/shard_map/far_grads/pallas_call | solution.py:346
  172.7 1.4 copy-done.2
  174.1 1.4 collective-permute-start.21
  175.5 3.3 %collective-permute-done.15 = bf16[4,2,96,768]{3,2,1,0:T(8,128)(2,1)S(1)} collective-permute-done((bf16[4,2,96,768]{3,2,1,0:T(8,128)(2,1)S(1)}, bf16[4,2,96,768]{3,2,1,0:T(8,128)(2,1)S(1)}, u32[]{:S(2)}, u32[]{:S(2)}) %collective-permute-start.15) | collective-permute-done | bytes 1179680 | tf_op jit(solution)/shard_map/ppermute | solution.py:95
  179.0 17.0 %collective-permute-done.20.b = bf16[4,400,384]{2,1,0:T(8,128)(2,1)S(1)} collective-permute-done((bf16[4,400,384]{2,1,0:T(8,128)(2,1)S(1)}, bf16[4,400,384]{2,1,0:T(8,128)(2,1)S(1)}, u32[]{:S(2)}, u32[]{:S(2)}) %collective-permute-start.20) | collective-permute-done | bytes 1228832 | tf_op jit(solution)/shard_map/ppermute | solution.py:95
  196.1 9.6 %far_grads.3 = (bf16[4,384,384]{2,1,0:T(8,128)(2,1)}, f32[4,384,384]{2,1,0:T(8,128)S(1)}, f32[4,384,384]{2,1,0:T(8,128)}) custom-call(s32[5]{0:T(128)S(1)} %stack.108.where, bf16[4,384,384]{2,1,0:T(8,128)(2,1)S(1)} %copy-done.11, bf16[4,400,384]{2,1,0:T(8,128)(2,1)S(1)} %collective-permute-done.20.b, bf16[768,1536]{1,0:T(8,128)(2,1)} %bitcast.115, ...), custom_call_target="tpu_custom_call" | custom-call | flops 99999997952 | bytes 1000000 | tf_op jit(solution)/shard_map/far_grads/pallas_call | solution.py:346
  205.7 1.4 copy-done.3
  207.1 6.7 %collective-permute-start.23 = (bf16[4,384,384]{2,1,0:T(8,128)(2,1)}, bf16[4,384,384]{2,1,0:T(8,128)(2,1)}, u32[]{:S(2)}, u32[]{:S(2)}) collective-permute-start(bf16[4,384,384]{2,1,0:T(8,128)(2,1)} %get-tuple-element.71), channel_id=1, source_target_pairs={{0,16},{2,18},{16,32},{18,34},{4,20},{6,22},{20,36},{22,38},{8,24}... | collective-permute-start | bytes 3538952 | tf_op jit(solution)/shard_map/ppermute | solution.py:95
  214.0 3.1 %collective-permute-start.19 = (bf16[2,96,768]{2,1,0:T(8,128)(2,1)S(1)}, bf16[2,96,768]{2,1,0:T(8,128)(2,1)}, u32[]{:S(2)}, u32[]{:S(2)}) collective-permute-start(bf16[2,96,768]{2,1,0:T(8,128)(2,1)S(1)} %get-tuple-element.110), channel_id=1, source_target_pairs={{0,96},{1,13},{2,98},{3,15},{16,112},{17,29},{18,114},{19,31},{4,1... | collective-permute-start | bytes 884744 | tf_op jit(solution)/shard_map/ppermute | solution.py:95
  217.1 6.4 %collective-permute-done.17 = bf16[2,96,768]{2,1,0:T(8,128)(2,1)} collective-permute-done((bf16[2,96,768]{2,1,0:T(8,128)(2,1)S(1)}, bf16[2,96,768]{2,1,0:T(8,128)(2,1)}, u32[]{:S(2)}, u32[]{:S(2)}) %collective-permute-start.17) | collective-permute-done | bytes 294944 | tf_op jit(solution)/shard_map/ppermute | solution.py:95
  223.6 3.0 %collective-permute-done.18 = bf16[2,96,768]{2,1,0:T(8,128)(2,1)} collective-permute-done((bf16[2,96,768]{2,1,0:T(8,128)(2,1)S(1)}, bf16[2,96,768]{2,1,0:T(8,128)(2,1)}, u32[]{:S(2)}, u32[]{:S(2)}) %collective-permute-start.18) | collective-permute-done | bytes 294944 | tf_op jit(solution)/shard_map/ppermute | solution.py:95
  226.6 1.4 fusion.5
  228.5 13.4 %own_grads.2 = (f32[2,768,384]{2,1,0:T(8,128)S(1)}, bf16[768,1536]{1,0:T(8,128)(2,1)}, bf16[768,1536]{1,0:T(8,128)(2,1)}) custom-call(s32[5]{0:T(128)S(1)} %stack.108.where, bf16[768,1536]{1,0:T(8,128)(2,1)} %bitcast.122, bf16[768,1536]{1,0:T(8,128)(2,1)} %bitcast.116, bf16[768,1536]{1,0:T(8,128)(2,1)} %bitcast.131, ...), custom_call_target="tpu_custom_call" | custom-call | flops 100000000 | bytes 100000 | tf_op jit(solution)/shard_map/own_grads/pallas_call | solution.py:297
  241.8 1.5 copy-done.6
  243.3 13.3 %own_grads.3 = (f32[2,768,384]{2,1,0:T(8,128)S(1)}, bf16[768,1536]{1,0:T(8,128)(2,1)}, bf16[768,1536]{1,0:T(8,128)(2,1)}) custom-call(s32[5]{0:T(128)S(1)} %stack.108.where, bf16[768,1536]{1,0:T(8,128)(2,1)} %bitcast.123, bf16[768,1536]{1,0:T(8,128)(2,1)} %bitcast.117, bf16[768,1536]{1,0:T(8,128)(2,1)} %bitcast.132, ...), custom_call_target="tpu_custom_call", output_to_operand_aliasing={{1}: (13, {}), {2}: (14, {})} | custom-call | flops 100000000 | bytes 100000 | tf_op jit(solution)/shard_map/own_grads/pallas_call | solution.py:297
  256.6 1.4 copy-done.8
  258.1 11.8 %collective-permute-start.24 = (bf16[96,768]{1,0:T(8,128)(2,1)S(1)}, bf16[96,768]{1,0:T(8,128)(2,1)S(1)}, u32[]{:S(2)}, u32[]{:S(2)}) collective-permute-start(bf16[96,768]{1,0:T(8,128)(2,1)S(1)} %add_convert_fusion.1), channel_id=1, source_target_pairs={{0,16},{1,17},{2,18},{3,19},{16,0},{17,1},{18,2},{19,3},{4,20},{5,... | collective-permute-start | bytes 442376 | tf_op jit(solution)/shard_map/ppermute | solution.py:95
  269.9 3.1 %collective-permute-done.24 = bf16[96,768]{1,0:T(8,128)(2,1)S(1)} collective-permute-done((bf16[96,768]{1,0:T(8,128)(2,1)S(1)}, bf16[96,768]{1,0:T(8,128)(2,1)S(1)}, u32[]{:S(2)}, u32[]{:S(2)}) %collective-permute-start.24) | collective-permute-done | bytes 147488 | tf_op jit(solution)/shard_map/ppermute | solution.py:95
  273.2 1.7 copy-done.7
  274.9 2.9 join_query_grad.2.rest_0_
  277.7 2.7 join_query_grad.3
  280.5 1.3 collective-permute-start.26
  282.5 6.3 %collective-permute-done.26 = f32[96,768]{1,0:T(8,128)S(1)} collective-permute-done((f32[96,768]{1,0:T(8,128)S(1)}, f32[96,768]{1,0:T(8,128)S(1)}, u32[]{:S(2)}, u32[]{:S(2)}) %collective-permute-start.26) | collective-permute-done | bytes 294944 | tf_op jit(solution)/shard_map/ppermute | solution.py:95
  288.8 3.0 %collective-permute-done.27 = f32[96,768]{1,0:T(8,128)S(1)} collective-permute-done((f32[96,768]{1,0:T(8,128)S(1)}, f32[96,768]{1,0:T(8,128)S(1)}, u32[]{:S(2)}, u32[]{:S(2)}) %collective-permute-start.27) | collective-permute-done | bytes 294944 | tf_op jit(solution)/shard_map/ppermute | solution.py:95
  (122 shorter events, 22.9 us)
Async XLA Ops:
  1.6 12.7 %collective-permute-start = (bf16[96,768]{1,0:T(8,128)(2,1)S(1)}, bf16[96,768]{1,0:T(8,128)(2,1)S(1)}, u32[]{:S(2)}, u32[]{:S(2)}) collective-permute-start(bf16[96,768]{1,0:T(8,128)(2,1)S(1)} %constant_dynamic-slice_fusion), channel_id=1, source_target_pairs={{0,2},{1,3},{2,0},{3,1},{16,18},{17,19},{18,16},{19,17},{4,6},{5,7... | collective-permute-start | bytes 442376 | tf_op jit(solution)/shard_map/ppermute | solution.py:95
  17.1 23.2 %collective-permute-start.4 = (bf16[2,384,384]{2,1,0:T(8,128)(2,1)}, bf16[2,384,384]{2,1,0:T(8,128)(2,1)}, u32[]{:S(2)}, u32[]{:S(2)}) collective-permute-start(bf16[2,384,384]{2,1,0:T(8,128)(2,1)} %pad_maximum_fusion.4), channel_id=1, source_target_pairs={{0,16},{2,18},{16,32},{18,34},{4,20},{6,22},{20,36},{22,38},{8,24}... | collective-permute-start | bytes 1769480 | tf_op jit(solution)/shard_map/ppermute | solution.py:95
  24.3 10.7 %collective-permute-start.1 = (bf16[2,96,768]{2,1,0:T(8,128)(2,1)}, bf16[2,96,768]{2,1,0:T(8,128)(2,1)}, u32[]{:S(2)}, u32[]{:S(2)}) collective-permute-start(bf16[2,96,768]{2,1,0:T(8,128)(2,1)} %get-tuple-element.116), channel_id=1, source_target_pairs={{0,12},{1,97},{2,14},{3,99},{16,28},{17,113},{18,30},{19,115},{4,0... | collective-permute-start | bytes 884744 | tf_op jit(solution)/shard_map/ppermute | solution.py:95
  27.3 11.0 %collective-permute-start.2 = (bf16[2,96,768]{2,1,0:T(8,128)(2,1)}, bf16[2,96,768]{2,1,0:T(8,128)(2,1)}, u32[]{:S(2)}, u32[]{:S(2)}) collective-permute-start(bf16[2,96,768]{2,1,0:T(8,128)(2,1)} %get-tuple-element.116), channel_id=1, source_target_pairs={{0,8},{1,65},{2,10},{3,67},{16,24},{17,81},{18,26},{19,83},{4,12},... | collective-permute-start | bytes 884744 | tf_op jit(solution)/shard_map/ppermute | solution.py:95
  27.9 11.1 %collective-permute-start.3 = (bf16[2,96,768]{2,1,0:T(8,128)(2,1)}, bf16[2,96,768]{2,1,0:T(8,128)(2,1)}, u32[]{:S(2)}, u32[]{:S(2)}) collective-permute-start(bf16[2,96,768]{2,1,0:T(8,128)(2,1)} %get-tuple-element.116), channel_id=1, source_target_pairs={{0,4},{1,33},{2,6},{3,35},{16,20},{17,49},{18,22},{19,51},{4,8},{5... | collective-permute-start | bytes 884744 | tf_op jit(solution)/shard_map/ppermute | solution.py:95
  29.2 15.6 %copy-start.16 = (bf16[1,768,1536]{2,1,0:T(8,128)(2,1)S(1)}, bf16[1,768,1536]{2,1,0:T(8,128)(2,1)}, u32[]{:S(2)}) copy-start(bf16[1,768,1536]{2,1,0:T(8,128)(2,1)} %param.11) | copy-start | bytes 7077892
  29.2 56.7 %collective-permute-start.9 = (bf16[4,384,384]{2,1,0:T(8,128)(2,1)S(1)}, bf16[4,384,384]{2,1,0:T(8,128)(2,1)S(1)}, u32[]{:S(2)}, u32[]{:S(2)}) collective-permute-start(bf16[4,384,384]{2,1,0:T(8,128)(2,1)S(1)} %pad_maximum_fusion.2), channel_id=1, source_target_pairs={{16,0},{18,2},{20,4},{22,6},{24,8},{26,10},{28,12},{30,14},{32,16}... | collective-permute-start | bytes 3538952 | tf_op jit(solution)/shard_map/ppermute | solution.py:95
  35.0 50.9 %collective-permute-start.8 = (bf16[2,384,384]{2,1,0:T(8,128)(2,1)S(1)}, bf16[2,384,384]{2,1,0:T(8,128)(2,1)S(1)}, u32[]{:S(2)}, u32[]{:S(2)}) collective-permute-start(bf16[2,384,384]{2,1,0:T(8,128)(2,1)S(1)} %pad_maximum_fusion.5), channel_id=1, source_target_pairs={{0,16},{2,18},{16,32},{18,34},{4,20},{6,22},{20,36},{22,38},{8,24}... | collective-permute-start | bytes 1769480 | tf_op jit(solution)/shard_map/ppermute | solution.py:95
  40.3 30.1 %collective-permute-start.5 = (bf16[4,2,96,768]{3,2,1,0:T(8,128)(2,1)S(1)}, bf16[4,2,96,768]{3,2,1,0:T(8,128)(2,1)S(1)}, u32[]{:S(2)}, u32[]{:S(2)}) collective-permute-start(bf16[4,2,96,768]{3,2,1,0:T(8,128)(2,1)S(1)} %pad_maximum_fusion.1), channel_id=1, source_target_pairs={{0,96},{1,13},{2,98},{3,15},{16,112},{17,29},{18,114},{19,31},{4,1... | collective-permute-start | bytes 3538952 | tf_op jit(solution)/shard_map/ppermute | solution.py:95
  43.6 26.8 %collective-permute-start.6 = (bf16[4,2,96,768]{3,2,1,0:T(8,128)(2,1)S(1)}, bf16[4,2,96,768]{3,2,1,0:T(8,128)(2,1)S(1)}, u32[]{:S(2)}, u32[]{:S(2)}) collective-permute-start(bf16[4,2,96,768]{3,2,1,0:T(8,128)(2,1)S(1)} %pad_maximum_fusion.1), channel_id=1, source_target_pairs={{0,64},{1,9},{2,66},{3,11},{16,80},{17,25},{18,82},{19,27},{4,68},... | collective-permute-start | bytes 3538952 | tf_op jit(solution)/shard_map/ppermute | solution.py:95
  43.6 39.8 %collective-permute-start.7 = (bf16[4,2,96,768]{3,2,1,0:T(8,128)(2,1)S(1)}, bf16[4,2,96,768]{3,2,1,0:T(8,128)(2,1)S(1)}, u32[]{:S(2)}, u32[]{:S(2)}) collective-permute-start(bf16[4,2,96,768]{3,2,1,0:T(8,128)(2,1)S(1)} %pad_maximum_fusion.1), channel_id=1, source_target_pairs={{0,32},{1,5},{2,34},{3,7},{16,48},{17,21},{18,50},{19,23},{4,36},{... | collective-permute-start | bytes 3538952 | tf_op jit(solution)/shard_map/ppermute | solution.py:95
  44.8 16.2 %copy-start = (bf16[1,768,1536]{2,1,0:T(8,128)(2,1)S(1)}, bf16[1,768,1536]{2,1,0:T(8,128)(2,1)}, u32[]{:S(2)}) copy-start(bf16[1,768,1536]{2,1,0:T(8,128)(2,1)} %param.9) | copy-start | bytes 7077892
  44.8 16.2 %copy-start.1 = (bf16[1,768,1536]{2,1,0:T(8,128)(2,1)S(1)}, bf16[1,768,1536]{2,1,0:T(8,128)(2,1)}, u32[]{:S(2)}) copy-start(bf16[1,768,1536]{2,1,0:T(8,128)(2,1)} %param.8) | copy-start | bytes 7077892
  85.9 5.1 %copy-start.10 = (bf16[4,384,384]{2,1,0:T(8,128)(2,1)}, bf16[4,384,384]{2,1,0:T(8,128)(2,1)S(1)}, u32[]{:S(2)}) copy-start(bf16[4,384,384]{2,1,0:T(8,128)(2,1)S(1)} %collective-permute-done.9.q) | copy-start | bytes 3538948
  85.9 26.9 %collective-permute-start.10 = (bf16[4,4,2,96,768]{4,3,2,1,0:T(8,128)(2,1)}, bf16[4,4,2,96,768]{4,3,2,1,0:T(8,128)(2,1)}, u32[]{:S(2)}, u32[]{:S(2)}) collective-permute-start(bf16[4,4,2,96,768]{4,3,2,1,0:T(8,128)(2,1)} %get-tuple-element.55), channel_id=1, source_target_pairs={{0,1},{1,0},{2,3},{3,2},{16,17},{17,16},{18,19},{19,18},{4,5},{5,4... | collective-permute-start | bytes 14155784 | tf_op jit(solution)/shard_map/ppermute | solution.py:95
  86.0 33.3 %collective-permute-start.12 = (bf16[4,4,2,96,768]{4,3,2,1,0:T(8,128)(2,1)}, bf16[4,4,2,96,768]{4,3,2,1,0:T(8,128)(2,1)}, u32[]{:S(2)}, u32[]{:S(2)}) collective-permute-start(bf16[4,4,2,96,768]{4,3,2,1,0:T(8,128)(2,1)} %pad_maximum_fusion.mine_z.mine_y), channel_id=1, source_target_pairs={{0,1},{1,0},{2,3},{3,2},{16,17},{17,16},{18,19},{19,18},{4,5},{5,4... | collective-permute-start | bytes 14155784 | tf_op jit(solution)/shard_map/ppermute | solution.py:95
  87.7 6.5 %copy-start.4 = (bf16[4,384,384]{2,1,0:T(8,128)(2,1)}, bf16[4,384,384]{2,1,0:T(8,128)(2,1)S(1)}, u32[]{:S(2)}) copy-start(bf16[4,384,384]{2,1,0:T(8,128)(2,1)S(1)} %constant_dynamic-update-slice_fusion.q) | copy-start | bytes 3538948
  94.2 6.5 %collective-permute-start.14 = (f32[12,1,384]{2,1,0:T(1,128)S(1)}, f32[12,1,384]{2,1,0:T(1,128)S(1)}, u32[]{:S(2)}, u32[]{:S(2)}) collective-permute-start(f32[12,1,384]{2,1,0:T(1,128)S(1)} %far_stats.3), channel_id=1, source_target_pairs={{0,16},{2,18},{16,32},{18,34},{4,20},{6,22},{20,36},{22,38},{8,24}... | collective-permute-start | bytes 55304 | tf_op jit(solution)/shard_map/ppermute | solution.py:95
  95.5 17.2 %collective-permute-start.13 = (f32[12,1,384]{2,1,0:T(1,128)S(1)}, f32[12,1,384]{2,1,0:T(1,128)S(1)}, u32[]{:S(2)}, u32[]{:S(2)}) collective-permute-start(f32[12,1,384]{2,1,0:T(1,128)S(1)} %far_stats.2), channel_id=1, source_target_pairs={{16,0},{18,2},{20,4},{22,6},{24,8},{26,10},{28,12},{30,14},{32,16}... | collective-permute-start | bytes 55304 | tf_op jit(solution)/shard_map/ppermute | solution.py:95
  112.8 6.5 %copy-start.17 = (bf16[1,768,1536]{2,1,0:T(8,128)(2,1)S(1)}, bf16[1,768,1536]{2,1,0:T(8,128)(2,1)}, u32[]{:S(2)}) copy-start(bf16[1,768,1536]{2,1,0:T(8,128)(2,1)} %param.11) | copy-start | bytes 7077892
  117.5 13.7 %copy-start.23 = (pred[768]{0:T(1024)(128)(4,1)S(1)}, pred[768]{0:T(1024)(128)(4,1)}, u32[]{:S(2)}) copy-start(pred[768]{0:T(1024)(128)(4,1)} %get-tuple-element.132) | copy-start | bytes 2308
  117.5 14.5 %copy-start.22 = (pred[768]{0:T(1024)(128)(4,1)S(1)}, pred[768]{0:T(1024)(128)(4,1)}, u32[]{:S(2)}) copy-start(pred[768]{0:T(1024)(128)(4,1)} %get-tuple-element.131) | copy-start | bytes 2308
  117.5 39.2 %collective-permute-start.11 = (bf16[2,4,2,96,768]{4,3,2,1,0:T(8,128)(2,1)}, bf16[2,4,2,96,768]{4,3,2,1,0:T(8,128)(2,1)}, u32[]{:S(2)}, u32[]{:S(2)}) collective-permute-start(bf16[2,4,2,96,768]{4,3,2,1,0:T(8,128)(2,1)} %fusion.1), channel_id=1, source_target_pairs={{0,4},{1,33},{2,6},{3,35},{16,20},{17,49},{18,22},{19,51},{4,0},{5... | collective-permute-start | bytes 7077896 | tf_op jit(solution)/shard_map/ppermute | solution.py:95
  131.2 1.5 copy-start.12
  133.3 29.8 %collective-permute-start.16 = (bf16[4,400,384]{2,1,0:T(8,128)(2,1)S(1)}, bf16[4,400,384]{2,1,0:T(8,128)(2,1)}, u32[]{:S(2)}, u32[]{:S(2)}) collective-permute-start(bf16[4,400,384]{2,1,0:T(8,128)(2,1)S(1)} %dynamic_update_slice.6.back_a), channel_id=1, source_target_pairs={{0,16},{2,18},{16,32},{18,34},{4,20},{6,22},{20,36},{22,38},{8,24}... | collective-permute-start | bytes 3686408 | tf_op jit(solution)/shard_map/ppermute | solution.py:95
  140.7 1.7 copy-start.18
  155.3 40.7 %collective-permute-start.20 = (bf16[4,400,384]{2,1,0:T(8,128)(2,1)S(1)}, bf16[4,400,384]{2,1,0:T(8,128)(2,1)S(1)}, u32[]{:S(2)}, u32[]{:S(2)}) collective-permute-start(bf16[4,400,384]{2,1,0:T(8,128)(2,1)S(1)} %dynamic_update_slice.7.back_b), channel_id=1, source_target_pairs={{16,0},{18,2},{20,4},{22,6},{24,8},{26,10},{28,12},{30,14},{32,16}... | collective-permute-start | bytes 3686408 | tf_op jit(solution)/shard_map/ppermute | solution.py:95
  160.9 2.2 copy-start.5
  161.0 17.8 %collective-permute-start.15 = (bf16[4,2,96,768]{3,2,1,0:T(8,128)(2,1)S(1)}, bf16[4,2,96,768]{3,2,1,0:T(8,128)(2,1)S(1)}, u32[]{:S(2)}, u32[]{:S(2)}) collective-permute-start(bf16[4,2,96,768]{3,2,1,0:T(8,128)(2,1)S(1)} %dynamic-slice_bitcast_fusion), channel_id=1, source_target_pairs={{0,8},{1,65},{2,10},{3,67},{16,24},{17,81},{18,26},{19,83},{4,12},... | collective-permute-start | bytes 3538952 | tf_op jit(solution)/shard_map/ppermute | solution.py:95
  174.1 22.0 %copy-start.11 = (bf16[4,384,384]{2,1,0:T(8,128)(2,1)S(1)}, bf16[4,384,384]{2,1,0:T(8,128)(2,1)}, u32[]{:S(2)}) copy-start(bf16[4,384,384]{2,1,0:T(8,128)(2,1)} %copy-done.10) | copy-start | bytes 3538948
  174.1 54.4 %collective-permute-start.21 = (bf16[4,384,384]{2,1,0:T(8,128)(2,1)}, bf16[4,384,384]{2,1,0:T(8,128)(2,1)}, u32[]{:S(2)}, u32[]{:S(2)}) collective-permute-start(bf16[4,384,384]{2,1,0:T(8,128)(2,1)} %get-tuple-element.68), channel_id=1, source_target_pairs={{16,0},{18,2},{20,4},{22,6},{24,8},{26,10},{28,12},{30,14},{32,16}... | collective-permute-start | bytes 3538952 | tf_op jit(solution)/shard_map/ppermute | solution.py:95
  179.0 34.7 %copy-start.19 = (bf16[4,2,96,768]{3,2,1,0:T(8,128)(2,1)}, bf16[4,2,96,768]{3,2,1,0:T(8,128)(2,1)S(1)}, u32[]{:S(2)}) copy-start(bf16[4,2,96,768]{3,2,1,0:T(8,128)(2,1)S(1)} %fusion.2) | copy-start | bytes 3538948
  207.1 21.3 %copy-start.20 = (f32[12,1,768]{2,1,0:T(1,128)S(1)}, f32[12,1,768]{2,1,0:T(1,128)}, u32[]{:S(2)}) copy-start(f32[12,1,768]{2,1,0:T(1,128)} %get-tuple-element.119) | copy-start | bytes 110596
  207.1 21.3 %copy-start.21 = (f32[12,1,768]{2,1,0:T(1,128)S(1)}, f32[12,1,768]{2,1,0:T(1,128)}, u32[]{:S(2)}) copy-start(f32[12,1,768]{2,1,0:T(1,128)} %get-tuple-element.96) | copy-start | bytes 110596
  207.1 21.4 %copy-start.13 = (f32[12,1,384]{2,1,0:T(1,128)S(1)}, f32[12,1,384]{2,1,0:T(1,128)}, u32[]{:S(2)}) copy-start(f32[12,1,384]{2,1,0:T(1,128)} %copy-done.12) | copy-start | bytes 55300
  207.1 21.4 %copy-start.15 = (f32[12,1,384]{2,1,0:T(1,128)S(1)}, f32[12,1,384]{2,1,0:T(1,128)}, u32[]{:S(2)}) copy-start(f32[12,1,384]{2,1,0:T(1,128)} %copy-done.14) | copy-start | bytes 55300
  207.1 51.0 %collective-permute-start.23 = (bf16[4,384,384]{2,1,0:T(8,128)(2,1)}, bf16[4,384,384]{2,1,0:T(8,128)(2,1)}, u32[]{:S(2)}, u32[]{:S(2)}) collective-permute-start(bf16[4,384,384]{2,1,0:T(8,128)(2,1)} %get-tuple-element.71), channel_id=1, source_target_pairs={{0,16},{2,18},{16,32},{18,34},{4,20},{6,22},{20,36},{22,38},{8,24}... | collective-permute-start | bytes 3538952 | tf_op jit(solution)/shard_map/ppermute | solution.py:95
  213.8 9.7 %collective-permute-start.17 = (bf16[2,96,768]{2,1,0:T(8,128)(2,1)S(1)}, bf16[2,96,768]{2,1,0:T(8,128)(2,1)}, u32[]{:S(2)}, u32[]{:S(2)}) collective-permute-start(bf16[2,96,768]{2,1,0:T(8,128)(2,1)S(1)} %get-tuple-element.112), channel_id=1, source_target_pairs={{0,32},{1,5},{2,34},{3,7},{16,48},{17,21},{18,50},{19,23},{4,36},{... | collective-permute-start | bytes 884744 | tf_op jit(solution)/shard_map/ppermute | solution.py:95
  213.9 12.7 %collective-permute-start.18 = (bf16[2,96,768]{2,1,0:T(8,128)(2,1)S(1)}, bf16[2,96,768]{2,1,0:T(8,128)(2,1)}, u32[]{:S(2)}, u32[]{:S(2)}) collective-permute-start(bf16[2,96,768]{2,1,0:T(8,128)(2,1)S(1)} %get-tuple-element.111), channel_id=1, source_target_pairs={{0,64},{1,9},{2,66},{3,11},{16,80},{17,25},{18,82},{19,27},{4,68},... | collective-permute-start | bytes 884744 | tf_op jit(solution)/shard_map/ppermute | solution.py:95
  214.0 12.6 %collective-permute-start.19 = (bf16[2,96,768]{2,1,0:T(8,128)(2,1)S(1)}, bf16[2,96,768]{2,1,0:T(8,128)(2,1)}, u32[]{:S(2)}, u32[]{:S(2)}) collective-permute-start(bf16[2,96,768]{2,1,0:T(8,128)(2,1)S(1)} %get-tuple-element.110), channel_id=1, source_target_pairs={{0,96},{1,13},{2,98},{3,15},{16,112},{17,29},{18,114},{19,31},{4,1... | collective-permute-start | bytes 884744 | tf_op jit(solution)/shard_map/ppermute | solution.py:95
  228.0 30.0 %collective-permute-start.22 = (bf16[96,768]{1,0:T(8,128)(2,1)S(1)}, bf16[96,768]{1,0:T(8,128)(2,1)S(1)}, u32[]{:S(2)}, u32[]{:S(2)}) collective-permute-start(bf16[96,768]{1,0:T(8,128)(2,1)S(1)} %get-tuple-element.113), channel_id=1, source_target_pairs={{0,2},{1,3},{2,0},{3,1},{16,18},{17,19},{18,16},{19,17},{4,6},{5,7... | collective-permute-start | bytes 442376 | tf_op jit(solution)/shard_map/ppermute | solution.py:95
  241.8 1.5 copy-start.6
  258.1 15.0 %collective-permute-start.24 = (bf16[96,768]{1,0:T(8,128)(2,1)S(1)}, bf16[96,768]{1,0:T(8,128)(2,1)S(1)}, u32[]{:S(2)}, u32[]{:S(2)}) collective-permute-start(bf16[96,768]{1,0:T(8,128)(2,1)S(1)} %add_convert_fusion.1), channel_id=1, source_target_pairs={{0,16},{1,17},{2,18},{3,19},{16,0},{17,1},{18,2},{19,3},{4,20},{5,... | collective-permute-start | bytes 442376 | tf_op jit(solution)/shard_map/ppermute | solution.py:95
  273.1 9.4 %collective-permute-start.25 = (f32[96,768]{1,0:T(8,128)S(1)}, f32[96,768]{1,0:T(8,128)S(1)}, u32[]{:S(2)}, u32[]{:S(2)}) collective-permute-start(f32[96,768]{1,0:T(8,128)S(1)} %add_multiply_fusion), channel_id=1, source_target_pairs={{0,96},{1,97},{2,98},{3,99},{16,112},{17,113},{18,114},{19,115},{4... | collective-permute-start | bytes 884744 | tf_op jit(solution)/shard_map/ppermute | solution.py:95
  273.2 1.7 copy-start.7
  274.9 2.9 copy-start.9
  280.5 8.3 %collective-permute-start.26 = (f32[96,768]{1,0:T(8,128)S(1)}, f32[96,768]{1,0:T(8,128)S(1)}, u32[]{:S(2)}, u32[]{:S(2)}) collective-permute-start(f32[96,768]{1,0:T(8,128)S(1)} %add_multiply_fusion), channel_id=1, source_target_pairs={{0,64},{1,65},{2,66},{3,67},{16,80},{17,81},{18,82},{19,83},{4,68}... | collective-permute-start | bytes 884744 | tf_op jit(solution)/shard_map/ppermute | solution.py:95
  281.8 10.1 %collective-permute-start.27 = (f32[96,768]{1,0:T(8,128)S(1)}, f32[96,768]{1,0:T(8,128)S(1)}, u32[]{:S(2)}, u32[]{:S(2)}) collective-permute-start(f32[96,768]{1,0:T(8,128)S(1)} %add_multiply_fusion), channel_id=1, source_target_pairs={{0,32},{1,33},{2,34},{3,35},{16,48},{17,49},{18,50},{19,51},{4,36}... | collective-permute-start | bytes 884744 | tf_op jit(solution)/shard_map/ppermute | solution.py:95
  (4 other events, 4.8 us)

commit v3 on v2

--- a/solution.py
+++ b/solution.py
@@ -518,21 +518,12 @@
     own_row = own_stats(where, after(q, term_mine), k, bias)
     plane = after(plane, qa[1], qb, own_row)
     other = send(plane, SWAP_CORE)
-    term_far = send(after(term_other, plane), SWAP_CORE)
+    term_far = send(after(term_other, other), SWAP_CORE)
 
     qa = jnp.concatenate(qa, axis=0)
     stat_a = far_stats(where, 0, after(qa, plane), k)
     stat_b = far_stats(where, 1, after(qb, stat_a), k)
     far_row = jnp.concatenate([send(stat_a, ROUTE_B), send(stat_b, ROUTE_A)], axis=2)
-
-    first, second = pick(core, y, z), pick(core, z, y)
-    term_far = after(term_far, stat_b)
-    rows_shape = (2, ROWS, QUARTER)
-    kept, given = split(term_mine.reshape(2, 2, 4, *rows_shape), first % 2, 1)
-    kept_far, given_far = split(term_far.reshape(2, 2, 4, *rows_shape), first % 2, 1)
-    halves = added(given, given_far)
-    g = after(g, halves)
-    halves = send(halves, swap_first(1))
 
     back_a, dots_a = back(where, 0, g, plane, other, o)
     far_row = after(far_row, dots_a)
@@ -549,6 +540,15 @@
     far_rows = jnp.where(far_allowed[None], row_total, NEVER)
     back_a = with_statistics(back_a, far_rows[:, :, :TILE], dots_a)
     far_a = send(back_a, ROUTE_A)
+    first, second = pick(core, y, z), pick(core, z, y)
+    term_far = after(term_far, back_a)
+    rows_shape = (2, ROWS, QUARTER)
+    kept, given = split(term_mine.reshape(2, 2, 4, *rows_shape), first % 2, 1)
+    kept_far, given_far = split(term_far.reshape(2, 2, 4, *rows_shape), first % 2, 1)
+    halves = added(given, given_far)
+    g = after(g, halves)
+    halves = send(halves, swap_first(1))
+
     back_b, dots_b = back(where, 1, after(g, back_a), plane, other, o)
     back_b = with_statistics(back_b, far_rows[:, :, TILE:], dots_b)
     far_b = send(back_b, ROUTE_B)
@@ -579,7 +579,6 @@
     dq0, *held = own_grads(where, q, k, v, *arguments, (), 0, 2)
     dq1, *held = own_grads(where, after(q, dq0), k, v, *arguments, held, 2, 2)
     both = added(kept, after(beside, dq1))
-    both, returned_b = lax.optimization_barrier((both, returned_b))
     both_far = send(both, SWAP_HIGH)
     joined = join(where, dq0, returned_a, returned_b, (), 0, 2)
     whole = (both.astype(F32) + both_far.astype(F32)) * (1.0 / math.sqrt(16 * 6144))

time: 295 us -> 308 us (1.044)
  the two profiles are of different devices: /device:TPU:0 before, /device:TPU:39 now
where the time goes in v3:
time: 308 us
  Pallas kernels  105 us (34%)
  starting transfers between devices  91.8 us (30%)
  waiting for transfers between devices  62.3 us (20%)
  other arithmetic  21.6 us (7%)
  local copies, waits for them, and re-layouts  13.9 us (5%)
  between operations  13.2 us (4%)
    ppermute x28, starting transfers between devices, send(): return lax.ppermute(block, AXES, pairs)  91.8 us
    ppermute x28, waiting for transfers between devices, send(): return lax.ppermute(block, AXES, pairs)  62.3 us
    pallas_call x2, Pallas kernels, own_grads(): pl.pallas_call(own_kernel, grid_spec=pltpu.PrefetchScalarGridSpec(num_sca...  26.7 us
    pallas_call x2, Pallas kernels, back(): pl.pallas_call(back_kernel, grid_spec=pltpu.PrefetchScalarGridSpec(num_sc...  23.7 us
    pallas_call x2, Pallas kernels, far_grads(): pl.pallas_call(functools.partial(far_kernel, side), grid_spec=pltpu.Prefe...  19.3 us
    pallas_call x1, Pallas kernels, weight_term(): pl.pallas_call(weight_term_kernel, grid_spec=pltpu.PrefetchScalarGridSpec...  16 us
    convert_element_type x5, other arithmetic, added(): return sum((v.astype(F32) for v in values)).astype(BF16)  9.38 us
    pallas_call x1, Pallas kernels, own_stats(): pl.pallas_call(own_stats_kernel, grid_spec=pltpu.PrefetchScalarGridSpec(n...  9.31 us
  transfers between devices with their start and end apart: 28, of which 8 were waited for; matrix products, arithmetic and copies ran while one was open for 8% of the time, Pallas kernels for 33%

profile of v3, /device:TPU:39, one launch (start us, length us, event | category | flops | bytes accessed | tf_op | source)
XLA Modules:
  0.0 307.6 jit_solution(1274028120236746688)
XLA Ops:
  3.6 1.4 fusion.18
  13.5 1.9 dynamic-slice_bitcast_fusion.11
  16.2 2.7 collective-permute-start.4
  20.7 3.5 %collective-permute-start.2 = (bf16[2,96,768]{2,1,0:T(8,128)(2,1)}, bf16[2,96,768]{2,1,0:T(8,128)(2,1)}, u32[]{:S(2)}, u32[]{:S(2)}) collective-permute-start(bf16[2,96,768]{2,1,0:T(8,128)(2,1)} %get-tuple-element.112), channel_id=1, source_target_pairs={{0,8},{1,65},{2,10},{3,67},{16,24},{17,81},{18,26},{19,83},{4,12},... | collective-permute-start | bytes 884744 | tf_op jit(solution)/shard_map/ppermute | solution.py:95
  24.2 2.1 collective-permute-start.3
  26.6 2.9 collective-permute-start.9
  29.6 2.2 collective-permute-done.1
  31.8 1.9 collective-permute-start.8
  33.7 3.8 %collective-permute-done.2 = bf16[2,96,768]{2,1,0:T(8,128)(2,1)} collective-permute-done((bf16[2,96,768]{2,1,0:T(8,128)(2,1)}, bf16[2,96,768]{2,1,0:T(8,128)(2,1)}, u32[]{:S(2)}, u32[]{:S(2)}) %collective-permute-start.2) | collective-permute-done | bytes 294944 | tf_op jit(solution)/shard_map/ppermute | solution.py:95
  37.5 1.3 pad_maximum_fusion.1
  38.8 2.5 collective-permute-start.5
  42.4 16.0 %weight_term.1 = (bf16[4,4,2,96,768]{4,3,2,1,0:T(8,128)(2,1)}, bf16[4,4,2,96,768]{4,3,2,1,0:T(8,128)(2,1)}) custom-call(s32[5]{0:T(128)S(1)} %stack.108.where, bf16[768,1536]{1,0:T(8,128)(2,1)S(1)} %bitcast.125, bf16[768,3072]{1,0:T(8,128)(2,1)} %bitcast.141), custom_call_target="tpu_custom_call" | custom-call | flops 99999997952 | bytes 1000000 | tf_op jit(solution)/shard_map/weight_term/pallas_call | solution.py:413
  58.4 9.3 %own_stats.1 = f32[12,1,768]{2,1,0:T(1,128)S(1)} custom-call(s32[5]{0:T(128)S(1)} %stack.108.where, bf16[768,1536]{1,0:T(8,128)(2,1)S(1)} %bitcast.124, bf16[768,1536]{1,0:T(8,128)(2,1)S(1)} %bitcast.118, f32[2,768]{1,0:T(2,128)S(1)} %add_select_fusion.bias), custom_call_target="tpu_custom_call" | custom-call | flops 100000000 | bytes 100000 | tf_op jit(solution)/shard_map/own_stats/pallas_call | solution.py:146
  67.7 3.1 %collective-permute-done.7 = bf16[4,2,96,768]{3,2,1,0:T(8,128)(2,1)S(1)} collective-permute-done((bf16[4,2,96,768]{3,2,1,0:T(8,128)(2,1)S(1)}, bf16[4,2,96,768]{3,2,1,0:T(8,128)(2,1)S(1)}, u32[]{:S(2)}, u32[]{:S(2)}) %collective-permute-start.7) | collective-permute-done | bytes 1179680 | tf_op jit(solution)/shard_map/ppermute | solution.py:95
  70.8 2.4 pad_maximum_fusion.mine_z.mine_y
  73.3 15.4 %collective-permute-start.10 = (bf16[4,4,2,96,768]{4,3,2,1,0:T(8,128)(2,1)}, bf16[4,4,2,96,768]{4,3,2,1,0:T(8,128)(2,1)}, u32[]{:S(2)}, u32[]{:S(2)}) collective-permute-start(bf16[4,4,2,96,768]{4,3,2,1,0:T(8,128)(2,1)} %pad_maximum_fusion.mine_z.mine_y), channel_id=1, source_target_pairs={{0,1},{1,0},{2,3},{3,2},{16,17},{17,16},{18,19},{19,18},{4,5},{5,4... | collective-permute-start | bytes 14155784 | tf_op jit(solution)/shard_map/ppermute | solution.py:95
  88.7 1.1 constant_dynamic-update-slice_fusion.1
  89.9 3.2 %far_stats.2 = f32[12,1,384]{2,1,0:T(1,128)S(1)} custom-call(s32[5]{0:T(128)S(1)} %stack.108.where, bf16[4,384,384]{2,1,0:T(8,128)(2,1)S(1)} %constant_dynamic-update-slice_fusion.q, bf16[768,1536]{1,0:T(8,128)(2,1)S(1)} %bitcast.119), custom_call_target="tpu_custom_call" | custom-call | flops 100000000 | bytes 100000 | tf_op jit(solution)/shard_map/far_stats/pallas_call | solution.py:174
  93.2 3.2 %far_stats.3 = f32[12,1,384]{2,1,0:T(1,128)S(1)} custom-call(s32[5]{0:T(128)S(1)} %stack.108.where, bf16[4,384,384]{2,1,0:T(8,128)(2,1)S(1)} %collective-permute-done.9.q, bf16[768,1536]{1,0:T(8,128)(2,1)S(1)} %bitcast.120), custom_call_target="tpu_custom_call" | custom-call | flops 100000000 | bytes 100000 | tf_op jit(solution)/shard_map/far_stats/pallas_call | solution.py:174
  96.4 6.6 %collective-permute-start.13 = (f32[12,1,384]{2,1,0:T(1,128)S(1)}, f32[12,1,384]{2,1,0:T(1,128)S(1)}, u32[]{:S(2)}, u32[]{:S(2)}) collective-permute-start(f32[12,1,384]{2,1,0:T(1,128)S(1)} %far_stats.3), channel_id=1, source_target_pairs={{0,16},{2,18},{16,32},{18,34},{4,20},{6,22},{20,36},{22,38},{8,24}... | collective-permute-start | bytes 55304 | tf_op jit(solution)/shard_map/ppermute | solution.py:95
  103.0 5.6 %collective-permute-start.12 = (f32[12,1,384]{2,1,0:T(1,128)S(1)}, f32[12,1,384]{2,1,0:T(1,128)S(1)}, u32[]{:S(2)}, u32[]{:S(2)}) collective-permute-start(f32[12,1,384]{2,1,0:T(1,128)S(1)} %far_stats.2), channel_id=1, source_target_pairs={{16,0},{18,2},{20,4},{22,6},{24,8},{26,10},{28,12},{30,14},{32,16}... | collective-permute-start | bytes 55304 | tf_op jit(solution)/shard_map/ppermute | solution.py:95
  112.7 2.8 collective-permute-start.11
  115.5 1.7 copy-done.19
  117.1 11.9 %out_back.2 = (bf16[4,400,384]{2,1,0:T(8,128)(2,1)S(1)}, f32[12,1,384]{2,1,0:T(1,128)S(1)}) custom-call(s32[5]{0:T(128)S(1)} %stack.108.where, bf16[768,3072]{1,0:T(8,128)(2,1)} %bitcast.142, bf16[4,4,2,96,768]{4,3,2,1,0:T(8,128)(2,1)} %pad_maximum_fusion.mine_z.mine_y, bf16[4,4,2,96,768]{4,3,2,1,0:T(8,128)(2,1)} %pad_maximum_fusion.mine_z.mine_y, ...), custom_call_target="tpu_custom_call" | custom-call | flops 99999997952 | bytes 1000000 | tf_op jit(solution)/shard_map/out_back/pallas_call | solution.py:225
  131.1 1.9 collective-permute-start.16
  133.0 4.6 %fusion.1 = bf16[2,4,2,96,768]{4,3,2,1,0:T(8,128)(2,1)} fusion(bf16[2,2,4,2,96,768]{5,4,3,2,1,0:T(8,128)(2,1)} %bitcast.37, s32[]{:T(128)S(6)} %select_n.251, bf16[2,2,4,2,96,768]{5,4,3,2,1,0:T(8,128)(2,1)} %bitcast.134), kind=kLoop, calls=%fused_computation.4 | loop fusion | flops 4718592 | bytes 7077892 | tf_op jit(solution)/shard_map/convert_element_type | solution.py:446
  137.7 11.9 %out_back.3 = (bf16[4,400,384]{2,1,0:T(8,128)(2,1)S(1)}, f32[12,1,384]{2,1,0:T(1,128)S(1)}) custom-call(s32[5]{0:T(128)S(1)} %stack.108.where, bf16[768,3072]{1,0:T(8,128)(2,1)} %bitcast.143, bf16[4,4,2,96,768]{4,3,2,1,0:T(8,128)(2,1)} %pad_maximum_fusion.mine_z.mine_y, bf16[4,4,2,96,768]{4,3,2,1,0:T(8,128)(2,1)} %pad_maximum_fusion.mine_z.mine_y, ...), custom_call_target="tpu_custom_call" | custom-call | flops 99999997952 | bytes 1000000 | tf_op jit(solution)/shard_map/out_back/pallas_call | solution.py:225
  150.7 5.8 %collective-permute-start.20 = (bf16[4,400,384]{2,1,0:T(8,128)(2,1)S(1)}, bf16[4,400,384]{2,1,0:T(8,128)(2,1)S(1)}, u32[]{:S(2)}, u32[]{:S(2)}) collective-permute-start(bf16[4,400,384]{2,1,0:T(8,128)(2,1)S(1)} %dynamic_update_slice.7.back_b), channel_id=1, source_target_pairs={{16,0},{18,2},{20,4},{22,6},{24,8},{26,10},{28,12},{30,14},{32,16}... | collective-permute-start | bytes 3686408 | tf_op jit(solution)/shard_map/ppermute | solution.py:95
  156.4 25.8 %collective-permute-done.14 = bf16[2,4,2,96,768]{4,3,2,1,0:T(8,128)(2,1)} collective-permute-done((bf16[2,4,2,96,768]{4,3,2,1,0:T(8,128)(2,1)}, bf16[2,4,2,96,768]{4,3,2,1,0:T(8,128)(2,1)}, u32[]{:S(2)}, u32[]{:S(2)}) %collective-permute-start.14) | collective-permute-done | bytes 2359328 | tf_op jit(solution)/shard_map/ppermute | solution.py:95
  182.2 4.2 %fusion = bf16[2,4,2,96,768]{4,3,2,1,0:T(8,128)(2,1)S(1)} fusion(bf16[2,4,2,96,768]{4,3,2,1,0:T(8,128)(2,1)} %collective-permute-done.14, bf16[2,2,4,2,96,768]{5,4,3,2,1,0:T(8,128)(2,1)} %bitcast.37, s32[]{:T(128)S(6)} %select_n.236, bf16[2,2,4,2,96,768]{5,4,3,2,1,0:T(8,128)(2,1)} %bitcast.135), kind=kLoop, calls=%fused_computation.2 | loop fusion | flops 7077888 | bytes 9437188 | tf_op jit(solution)/shard_map/convert_element_type | solution.py:446
  186.6 21.7 %collective-permute-start.15 = (bf16[4,2,96,768]{3,2,1,0:T(8,128)(2,1)S(1)}, bf16[4,2,96,768]{3,2,1,0:T(8,128)(2,1)S(1)}, u32[]{:S(2)}, u32[]{:S(2)}) collective-permute-start(bf16[4,2,96,768]{3,2,1,0:T(8,128)(2,1)S(1)} %dynamic-slice_bitcast_fusion), channel_id=1, source_target_pairs={{0,8},{1,65},{2,10},{3,67},{16,24},{17,81},{18,26},{19,83},{4,12},... | collective-permute-start | bytes 3538952 | tf_op jit(solution)/shard_map/ppermute | solution.py:95
  208.3 9.7 %far_grads.2 = (bf16[4,384,384]{2,1,0:T(8,128)(2,1)S(1)}, f32[4,384,384]{2,1,0:T(8,128)S(1)}, f32[4,384,384]{2,1,0:T(8,128)}) custom-call(s32[5]{0:T(128)S(1)} %stack.108.where, bf16[4,384,384]{2,1,0:T(8,128)(2,1)S(1)} %copy-done.7, bf16[4,400,384]{2,1,0:T(8,128)(2,1)} %collective-permute-done.16.b, bf16[768,1536]{1,0:T(8,128)(2,1)} %bitcast.114, ...), custom_call_target="tpu_custom_call" | custom-call | flops 99999997952 | bytes 1000000 | tf_op jit(solution)/shard_map/far_grads/pallas_call | solution.py:346
  218.0 2.2 collective-permute-start.21
  220.2 4.3 %collective-permute-done.15 = bf16[4,2,96,768]{3,2,1,0:T(8,128)(2,1)S(1)} collective-permute-done((bf16[4,2,96,768]{3,2,1,0:T(8,128)(2,1)S(1)}, bf16[4,2,96,768]{3,2,1,0:T(8,128)(2,1)S(1)}, u32[]{:S(2)}, u32[]{:S(2)}) %collective-permute-start.15) | collective-permute-done | bytes 1179680 | tf_op jit(solution)/shard_map/ppermute | solution.py:95
  225.5 2.7 collective-permute-start.18
  228.3 9.6 %far_grads.3 = (bf16[4,384,384]{2,1,0:T(8,128)(2,1)S(1)}, f32[4,384,384]{2,1,0:T(8,128)S(1)}, f32[4,384,384]{2,1,0:T(8,128)}) custom-call(s32[5]{0:T(128)S(1)} %stack.108.where, bf16[4,384,384]{2,1,0:T(8,128)(2,1)S(1)} %copy-done.13, bf16[4,400,384]{2,1,0:T(8,128)(2,1)S(1)} %collective-permute-done.20.b, bf16[768,1536]{1,0:T(8,128)(2,1)} %bitcast.115, ...), custom_call_target="tpu_custom_call" | custom-call | flops 99999997952 | bytes 1000000 | tf_op jit(solution)/shard_map/far_grads/pallas_call | solution.py:346
  237.9 1.4 copy-done.3
  239.6 1.4 collective-permute-start.23
  241.1 13.4 %own_grads.2 = (f32[2,768,384]{2,1,0:T(8,128)S(1)}, bf16[768,1536]{1,0:T(8,128)(2,1)}, bf16[768,1536]{1,0:T(8,128)(2,1)}) custom-call(s32[5]{0:T(128)S(1)} %stack.108.where, bf16[768,1536]{1,0:T(8,128)(2,1)} %bitcast.122, bf16[768,1536]{1,0:T(8,128)(2,1)} %bitcast.116, bf16[768,1536]{1,0:T(8,128)(2,1)} %bitcast.131, ...), custom_call_target="tpu_custom_call" | custom-call | flops 100000000 | bytes 100000 | tf_op jit(solution)/shard_map/own_grads/pallas_call | solution.py:297
  254.5 1.5 copy-done.8
  255.9 13.3 %own_grads.3 = (f32[2,768,384]{2,1,0:T(8,128)S(1)}, bf16[768,1536]{1,0:T(8,128)(2,1)}, bf16[768,1536]{1,0:T(8,128)(2,1)}) custom-call(s32[5]{0:T(128)S(1)} %stack.108.where, bf16[768,1536]{1,0:T(8,128)(2,1)} %bitcast.123, bf16[768,1536]{1,0:T(8,128)(2,1)} %bitcast.117, bf16[768,1536]{1,0:T(8,128)(2,1)} %bitcast.132, ...), custom_call_target="tpu_custom_call", output_to_operand_aliasing={{1}: (13, {}), {2}: (14, {})} | custom-call | flops 100000000 | bytes 100000 | tf_op jit(solution)/shard_map/own_grads/pallas_call | solution.py:297
  269.3 1.4 copy-done.10
  271.7 4.6 %collective-permute-done.24 = bf16[96,768]{1,0:T(8,128)(2,1)S(1)} collective-permute-done((bf16[96,768]{1,0:T(8,128)(2,1)S(1)}, bf16[96,768]{1,0:T(8,128)(2,1)S(1)}, u32[]{:S(2)}, u32[]{:S(2)}) %collective-permute-start.24) | collective-permute-done | bytes 147488 | tf_op jit(solution)/shard_map/ppermute | solution.py:95
  276.3 1.6 collective-permute-start.25
  278.0 3.8 %collective-permute-start.22 = (bf16[4,384,384]{2,1,0:T(8,128)(2,1)}, bf16[4,384,384]{2,1,0:T(8,128)(2,1)S(1)}, u32[]{:S(2)}, u32[]{:S(2)}) collective-permute-start(bf16[4,384,384]{2,1,0:T(8,128)(2,1)} %copy-done.21), channel_id=1, source_target_pairs={{0,16},{2,18},{16,32},{18,34},{4,20},{6,22},{20,36},{22,38},{8,24}... | collective-permute-start | bytes 3538952 | tf_op jit(solution)/shard_map/ppermute | solution.py:95
  283.3 18.3 %collective-permute-done.26 = f32[96,768]{1,0:T(8,128)S(1)} collective-permute-done((f32[96,768]{1,0:T(8,128)S(1)}, f32[96,768]{1,0:T(8,128)S(1)}, u32[]{:S(2)}, u32[]{:S(2)}) %collective-permute-start.26) | collective-permute-done | bytes 294944 | tf_op jit(solution)/shard_map/ppermute | solution.py:95
  304.2 1.7 join_query_grad.2.rest_0_
  305.9 1.7 join_query_grad.3
  (126 shorter events, 17.5 us)
Async XLA Ops:
  1.6 11.9 %collective-permute-start = (bf16[96,768]{1,0:T(8,128)(2,1)S(1)}, bf16[96,768]{1,0:T(8,128)(2,1)S(1)}, u32[]{:S(2)}, u32[]{:S(2)}) collective-permute-start(bf16[96,768]{1,0:T(8,128)(2,1)S(1)} %constant_dynamic-slice_fusion), channel_id=1, source_target_pairs={{0,2},{1,3},{2,0},{3,1},{16,18},{17,19},{18,16},{19,17},{4,6},{5,7... | collective-permute-start | bytes 442376 | tf_op jit(solution)/shard_map/ppermute | solution.py:95
  16.2 22.6 %collective-permute-start.4 = (bf16[2,384,384]{2,1,0:T(8,128)(2,1)}, bf16[2,384,384]{2,1,0:T(8,128)(2,1)}, u32[]{:S(2)}, u32[]{:S(2)}) collective-permute-start(bf16[2,384,384]{2,1,0:T(8,128)(2,1)} %pad_maximum_fusion.4), channel_id=1, source_target_pairs={{0,16},{2,18},{16,32},{18,34},{4,20},{6,22},{20,36},{22,38},{8,24}... | collective-permute-start | bytes 1769480 | tf_op jit(solution)/shard_map/ppermute | solution.py:95
  20.7 11.1 %collective-permute-start.1 = (bf16[2,96,768]{2,1,0:T(8,128)(2,1)}, bf16[2,96,768]{2,1,0:T(8,128)(2,1)}, u32[]{:S(2)}, u32[]{:S(2)}) collective-permute-start(bf16[2,96,768]{2,1,0:T(8,128)(2,1)} %get-tuple-element.112), channel_id=1, source_target_pairs={{0,12},{1,97},{2,14},{3,99},{16,28},{17,113},{18,30},{19,115},{4,0... | collective-permute-start | bytes 884744 | tf_op jit(solution)/shard_map/ppermute | solution.py:95
  20.7 16.8 %collective-permute-start.2 = (bf16[2,96,768]{2,1,0:T(8,128)(2,1)}, bf16[2,96,768]{2,1,0:T(8,128)(2,1)}, u32[]{:S(2)}, u32[]{:S(2)}) collective-permute-start(bf16[2,96,768]{2,1,0:T(8,128)(2,1)} %get-tuple-element.112), channel_id=1, source_target_pairs={{0,8},{1,65},{2,10},{3,67},{16,24},{17,81},{18,26},{19,83},{4,12},... | collective-permute-start | bytes 884744 | tf_op jit(solution)/shard_map/ppermute | solution.py:95
  24.2 13.3 %collective-permute-start.3 = (bf16[2,96,768]{2,1,0:T(8,128)(2,1)}, bf16[2,96,768]{2,1,0:T(8,128)(2,1)}, u32[]{:S(2)}, u32[]{:S(2)}) collective-permute-start(bf16[2,96,768]{2,1,0:T(8,128)(2,1)} %get-tuple-element.112), channel_id=1, source_target_pairs={{0,4},{1,33},{2,6},{3,35},{16,20},{17,49},{18,22},{19,51},{4,8},{5... | collective-permute-start | bytes 884744 | tf_op jit(solution)/shard_map/ppermute | solution.py:95
  26.6 15.8 %copy-start.18 = (bf16[1,768,1536]{2,1,0:T(8,128)(2,1)S(1)}, bf16[1,768,1536]{2,1,0:T(8,128)(2,1)}, u32[]{:S(2)}) copy-start(bf16[1,768,1536]{2,1,0:T(8,128)(2,1)} %param.11) | copy-start | bytes 7077892
  26.6 46.7 %collective-permute-start.9 = (bf16[4,384,384]{2,1,0:T(8,128)(2,1)S(1)}, bf16[4,384,384]{2,1,0:T(8,128)(2,1)S(1)}, u32[]{:S(2)}, u32[]{:S(2)}) collective-permute-start(bf16[4,384,384]{2,1,0:T(8,128)(2,1)S(1)} %pad_maximum_fusion.2), channel_id=1, source_target_pairs={{16,0},{18,2},{20,4},{22,6},{24,8},{26,10},{28,12},{30,14},{32,16}... | collective-permute-start | bytes 3538952 | tf_op jit(solution)/shard_map/ppermute | solution.py:95
  31.8 41.5 %collective-permute-start.8 = (bf16[2,384,384]{2,1,0:T(8,128)(2,1)S(1)}, bf16[2,384,384]{2,1,0:T(8,128)(2,1)S(1)}, u32[]{:S(2)}, u32[]{:S(2)}) collective-permute-start(bf16[2,384,384]{2,1,0:T(8,128)(2,1)S(1)} %pad_maximum_fusion.5), channel_id=1, source_target_pairs={{0,16},{2,18},{16,32},{18,34},{4,20},{6,22},{20,36},{22,38},{8,24}... | collective-permute-start | bytes 1769480 | tf_op jit(solution)/shard_map/ppermute | solution.py:95
  38.8 28.8 %collective-permute-start.5 = (bf16[4,2,96,768]{3,2,1,0:T(8,128)(2,1)S(1)}, bf16[4,2,96,768]{3,2,1,0:T(8,128)(2,1)S(1)}, u32[]{:S(2)}, u32[]{:S(2)}) collective-permute-start(bf16[4,2,96,768]{3,2,1,0:T(8,128)(2,1)S(1)} %pad_maximum_fusion.1), channel_id=1, source_target_pairs={{0,96},{1,13},{2,98},{3,15},{16,112},{17,29},{18,114},{19,31},{4,1... | collective-permute-start | bytes 3538952 | tf_op jit(solution)/shard_map/ppermute | solution.py:95
  41.4 26.3 %collective-permute-start.6 = (bf16[4,2,96,768]{3,2,1,0:T(8,128)(2,1)S(1)}, bf16[4,2,96,768]{3,2,1,0:T(8,128)(2,1)S(1)}, u32[]{:S(2)}, u32[]{:S(2)}) collective-permute-start(bf16[4,2,96,768]{3,2,1,0:T(8,128)(2,1)S(1)} %pad_maximum_fusion.1), channel_id=1, source_target_pairs={{0,64},{1,9},{2,66},{3,11},{16,80},{17,25},{18,82},{19,27},{4,68},... | collective-permute-start | bytes 3538952 | tf_op jit(solution)/shard_map/ppermute | solution.py:95
  41.7 29.1 %collective-permute-start.7 = (bf16[4,2,96,768]{3,2,1,0:T(8,128)(2,1)S(1)}, bf16[4,2,96,768]{3,2,1,0:T(8,128)(2,1)S(1)}, u32[]{:S(2)}, u32[]{:S(2)}) collective-permute-start(bf16[4,2,96,768]{3,2,1,0:T(8,128)(2,1)S(1)} %pad_maximum_fusion.1), channel_id=1, source_target_pairs={{0,32},{1,5},{2,34},{3,7},{16,48},{17,21},{18,50},{19,23},{4,36},{... | collective-permute-start | bytes 3538952 | tf_op jit(solution)/shard_map/ppermute | solution.py:95
  42.4 16.0 %copy-start = (bf16[1,768,1536]{2,1,0:T(8,128)(2,1)S(1)}, bf16[1,768,1536]{2,1,0:T(8,128)(2,1)}, u32[]{:S(2)}) copy-start(bf16[1,768,1536]{2,1,0:T(8,128)(2,1)} %param.9) | copy-start | bytes 7077892
  42.4 16.0 %copy-start.1 = (bf16[1,768,1536]{2,1,0:T(8,128)(2,1)S(1)}, bf16[1,768,1536]{2,1,0:T(8,128)(2,1)}, u32[]{:S(2)}) copy-start(bf16[1,768,1536]{2,1,0:T(8,128)(2,1)} %param.8) | copy-start | bytes 7077892
  73.3 19.9 %copy-start.12 = (bf16[4,384,384]{2,1,0:T(8,128)(2,1)}, bf16[4,384,384]{2,1,0:T(8,128)(2,1)S(1)}, u32[]{:S(2)}) copy-start(bf16[4,384,384]{2,1,0:T(8,128)(2,1)S(1)} %collective-permute-done.9.q) | copy-start | bytes 3538948
  73.3 39.4 %collective-permute-start.10 = (bf16[4,4,2,96,768]{4,3,2,1,0:T(8,128)(2,1)}, bf16[4,4,2,96,768]{4,3,2,1,0:T(8,128)(2,1)}, u32[]{:S(2)}, u32[]{:S(2)}) collective-permute-start(bf16[4,4,2,96,768]{4,3,2,1,0:T(8,128)(2,1)} %pad_maximum_fusion.mine_z.mine_y), channel_id=1, source_target_pairs={{0,1},{1,0},{2,3},{3,2},{16,17},{17,16},{18,19},{19,18},{4,5},{5,4... | collective-permute-start | bytes 14155784 | tf_op jit(solution)/shard_map/ppermute | solution.py:95
  89.9 6.5 %copy-start.6 = (bf16[4,384,384]{2,1,0:T(8,128)(2,1)}, bf16[4,384,384]{2,1,0:T(8,128)(2,1)S(1)}, u32[]{:S(2)}) copy-start(bf16[4,384,384]{2,1,0:T(8,128)(2,1)S(1)} %constant_dynamic-update-slice_fusion.q) | copy-start | bytes 3538948
  96.4 16.2 %collective-permute-start.13 = (f32[12,1,384]{2,1,0:T(1,128)S(1)}, f32[12,1,384]{2,1,0:T(1,128)S(1)}, u32[]{:S(2)}, u32[]{:S(2)}) collective-permute-start(f32[12,1,384]{2,1,0:T(1,128)S(1)} %far_stats.3), channel_id=1, source_target_pairs={{0,16},{2,18},{16,32},{18,34},{4,20},{6,22},{20,36},{22,38},{8,24}... | collective-permute-start | bytes 55304 | tf_op jit(solution)/shard_map/ppermute | solution.py:95
  103.0 9.7 %collective-permute-start.12 = (f32[12,1,384]{2,1,0:T(1,128)S(1)}, f32[12,1,384]{2,1,0:T(1,128)S(1)}, u32[]{:S(2)}, u32[]{:S(2)}) collective-permute-start(f32[12,1,384]{2,1,0:T(1,128)S(1)} %far_stats.2), channel_id=1, source_target_pairs={{16,0},{18,2},{20,4},{22,6},{24,8},{26,10},{28,12},{30,14},{32,16}... | collective-permute-start | bytes 55304 | tf_op jit(solution)/shard_map/ppermute | solution.py:95
  112.7 20.3 %collective-permute-start.11 = (bf16[4,4,2,96,768]{4,3,2,1,0:T(8,128)(2,1)}, bf16[4,4,2,96,768]{4,3,2,1,0:T(8,128)(2,1)}, u32[]{:S(2)}, u32[]{:S(2)}) collective-permute-start(bf16[4,4,2,96,768]{4,3,2,1,0:T(8,128)(2,1)} %get-tuple-element.53), channel_id=1, source_target_pairs={{0,1},{1,0},{2,3},{3,2},{16,17},{17,16},{18,19},{19,18},{4,5},{5,4... | collective-permute-start | bytes 14155784 | tf_op jit(solution)/shard_map/ppermute | solution.py:95
  115.5 1.7 copy-start.19
  117.1 11.9 %copy-start.25 = (pred[768]{0:T(1024)(128)(4,1)S(1)}, pred[768]{0:T(1024)(128)(4,1)}, u32[]{:S(2)}) copy-start(pred[768]{0:T(1024)(128)(4,1)} %get-tuple-element.128) | copy-start | bytes 2308
  117.1 12.7 %copy-start.24 = (pred[768]{0:T(1024)(128)(4,1)S(1)}, pred[768]{0:T(1024)(128)(4,1)}, u32[]{:S(2)}) copy-start(pred[768]{0:T(1024)(128)(4,1)} %get-tuple-element.127) | copy-start | bytes 2308
  131.1 77.2 %collective-permute-start.16 = (bf16[4,400,384]{2,1,0:T(8,128)(2,1)S(1)}, bf16[4,400,384]{2,1,0:T(8,128)(2,1)}, u32[]{:S(2)}, u32[]{:S(2)}) collective-permute-start(bf16[4,400,384]{2,1,0:T(8,128)(2,1)S(1)} %dynamic_update_slice.6.back_a), channel_id=1, source_target_pairs={{0,16},{2,18},{16,32},{18,34},{4,20},{6,22},{20,36},{22,38},{8,24}... | collective-permute-start | bytes 3686408 | tf_op jit(solution)/shard_map/ppermute | solution.py:95
  133.0 4.7 %copy-start.20 = (bf16[1,768,1536]{2,1,0:T(8,128)(2,1)S(1)}, bf16[1,768,1536]{2,1,0:T(8,128)(2,1)}, u32[]{:S(2)}) copy-start(bf16[1,768,1536]{2,1,0:T(8,128)(2,1)} %param.11) | copy-start | bytes 7077892
  137.7 44.6 %collective-permute-start.14 = (bf16[2,4,2,96,768]{4,3,2,1,0:T(8,128)(2,1)}, bf16[2,4,2,96,768]{4,3,2,1,0:T(8,128)(2,1)}, u32[]{:S(2)}, u32[]{:S(2)}) collective-permute-start(bf16[2,4,2,96,768]{4,3,2,1,0:T(8,128)(2,1)} %fusion.1), channel_id=1, source_target_pairs={{0,4},{1,33},{2,6},{3,35},{16,20},{17,49},{18,22},{19,51},{4,0},{5... | collective-permute-start | bytes 7077896 | tf_op jit(solution)/shard_map/ppermute | solution.py:95
  150.7 77.6 %collective-permute-start.20 = (bf16[4,400,384]{2,1,0:T(8,128)(2,1)S(1)}, bf16[4,400,384]{2,1,0:T(8,128)(2,1)S(1)}, u32[]{:S(2)}, u32[]{:S(2)}) collective-permute-start(bf16[4,400,384]{2,1,0:T(8,128)(2,1)S(1)} %dynamic_update_slice.7.back_b), channel_id=1, source_target_pairs={{16,0},{18,2},{20,4},{22,6},{24,8},{26,10},{28,12},{30,14},{32,16}... | collective-permute-start | bytes 3686408 | tf_op jit(solution)/shard_map/ppermute | solution.py:95
  186.5 21.8 %copy-start.7 = (bf16[4,384,384]{2,1,0:T(8,128)(2,1)S(1)}, bf16[4,384,384]{2,1,0:T(8,128)(2,1)}, u32[]{:S(2)}) copy-start(bf16[4,384,384]{2,1,0:T(8,128)(2,1)} %copy-done.6) | copy-start | bytes 3538948
  186.6 37.9 %collective-permute-start.15 = (bf16[4,2,96,768]{3,2,1,0:T(8,128)(2,1)S(1)}, bf16[4,2,96,768]{3,2,1,0:T(8,128)(2,1)S(1)}, u32[]{:S(2)}, u32[]{:S(2)}) collective-permute-start(bf16[4,2,96,768]{3,2,1,0:T(8,128)(2,1)S(1)} %dynamic-slice_bitcast_fusion), channel_id=1, source_target_pairs={{0,8},{1,65},{2,10},{3,67},{16,24},{17,81},{18,26},{19,83},{4,12},... | collective-permute-start | bytes 3538952 | tf_op jit(solution)/shard_map/ppermute | solution.py:95
  218.0 6.9 %copy-start.2 = (f32[4,384,384]{2,1,0:T(8,128)}, f32[4,384,384]{2,1,0:T(8,128)S(1)}, u32[]{:S(2)}) copy-start(f32[4,384,384]{2,1,0:T(8,128)S(1)} %get-tuple-element.76.dk_a) | copy-start | bytes 7077892
  218.0 10.3 %copy-start.13 = (bf16[4,384,384]{2,1,0:T(8,128)(2,1)S(1)}, bf16[4,384,384]{2,1,0:T(8,128)(2,1)}, u32[]{:S(2)}) copy-start(bf16[4,384,384]{2,1,0:T(8,128)(2,1)} %copy-done.12) | copy-start | bytes 3538948
  218.0 23.1 %collective-permute-start.21 = (bf16[4,384,384]{2,1,0:T(8,128)(2,1)S(1)}, bf16[4,384,384]{2,1,0:T(8,128)(2,1)S(1)}, u32[]{:S(2)}, u32[]{:S(2)}) collective-permute-start(bf16[4,384,384]{2,1,0:T(8,128)(2,1)S(1)} %get-tuple-element.66), channel_id=1, source_target_pairs={{16,0},{18,2},{20,4},{22,6},{24,8},{26,10},{28,12},{30,14},{32,16}... | collective-permute-start | bytes 3538952 | tf_op jit(solution)/shard_map/ppermute | solution.py:95
  224.8 14.5 %collective-permute-start.17 = (bf16[2,96,768]{2,1,0:T(8,128)(2,1)S(1)}, bf16[2,96,768]{2,1,0:T(8,128)(2,1)S(1)}, u32[]{:S(2)}, u32[]{:S(2)}) collective-permute-start(bf16[2,96,768]{2,1,0:T(8,128)(2,1)S(1)} %get-tuple-element.108), channel_id=1, source_target_pairs={{0,32},{1,5},{2,34},{3,7},{16,48},{17,21},{18,50},{19,23},{4,36},{... | collective-permute-start | bytes 884744 | tf_op jit(solution)/shard_map/ppermute | solution.py:95
  225.5 13.8 %collective-permute-start.18 = (bf16[2,96,768]{2,1,0:T(8,128)(2,1)S(1)}, bf16[2,96,768]{2,1,0:T(8,128)(2,1)S(1)}, u32[]{:S(2)}, u32[]{:S(2)}) collective-permute-start(bf16[2,96,768]{2,1,0:T(8,128)(2,1)S(1)} %get-tuple-element.107), channel_id=1, source_target_pairs={{0,64},{1,9},{2,66},{3,11},{16,80},{17,25},{18,82},{19,27},{4,68},... | collective-permute-start | bytes 884744 | tf_op jit(solution)/shard_map/ppermute | solution.py:95
  228.2 12.8 %copy-start.22 = (f32[12,1,768]{2,1,0:T(1,128)S(1)}, f32[12,1,768]{2,1,0:T(1,128)}, u32[]{:S(2)}) copy-start(f32[12,1,768]{2,1,0:T(1,128)} %get-tuple-element.115) | copy-start | bytes 110596
  228.2 12.8 %copy-start.23 = (f32[12,1,768]{2,1,0:T(1,128)S(1)}, f32[12,1,768]{2,1,0:T(1,128)}, u32[]{:S(2)}) copy-start(f32[12,1,768]{2,1,0:T(1,128)} %get-tuple-element.92) | copy-start | bytes 110596
  228.2 12.8 %copy-start.15 = (f32[12,1,384]{2,1,0:T(1,128)S(1)}, f32[12,1,384]{2,1,0:T(1,128)}, u32[]{:S(2)}) copy-start(f32[12,1,384]{2,1,0:T(1,128)} %copy-done.14) | copy-start | bytes 55300
  228.2 12.9 %copy-start.17 = (f32[12,1,384]{2,1,0:T(1,128)S(1)}, f32[12,1,384]{2,1,0:T(1,128)}, u32[]{:S(2)}) copy-start(f32[12,1,384]{2,1,0:T(1,128)} %copy-done.16) | copy-start | bytes 55300
  228.2 11.1 %collective-permute-start.19 = (bf16[2,96,768]{2,1,0:T(8,128)(2,1)S(1)}, bf16[2,96,768]{2,1,0:T(8,128)(2,1)S(1)}, u32[]{:S(2)}, u32[]{:S(2)}) collective-permute-start(bf16[2,96,768]{2,1,0:T(8,128)(2,1)S(1)} %get-tuple-element.106), channel_id=1, source_target_pairs={{0,96},{1,13},{2,98},{3,15},{16,112},{17,29},{18,114},{19,31},{4,1... | collective-permute-start | bytes 884744 | tf_op jit(solution)/shard_map/ppermute | solution.py:95
  239.3 15.1 %copy-start.21 = (bf16[4,384,384]{2,1,0:T(8,128)(2,1)}, bf16[4,384,384]{2,1,0:T(8,128)(2,1)S(1)}, u32[]{:S(2)}) copy-start(bf16[4,384,384]{2,1,0:T(8,128)(2,1)S(1)} %get-tuple-element.69) | copy-start | bytes 3538948
  239.6 31.1 %collective-permute-start.23 = (bf16[96,768]{1,0:T(8,128)(2,1)S(1)}, bf16[96,768]{1,0:T(8,128)(2,1)S(1)}, u32[]{:S(2)}, u32[]{:S(2)}) collective-permute-start(bf16[96,768]{1,0:T(8,128)(2,1)S(1)} %get-tuple-element.109), channel_id=1, source_target_pairs={{0,2},{1,3},{2,0},{3,1},{16,18},{17,19},{18,16},{19,17},{4,6},{5,7... | collective-permute-start | bytes 442376 | tf_op jit(solution)/shard_map/ppermute | solution.py:95
  241.0 13.4 %copy-start.4 = (bf16[4,384,384]{2,1,0:T(8,128)(2,1)}, bf16[4,384,384]{2,1,0:T(8,128)(2,1)S(1)}, u32[]{:S(2)}) copy-start(bf16[4,384,384]{2,1,0:T(8,128)(2,1)S(1)} %collective-permute-done.21.first) | copy-start | bytes 3538948
  270.7 5.6 %collective-permute-start.24 = (bf16[96,768]{1,0:T(8,128)(2,1)S(1)}, bf16[96,768]{1,0:T(8,128)(2,1)S(1)}, u32[]{:S(2)}, u32[]{:S(2)}) collective-permute-start(bf16[96,768]{1,0:T(8,128)(2,1)S(1)} %add_convert_fusion.1), channel_id=1, source_target_pairs={{0,16},{1,17},{2,18},{3,19},{16,0},{17,1},{18,2},{19,3},{4,20},{5,... | collective-permute-start | bytes 442376 | tf_op jit(solution)/shard_map/ppermute | solution.py:95
  276.3 6.9 %collective-permute-start.25 = (f32[96,768]{1,0:T(8,128)S(1)}, f32[96,768]{1,0:T(8,128)S(1)}, u32[]{:S(2)}, u32[]{:S(2)}) collective-permute-start(f32[96,768]{1,0:T(8,128)S(1)} %add_multiply_fusion), channel_id=1, source_target_pairs={{0,96},{1,97},{2,98},{3,99},{16,112},{17,113},{18,114},{19,115},{4... | collective-permute-start | bytes 884744 | tf_op jit(solution)/shard_map/ppermute | solution.py:95
  278.0 25.1 %collective-permute-start.22 = (bf16[4,384,384]{2,1,0:T(8,128)(2,1)}, bf16[4,384,384]{2,1,0:T(8,128)(2,1)S(1)}, u32[]{:S(2)}, u32[]{:S(2)}) collective-permute-start(bf16[4,384,384]{2,1,0:T(8,128)(2,1)} %copy-done.21), channel_id=1, source_target_pairs={{0,16},{2,18},{16,32},{18,34},{4,20},{6,22},{20,36},{22,38},{8,24}... | collective-permute-start | bytes 3538952 | tf_op jit(solution)/shard_map/ppermute | solution.py:95
  281.8 19.8 %collective-permute-start.26 = (f32[96,768]{1,0:T(8,128)S(1)}, f32[96,768]{1,0:T(8,128)S(1)}, u32[]{:S(2)}, u32[]{:S(2)}) collective-permute-start(f32[96,768]{1,0:T(8,128)S(1)} %add_multiply_fusion), channel_id=1, source_target_pairs={{0,64},{1,65},{2,66},{3,67},{16,80},{17,81},{18,82},{19,83},{4,68}... | collective-permute-start | bytes 884744 | tf_op jit(solution)/shard_map/ppermute | solution.py:95
  282.7 18.9 %collective-permute-start.27 = (f32[96,768]{1,0:T(8,128)S(1)}, f32[96,768]{1,0:T(8,128)S(1)}, u32[]{:S(2)}, u32[]{:S(2)}) collective-permute-start(f32[96,768]{1,0:T(8,128)S(1)} %add_multiply_fusion), channel_id=1, source_target_pairs={{0,32},{1,33},{2,34},{3,35},{16,48},{17,49},{18,50},{19,51},{4,36}... | collective-permute-start | bytes 884744 | tf_op jit(solution)/shard_map/ppermute | solution.py:95
  301.8 2.4 copy-start.9
  303.0 2.9 copy-start.11
  (6 other events, 7.9 us)
